TPU v7x, 128 devices: a whole 4x4x4 slice. The times are simulated.
128 devices in a mesh: fsdp: 4 (over z_hi, core), ctx: 8 (over x, z_lo), tp: 4 (over y).
Axes of the slice: x: 4, y: 4, z: 4 (z_hi: 2, z_lo: 2; z = z_hi * 2 + z_lo), core: 2. Of those that a mesh axis runs over, the one named last changes fastest.
Arguments:
- tokens: bfloat16 [4, 1024, 1024], P('fsdp', 'ctx'), may hold values from -6 to 6
- cotangent: bfloat16 [4, 1024, 1024], P('fsdp', 'ctx'), may hold values from -6 to 6
- w_qkv: bfloat16 [2, 3, 1024, 1024], P(None, None, ('fsdp', 'ctx'), 'tp'), may hold values from -0.1875 to 0.1875
- w_attn: bfloat16 [2, 1024, 1024], P(None, 'tp', ('fsdp', 'ctx')), may hold values from -0.75 to 0.75
- w_in: bfloat16 [2, 1024, 4096], P(None, ('fsdp', 'ctx'), 'tp'), may hold values from -0.1875 to 0.1875
- w_out: bfloat16 [2, 4096, 1024], P(None, 'tp', ('fsdp', 'ctx')), may hold values from -0.09375 to 0.09375
- ln_gain: bfloat16 [2, 2, 1024], P(None, None, ('fsdp', 'ctx')), may hold values from 0.5 to 1.5
- ln_bias: bfloat16 [2, 2, 1024], P(None, None, ('fsdp', 'ctx')), may hold values from -1 to 1
- rel_emb: bfloat16 [512, 1024], P(('fsdp', 'ctx')), may hold values from -6 to 6
- rel_gain: bfloat16 [1024], P(('fsdp', 'ctx')), may hold values from 0.5 to 1.5
- rel_bias: bfloat16 [1024], P(('fsdp', 'ctx')), may hold values from -1 to 1
- doc_ids: int32 [4, 1024], P('fsdp', 'ctx'), may hold values from 0 to 3, as said below
- rel_bucket: int32 [2047], replicated, may hold values from 0 to 511, as said below
Outputs:
- out: bfloat16 [4, 1024, 1024], P('fsdp', 'ctx')
- grad_tokens: bfloat16 [4, 1024, 1024], P('fsdp', 'ctx')
- grad_qkv: float32 [2, 3, 1024, 1024], P(None, None, ('fsdp', 'ctx'), 'tp')
- grad_attn: float32 [2, 1024, 1024], P(None, 'tp', ('fsdp', 'ctx'))
- grad_in: float32 [2, 1024, 4096], P(None, ('fsdp', 'ctx'), 'tp')
- grad_out: float32 [2, 4096, 1024], P(None, 'tp', ('fsdp', 'ctx'))
- grad_gain: float32 [2, 2, 1024], P(None, None, ('fsdp', 'ctx'))
- grad_bias: float32 [2, 2, 1024], P(None, None, ('fsdp', 'ctx'))
- grad_rel: float32 [512, 1024], P(('fsdp', 'ctx'))
- grad_rel_gain: float32 [1024], P(('fsdp', 'ctx'))
- grad_rel_bias: float32 [1024], P(('fsdp', 'ctx'))
Inputs may be any that keep to these rules, and one draw needn't show every extreme that they name: `doc_ids`: nondecreasing along each sequence, 0 at its first token and 3 at its last; in every sequence, document 1 covers at least positions 127 to 896. `rel_bucket`: entry o is the bucket of the offset o - (1023) from a key's position to a query's; nondecreasing in o, equal to 256 + o - (1023) where that offset lies within 128 of zero, 0 at the first entry and 511 at the last.
All inputs are finite; a program needn't handle non-finite values.
Results may differ from a plain program's by a relative error of at most 0.03.
Values may be sent and summed in bfloat16 or wider, within the bound.
No kernel may reach another device: no remote copies, remote signals or barrier semaphores. Data moves between devices by JAX's collectives and lax.ppermute only.
A program may use at most 192 MiB of HBM per device.

v0:
```python
import math

import jax
import jax.numpy as jnp
from jax import lax
from jax.sharding import PartitionSpec as P

HEAD_DIM = 64


EPS = 1e-07
NEG = -1e30
PRECISION_TOP = lax.Precision.HIGHEST


def normalize(values, gain_vec, offset):
    average = jnp.mean(values, axis=-1, keepdims=True)
    centered = values - average
    spread = jnp.mean(centered * centered, axis=-1, keepdims=True)
    return centered * lax.rsqrt(spread + EPS) * gain_vec + offset


def skew_query(values, key_count):
    sequences, rows_here, window = values.shape
    mirrored_scores = jnp.pad(values[..., ::-1], ((0, 0), (0, 0), (0, 1)))
    flat = mirrored_scores.reshape(sequences, rows_here * (window + 1))[:, : rows_here * window]
    shifted = flat.reshape(sequences, rows_here, window)
    return shifted[:, :, rows_here - 1 : rows_here - 1 + key_count]


def skew_key(values, rows_here):
    sequences, key_count, window = values.shape
    flat = jnp.pad(values.reshape(sequences, key_count * window), ((0, 0), (0, key_count)))
    shifted = flat.reshape(sequences, key_count, window + 1)[:, :, :rows_here]
    return jnp.swapaxes(shifted[:, :, ::-1], 1, 2)


def gelu_exact(values):
    return jax.nn.gelu(values, approximate=False)


def branch_total(values):
    return lax.psum(values.astype(jnp.bfloat16), "tp").astype(jnp.float32)


def back_total(values):
    return lax.psum(values.astype(jnp.bfloat16), "tp").astype(jnp.float32)


def local(
    tokens,
    cotangent,
    w_qkv,
    w_attn,
    w_in,
    w_out,
    ln_gain,
    ln_bias,
    rel_emb,
    rel_gain,
    rel_bias,
    doc_ids,
    rel_bucket,
):
    sequences, rows_here, model_width = tokens.shape
    layer_count = w_qkv.shape[0]
    heads_here = w_qkv.shape[3] // HEAD_DIM
    sequence_length = rows_here * lax.axis_size("ctx")
    row_start = lax.axis_index("ctx") * rows_here
    score_scale = 1.0 / math.sqrt(3.0 * HEAD_DIM)
    rel_rows, rel_gain_all, rel_bias_all = (
        lax.all_gather(rel_emb, ("fsdp", "ctx"), axis=0, tiled=True),
        lax.all_gather(rel_gain, ("fsdp", "ctx"), axis=0, tiled=True),
        lax.all_gather(rel_bias, ("fsdp", "ctx"), axis=0, tiled=True),
    )
    rel_whole = rel_rows.astype(jnp.float32)
    gain_float = rel_gain_all.astype(jnp.float32)
    bias_float = rel_bias_all.astype(jnp.float32)
    rel_low = normalize(rel_whole, gain_float, bias_float).astype(jnp.bfloat16)
    rel_float = rel_low.astype(jnp.float32)
    bucket_count = rel_low.shape[0]
    doc_all = lax.all_gather(doc_ids, "ctx", axis=1, tiled=True)
    same_doc = doc_ids[:, :, None] == doc_all[:, None, :]
    window = sequence_length + rows_here - 1
    to_window = lax.dynamic_slice_in_dim(rel_bucket, row_start, window, 0)
    from_window = lax.dynamic_slice_in_dim(
        rel_bucket, sequence_length - rows_here - row_start, window, 0
    )
    bucket_ids = lax.broadcasted_iota(jnp.int32, (window, bucket_count), 1)
    to_table = (to_window[:, None] == bucket_ids).astype(jnp.bfloat16)
    from_table = (from_window[:, None] == bucket_ids).astype(jnp.bfloat16)
    from_table_float = from_table.astype(jnp.float32)

    def widen(table, head_table):
        return jnp.dot(table, head_table, preferred_element_type=jnp.float32).astype(jnp.bfloat16)

    def head_scores(query_head, key_head, key_offsets, query_offsets):
        content = jnp.einsum(
            "sid,sjd->sij", query_head, key_head, preferred_element_type=jnp.float32
        )
        to_off = jnp.einsum(
            "sid,wd->siw", query_head, key_offsets, preferred_element_type=jnp.float32
        )
        from_off = jnp.einsum(
            "sjd,wd->sjw", key_head, query_offsets, preferred_element_type=jnp.float32
        )
        total = content + skew_query(to_off, sequence_length) + skew_key(from_off, rows_here)
        return (jnp.where(same_doc, total, NEG), to_off, from_off)

    stream = tokens.astype(jnp.float32)
    kept_values = []
    for layer_id in range(layer_count):
        gathered = (
            lax.all_gather(w_qkv[layer_id], ("fsdp", "ctx"), axis=1, tiled=True),
            lax.all_gather(w_attn[layer_id], ("fsdp", "ctx"), axis=1, tiled=True),
            lax.all_gather(w_in[layer_id], ("fsdp", "ctx"), axis=0, tiled=True),
            lax.all_gather(w_out[layer_id], ("fsdp", "ctx"), axis=1, tiled=True),
            lax.all_gather(ln_gain[layer_id], ("fsdp", "ctx"), axis=1, tiled=True),
            lax.all_gather(ln_bias[layer_id], ("fsdp", "ctx"), axis=1, tiled=True),
        )
        qkv_full, attn_full, in_full, out_full, gain_raw, shift_raw = gathered
        gain_pair = gain_raw.astype(jnp.float32)
        shift_pair = shift_raw.astype(jnp.float32)
        stream_low = stream.astype(jnp.bfloat16)
        projected = jnp.einsum(
            "sid,kdc->ksic", stream_low, qkv_full, preferred_element_type=jnp.float32
        )
        query_rows = (score_scale * projected[0]).astype(jnp.bfloat16)
        key_vecs = projected[1].astype(jnp.bfloat16)
        value_vecs = projected[2].astype(jnp.bfloat16)
        pos_proj = jnp.einsum(
            "bd,kdc->kbc", rel_low, qkv_full[:2], preferred_element_type=jnp.float32
        )
        pos_queries = (score_scale * pos_proj[0]).astype(jnp.bfloat16)
        position_key_rows = pos_proj[1].astype(jnp.bfloat16)
        key_all, value_all = (
            lax.all_gather(key_vecs, "ctx", axis=1, tiled=True),
            lax.all_gather(value_vecs, "ctx", axis=1, tiled=True),
        )
        mixed_heads = []
        log_totals = []
        for head_id in range(heads_here):
            head_slice = slice(head_id * HEAD_DIM, (head_id + 1) * HEAD_DIM)
            key_offsets = widen(to_table, position_key_rows[:, head_slice])
            query_offsets = widen(from_table, pos_queries[:, head_slice])
            score_matrix = head_scores(
                query_rows[..., head_slice], key_all[..., head_slice], key_offsets, query_offsets
            )[0]
            row_peak = jnp.max(score_matrix, axis=-1, keepdims=True)
            exp_terms = jnp.exp(score_matrix - row_peak)
            totals = jnp.sum(exp_terms, axis=-1, keepdims=True)
            attention = exp_terms / totals
            mixed_heads.append(
                jnp.einsum(
                    "sij,sjd->sid",
                    attention.astype(jnp.bfloat16),
                    value_all[..., head_slice],
                    preferred_element_type=jnp.float32,
                )
            )
            log_totals.append(row_peak + jnp.log(totals))
        mixture = jnp.concatenate(mixed_heads, axis=-1).astype(jnp.bfloat16)
        attended = branch_total(
            jnp.einsum("sic,cd->sid", mixture, attn_full, preferred_element_type=jnp.float32)
        )
        pre_hidden = stream + attended
        hidden = normalize(pre_hidden, gain_pair[0], shift_pair[0])
        hidden_low = hidden.astype(jnp.bfloat16)
        inner_pre = jnp.einsum(
            "sid,df->sif", hidden_low, in_full, preferred_element_type=jnp.float32
        )
        active = gelu_exact(inner_pre).astype(jnp.bfloat16)
        branch = branch_total(
            jnp.einsum("sif,fd->sid", active, out_full, preferred_element_type=jnp.float32)
        )
        pre_out = hidden + branch
        kept_values.append(
            (
                stream_low,
                query_rows,
                key_vecs,
                value_vecs,
                key_all,
                value_all,
                position_key_rows,
                pos_queries,
                log_totals,
                mixture,
                pre_hidden,
                hidden_low,
                inner_pre,
                active,
                pre_out,
                gathered,
            )
        )
        stream = normalize(pre_out, gain_pair[1], shift_pair[1])
    out_local = stream.astype(jnp.bfloat16)
    to_shape = jnp.zeros((sequences, rows_here, window), jnp.float32)
    from_shape = jnp.zeros((sequences, sequence_length, window), jnp.float32)
    to_unskew = jax.vjp(lambda source: skew_query(source, sequence_length), to_shape)[1]
    from_unskew = jax.vjp(lambda source: skew_key(source, rows_here), from_shape)[1]
    gradient = cotangent.astype(jnp.float32)
    rel_grad = jnp.zeros(rel_whole.shape, jnp.float32)
    weight_parts = []
    for layer_id in reversed(range(layer_count)):
        (
            stream_low,
            query_rows,
            key_vecs,
            value_vecs,
            key_kept,
            value_kept,
            position_key_rows,
            pos_queries,
            log_totals,
            mixture,
            pre_hidden,
            hidden_low,
            inner_pre,
            active,
            pre_out,
            kept_weights,
        ) = kept_values[layer_id]
        weights_now = (
            lax.all_gather(w_qkv[layer_id], ("fsdp", "ctx"), axis=1, tiled=True),
            lax.all_gather(w_attn[layer_id], ("fsdp", "ctx"), axis=1, tiled=True),
            lax.all_gather(w_in[layer_id], ("fsdp", "ctx"), axis=0, tiled=True),
            lax.all_gather(w_out[layer_id], ("fsdp", "ctx"), axis=1, tiled=True),
            lax.all_gather(ln_gain[layer_id], ("fsdp", "ctx"), axis=1, tiled=True),
            lax.all_gather(ln_bias[layer_id], ("fsdp", "ctx"), axis=1, tiled=True),
        )
        qkv_full, attn_full, in_full, out_full, gain_raw, shift_raw = weights_now
        gain_pair = gain_raw.astype(jnp.float32)
        shift_pair = shift_raw.astype(jnp.float32)
        key_all, value_all = (
            lax.all_gather(key_vecs, "ctx", axis=1, tiled=True),
            lax.all_gather(value_vecs, "ctx", axis=1, tiled=True),
        )
        out_pull = jax.vjp(normalize, pre_out, gain_pair[1], shift_pair[1])[1]
        d_pre_out, d_gain_out, d_shift_out = out_pull(gradient)
        d_out_low = d_pre_out.astype(jnp.bfloat16)
        grad_out_w = jnp.einsum(
            "sif,sid->fd", active, d_out_low, preferred_element_type=jnp.float32
        )
        d_active = jnp.einsum(
            "sid,fd->sif", d_out_low, out_full, preferred_element_type=jnp.float32
        )
        d_inner = jax.vjp(gelu_exact, inner_pre)[1](d_active)[0].astype(jnp.bfloat16)
        grad_in_w = jnp.einsum(
            "sid,sif->df", hidden_low, d_inner, preferred_element_type=jnp.float32
        )
        d_hidden = d_pre_out + back_total(
            jnp.einsum("sif,df->sid", d_inner, in_full, preferred_element_type=jnp.float32)
        )
        hidden_pull = jax.vjp(normalize, pre_hidden, gain_pair[0], shift_pair[0])[1]
        d_pre_hidden, d_gain_hidden, d_shift_hidden = hidden_pull(d_hidden)
        d_attended = d_pre_hidden.astype(jnp.bfloat16)
        grad_attn_w = jnp.einsum(
            "sic,sid->cd", mixture, d_attended, preferred_element_type=jnp.float32
        )
        d_mixture = jnp.einsum(
            "sid,cd->sic", d_attended, attn_full, preferred_element_type=jnp.float32
        ).astype(jnp.bfloat16)
        query_grads, key_grads, value_grads, pos_key_grads, pos_query_grads = ([], [], [], [], [])
        for head_id in range(heads_here):
            head_slice = slice(head_id * HEAD_DIM, (head_id + 1) * HEAD_DIM)
            query_head = query_rows[..., head_slice]
            key_head = key_all[..., head_slice]
            value_head = value_all[..., head_slice]
            pos_key_head = position_key_rows[:, head_slice]
            key_offsets = widen(to_table, pos_key_head)
            query_offsets = widen(from_table, pos_queries[:, head_slice])
            mix_grad = d_mixture[..., head_slice]
            score_matrix = head_scores(query_head, key_head, key_offsets, query_offsets)[0]
            attention = jnp.exp(score_matrix - log_totals[head_id])
            attention_grad = jnp.einsum(
                "sid,sjd->sij", mix_grad, value_head, preferred_element_type=jnp.float32
            )
            value_grads.append(
                jnp.einsum(
                    "sij,sid->sjd",
                    attention.astype(jnp.bfloat16),
                    mix_grad,
                    preferred_element_type=jnp.float32,
                )
            )
            score_grad = (
                attention
                * (attention_grad - jnp.sum(attention * attention_grad, axis=-1, keepdims=True))
            ).astype(jnp.bfloat16)
            score_float = score_grad.astype(jnp.float32)
            to_off_grad = to_unskew(score_float)[0].astype(jnp.bfloat16)
            from_off_grad = from_unskew(score_float)[0].astype(jnp.bfloat16)
            to_grad = jnp.einsum(
                "siw,wb->sib", to_off_grad, to_table, preferred_element_type=jnp.float32
            ).astype(jnp.bfloat16)
            query_grads.append(
                jnp.einsum("sij,sjd->sid", score_grad, key_head, preferred_element_type=jnp.float32)
                + jnp.einsum(
                    "sib,bd->sid", to_grad, pos_key_head, preferred_element_type=jnp.float32
                )
            )
            key_grads.append(
                jnp.einsum(
                    "sij,sid->sjd", score_grad, query_head, preferred_element_type=jnp.float32
                )
                + jnp.einsum(
                    "sjw,wd->sjd", from_off_grad, query_offsets, preferred_element_type=jnp.float32
                )
            )
            pos_key_grads.append(
                jnp.einsum("sib,sid->bd", to_grad, query_head, preferred_element_type=jnp.float32)
            )
            offset_sums = jnp.einsum(
                "sjw,sjd->wd", from_off_grad, key_head, preferred_element_type=jnp.float32
            )
            pos_query_grads.append(
                jnp.einsum("wb,wd->bd", from_table_float, offset_sums, precision=PRECISION_TOP)
            )
        key_part = jnp.concatenate(key_grads, axis=-1)
        value_part = jnp.concatenate(value_grads, axis=-1)
        key_summed, value_summed = (
            lax.psum_scatter(
                key_part.astype(jnp.bfloat16), "ctx", scatter_dimension=1, tiled=True
            ).astype(jnp.float32),
            lax.psum_scatter(
                value_part.astype(jnp.bfloat16), "ctx", scatter_dimension=1, tiled=True
            ).astype(jnp.float32),
        )
        query_low = (score_scale * jnp.concatenate(query_grads, axis=-1)).astype(jnp.bfloat16)
        projected_grads = jnp.stack(
            [query_low, key_summed.astype(jnp.bfloat16), value_summed.astype(jnp.bfloat16)]
        )
        pos_grads = jnp.stack(
            [
                score_scale * jnp.concatenate(pos_query_grads, axis=-1),
                jnp.concatenate(pos_key_grads, axis=-1),
            ]
        )
        grad_qkv_w = jnp.einsum(
            "sid,ksic->kdc", stream_low, projected_grads, preferred_element_type=jnp.float32
        )
        rel_terms = jnp.einsum("bd,kbc->kdc", rel_float, pos_grads, precision=PRECISION_TOP)
        grad_qkv_w = grad_qkv_w + jnp.pad(rel_terms, ((0, 1), (0, 0), (0, 0)))
        rel_grad = rel_grad + jnp.einsum(
            "kbc,kdc->bd", pos_grads, qkv_full[:2].astype(jnp.float32), precision=PRECISION_TOP
        )
        gradient = d_pre_hidden + back_total(
            jnp.einsum(
                "ksic,kdc->sid", projected_grads, qkv_full, preferred_element_type=jnp.float32
            )
        )
        weight_parts.append(
            (
                lax.psum_scatter(
                    grad_qkv_w.astype(jnp.bfloat16),
                    ("fsdp", "ctx"),
                    scatter_dimension=1,
                    tiled=True,
                ).astype(jnp.float32),
                lax.psum_scatter(
                    grad_attn_w.astype(jnp.bfloat16),
                    ("fsdp", "ctx"),
                    scatter_dimension=1,
                    tiled=True,
                ).astype(jnp.float32),
                lax.psum_scatter(
                    grad_in_w.astype(jnp.bfloat16), ("fsdp", "ctx"), scatter_dimension=0, tiled=True
                ).astype(jnp.float32),
                lax.psum_scatter(
                    grad_out_w.astype(jnp.bfloat16),
                    ("fsdp", "ctx"),
                    scatter_dimension=1,
                    tiled=True,
                ).astype(jnp.float32),
                lax.psum_scatter(
                    jnp.stack([d_gain_hidden, d_gain_out]).astype(jnp.bfloat16),
                    ("fsdp", "ctx"),
                    scatter_dimension=1,
                    tiled=True,
                ).astype(jnp.float32),
                lax.psum_scatter(
                    jnp.stack([d_shift_hidden, d_shift_out]).astype(jnp.bfloat16),
                    ("fsdp", "ctx"),
                    scatter_dimension=1,
                    tiled=True,
                ).astype(jnp.float32),
            )
        )
    weight_parts = weight_parts[::-1]
    stacked = [jnp.stack([record[member] for record in weight_parts]) for member in range(6)]
    rel_total = lax.psum(rel_grad, ("fsdp", "ctx", "tp"))
    rel_pull = jax.vjp(normalize, rel_whole, gain_float, bias_float)[1]
    d_rel, d_rel_gain, d_rel_bias = rel_pull(rel_total)
    owner_index = lax.axis_index(("fsdp", "ctx"))
    own_rows = rel_emb.shape[0]
    own_cols = rel_gain.shape[0]
    grad_rel = lax.dynamic_slice_in_dim(d_rel, owner_index * own_rows, own_rows, 0)
    grad_rel_gain = lax.dynamic_slice_in_dim(d_rel_gain, owner_index * own_cols, own_cols, 0)
    grad_rel_bias = lax.dynamic_slice_in_dim(d_rel_bias, owner_index * own_cols, own_cols, 0)
    return (
        out_local,
        gradient.astype(jnp.bfloat16),
        stacked[0],
        stacked[1],
        stacked[2],
        stacked[3],
        stacked[4],
        stacked[5],
        grad_rel,
        grad_rel_gain,
        grad_rel_bias,
    )


def solution(mesh):
    return jax.shard_map(
        local,
        mesh=mesh,
        in_specs=(
            P("fsdp", "ctx", None),
            P("fsdp", "ctx", None),
            P(None, None, ("fsdp", "ctx"), "tp"),
            P(None, "tp", ("fsdp", "ctx")),
            P(None, ("fsdp", "ctx"), "tp"),
            P(None, "tp", ("fsdp", "ctx")),
            P(None, None, ("fsdp", "ctx")),
            P(None, None, ("fsdp", "ctx")),
            P(("fsdp", "ctx"), None),
            P(("fsdp", "ctx")),
            P(("fsdp", "ctx")),
            P("fsdp", "ctx"),
            P(),
        ),
        out_specs=(
            P("fsdp", "ctx", None),
            P("fsdp", "ctx", None),
            P(None, None, ("fsdp", "ctx"), "tp"),
            P(None, "tp", ("fsdp", "ctx")),
            P(None, ("fsdp", "ctx"), "tp"),
            P(None, "tp", ("fsdp", "ctx")),
            P(None, None, ("fsdp", "ctx")),
            P(None, None, ("fsdp", "ctx")),
            P(("fsdp", "ctx"), None),
            P(("fsdp", "ctx")),
            P(("fsdp", "ctx")),
        ),
        check_vma=False,
    )
```

profile of v0, /device:TPU:0, one launch (start us, length us, event | category | flops | bytes accessed | tf_op | source)
XLA Modules:
  0.0 4135.5 jit_solution(16353212038178567346)
XLA Ops:
  13.9 68.5 %all-reduce.46 = (bf16[1024]{0:T(1024)(128)(2,1)S(1)}, bf16[1024]{0:T(1024)(128)(2,1)S(1)}) all-reduce(bf16[1024]{0:T(1024)(128)(2,1)S(1)} %dynamic-update-slice.1, bf16[1024]{0:T(1024)(128)(2,1)S(1)} %dynamic-update-slice), channel_id=1, replica_groups=mesh['fsdp'=4,'ctx'=8,'tp'=4] {'fsdp','ctx'}, use_global_device_ids=true, to_apply=%add.43 | all-reduce | flops 2048 | bytes 8192
  99.0 66.0 %all-gather.3 = bf16[1,256,1024]{1,2,0:T(8,128)(2,1)S(1)} all-gather(bf16[1,256,32]{1,2,0:T(8,128)(2,1)S(1)} %get-tuple-element.86), channel_id=5, replica_groups=mesh['fsdp'=4,'ctx'=8,'tp'=4] {'fsdp','ctx'}, dimensions={2}, use_global_device_ids=true | all-gather | bytes 540672 | tf_op jit(solution)/shard_map/all_gather | solution.py:115
  252.1 52.3 %pad_reduce_fusion.7 = f32[1179648]{0:T(1024)} fusion(f32[1,1178624]{1,0:T(1,128)} %reshape.2301), kind=kLoop, calls=%fused_computation.15 | loop fusion | bytes 9433088 | tf_op jit(solution)/shard_map/jit(_pad)/pad | solution.py:33
  343.0 52.1 %pad_reduce_fusion.6 = f32[1179648]{0:T(1024)} fusion(f32[1,1178624]{1,0:T(1,128)} %reshape.2309), kind=kLoop, calls=%fused_computation.14 | loop fusion | bytes 9433088 | tf_op jit(solution)/shard_map/jit(_pad)/pad | solution.py:33
  433.9 51.9 %pad_reduce_fusion.5 = f32[1179648]{0:T(1024)} fusion(f32[1,1178624]{1,0:T(1,128)} %reshape.2317), kind=kLoop, calls=%fused_computation.13 | loop fusion | bytes 9433088 | tf_op jit(solution)/shard_map/jit(_pad)/pad | solution.py:33
  517.7 52.1 %pad_reduce_fusion.4 = f32[1179648]{0:T(1024)} fusion(f32[1,1178624]{1,0:T(1,128)} %reshape.2325), kind=kLoop, calls=%fused_computation.12 | loop fusion | bytes 9433088 | tf_op jit(solution)/shard_map/jit(_pad)/pad | solution.py:33
  626.6 64.4 %all-gather.4 = bf16[1,2,1024]{1,0,2:T(2,128)(2,1)S(1)} all-gather(bf16[1,2,32]{1,0,2:T(2,128)(2,1)S(1)} %copy.162), channel_id=6, replica_groups=mesh['fsdp'=4,'ctx'=8,'tp'=4] {'fsdp','ctx'}, dimensions={2}, use_global_device_ids=true | all-gather | bytes 4224 | tf_op jit(solution)/shard_map/all_gather | solution.py:118
  692.2 66.6 %all-gather.5 = bf16[1,2,1024]{1,0,2:T(2,128)(2,1)S(1)} all-gather(bf16[1,2,32]{1,0,2:T(2,128)(2,1)S(1)} %copy.163), channel_id=7, replica_groups=mesh['fsdp'=4,'ctx'=8,'tp'=4] {'fsdp','ctx'}, dimensions={2}, use_global_device_ids=true | all-gather | bytes 4224 | tf_op jit(solution)/shard_map/all_gather | solution.py:119
  771.8 64.3 %all-gather.11 = bf16[1,256,1024]{1,2,0:T(8,128)(2,1)S(1)} all-gather(bf16[1,256,32]{1,2,0:T(8,128)(2,1)S(1)} %copy-done.157), channel_id=13, replica_groups=mesh['fsdp'=4,'ctx'=8,'tp'=4] {'fsdp','ctx'}, dimensions={2}, use_global_device_ids=true | all-gather | bytes 540672 | tf_op jit(solution)/shard_map/all_gather | solution.py:115
  959.1 54.2 %pad_reduce_fusion.2 = (f32[1179648]{0:T(1024)}, f32[1179648]{0:T(1024)}) fusion(f32[1,1178624]{1,0:T(1,128)} %reshape.2343, f32[1,1178624]{1,0:T(1,128)} %reshape.2335), kind=kLoop, calls=%fused_computation.10 | loop fusion | bytes 18866176 | tf_op jit(solution)/shard_map/jit(_pad)/pad | solution.py:33
  1122.4 55.8 %pad_reduce_fusion = (f32[1179648]{0:T(1024)}, f32[1179648]{0:T(1024)}) fusion(f32[1,1178624]{1,0:T(1,128)} %reshape.2359, f32[1,1178624]{1,0:T(1,128)} %reshape.2351), kind=kLoop, calls=%fused_computation.8 | loop fusion | bytes 18866176 | tf_op jit(solution)/shard_map/jit(_pad)/pad | solution.py:33
  1246.3 64.0 %all-gather.12 = bf16[1,2,1024]{1,0,2:T(2,128)(2,1)S(1)} all-gather(bf16[1,2,32]{1,0,2:T(2,128)(2,1)S(1)} %copy.168), channel_id=14, replica_groups=mesh['fsdp'=4,'ctx'=8,'tp'=4] {'fsdp','ctx'}, dimensions={2}, use_global_device_ids=true | all-gather | bytes 4224 | tf_op jit(solution)/shard_map/all_gather | solution.py:118
  1311.0 66.5 %all-gather.13 = bf16[1,2,1024]{1,0,2:T(2,128)(2,1)S(1)} all-gather(bf16[1,2,32]{1,0,2:T(2,128)(2,1)S(1)} %copy.169), channel_id=15, replica_groups=mesh['fsdp'=4,'ctx'=8,'tp'=4] {'fsdp','ctx'}, dimensions={2}, use_global_device_ids=true | all-gather | bytes 4224 | tf_op jit(solution)/shard_map/all_gather | solution.py:119
  1398.8 59.1 %all-gather.36.cloned.1.call-done = bf16[1,1024,1024]{1,2,0:T(8,128)(2,1)} async-done(((bf16[1,1024,32]{1,2,0:T(8,128)(2,1)}), bf16[1,1024,1024]{1,2,0:T(8,128)(2,1)}) %all-gather.36.cloned.1.call-update) | async-done | bytes 2097168 | tf_op jit(solution)/shard_map/all_gather | solution.py:117
  1641.6 48.5 %fusion.6 = bf16[1178624]{0:T(1024)(128)(2,1)} fusion(bf16[1,1179648]{1,0:T(2,128)(2,1)} %bitcast.1013), kind=kLoop, calls=%fused_computation.29 | loop fusion | bytes 4714496 | tf_op jit(solution)/shard_map/convert_element_type | solution.py:294
  1769.6 48.5 %fusion.4 = bf16[1178624]{0:T(1024)(128)(2,1)} fusion(bf16[1,1179648]{1,0:T(2,128)(2,1)} %bitcast.1015), kind=kLoop, calls=%fused_computation.25 | loop fusion | bytes 4714496 | tf_op jit(solution)/shard_map/convert_element_type | solution.py:294
  2111.2 48.7 %fusion.3 = bf16[1178624]{0:T(1024)(128)(2,1)} fusion(bf16[1,1179648]{1,0:T(2,128)(2,1)} %bitcast.1016), kind=kLoop, calls=%fused_computation.23 | loop fusion | bytes 4714496 | tf_op jit(solution)/shard_map/convert_element_type | solution.py:294
  2187.1 48.5 %fusion.2 = bf16[1178624]{0:T(1024)(128)(2,1)} fusion(bf16[1,1179648]{1,0:T(2,128)(2,1)} %bitcast.1017), kind=kLoop, calls=%fused_computation.21 | loop fusion | bytes 4714496 | tf_op jit(solution)/shard_map/convert_element_type | solution.py:294
  2262.9 48.7 %fusion.1 = bf16[1178624]{0:T(1024)(128)(2,1)} fusion(bf16[1,1179648]{1,0:T(2,128)(2,1)} %bitcast.1018), kind=kLoop, calls=%fused_computation.19 | loop fusion | bytes 4714496 | tf_op jit(solution)/shard_map/convert_element_type | solution.py:294
  2338.8 48.5 %fusion = bf16[1178624]{0:T(1024)(128)(2,1)} fusion(bf16[1,1179648]{1,0:T(2,128)(2,1)} %bitcast.1019), kind=kLoop, calls=%fused_computation.17 | loop fusion | bytes 4714496 | tf_op jit(solution)/shard_map/convert_element_type | solution.py:294
  2557.7 60.7 %reduce-scatter.57.cloned.1.call-done = bf16[32,2]{1,0:T(8,128)(2,1)} async-done(((bf16[1024,2]{1,0:T(8,128)(2,1)}), bf16[32,2]{1,0:T(8,128)(2,1)}) %reduce-scatter.57.cloned.1.call-update) | async-done | bytes 144
  2619.2 130.3 %reduce-scatter.53.cloned.1.call-done = bf16[32,2]{1,0:T(8,128)(2,1)} async-done(((bf16[1024,2]{1,0:T(8,128)(2,1)}), bf16[32,2]{1,0:T(8,128)(2,1)}) %reduce-scatter.53.cloned.1.call-update) | async-done | bytes 144
  2750.3 130.0 %reduce-scatter.55.cloned.1.call-done = bf16[32,2]{1,0:T(8,128)(2,1)} async-done(((bf16[1024,2]{1,0:T(8,128)(2,1)}), bf16[32,2]{1,0:T(8,128)(2,1)}) %reduce-scatter.55.cloned.1.call-update) | async-done | bytes 144
  2881.2 130.5 %reduce-scatter.51.cloned.1.call-done = bf16[32,2]{1,0:T(8,128)(2,1)} async-done(((bf16[1024,2]{1,0:T(8,128)(2,1)}), bf16[32,2]{1,0:T(8,128)(2,1)}) %reduce-scatter.51.cloned.1.call-update) | async-done | bytes 144
  3013.6 150.7 %all-reduce.75.cloned.1.call-done = f32[512,1024]{1,0:T(8,128)} async-done(((f32[512,1024]{1,0:T(8,128)}), f32[512,1024]{1,0:T(8,128)}) %all-reduce.75.cloned.1.call-update) | async-done | bytes 2097168 | tf_op jit(solution)/shard_map/psum | solution.py:393
  3169.6 127.8 %reduce-scatter.33.cloned.1.call-done = bf16[256,32]{0,1:T(8,128)(2,1)} async-done(((bf16[256,1024]{0,1:T(8,128)(2,1)}), bf16[256,32]{0,1:T(8,128)(2,1)}) %reduce-scatter.33.cloned.1.call-update) | async-done | bytes 16400 | tf_op jit(solution)/shard_map/reduce_scatter | solution.py:362
  3297.4 131.1 %reduce-scatter.31.cloned.1.call-done = bf16[256,32]{0,1:T(8,128)(2,1)} async-done(((bf16[256,1024]{0,1:T(8,128)(2,1)}), bf16[256,32]{0,1:T(8,128)(2,1)}) %reduce-scatter.31.cloned.1.call-update) | async-done | bytes 16400 | tf_op jit(solution)/shard_map/reduce_scatter | solution.py:362
  3471.5 113.9 %all-reduce.77.cloned.1.call-done = (bf16[3,1024,256]{2,0,1:T(4,128)(2,1)}, bf16[3,1024,256]{2,0,1:T(4,128)(2,1)}) async-done(((bf16[3,1024,256]{2,0,1:T(4,128)(2,1)}, bf16[3,1024,256]{2,0,1:T(4,128)(2,1)}), (bf16[3,1024,256]{2,0,1:T(4,128)(2,1)}, bf16[3,1024,256]{2,0,1:T(4,128)(2,1)})) %all-reduce.77.cloned.1.call-update) | async-done | bytes 3145744
  3587.9 134.8 %reduce-scatter.41.cloned.1.call-done = bf16[1024,32]{0,1:T(8,128)(2,1)} async-done(((bf16[1024,1024]{0,1:T(8,128)(2,1)}), bf16[1024,32]{0,1:T(8,128)(2,1)}) %reduce-scatter.41.cloned.1.call-update) | async-done | bytes 65552 | tf_op jit(solution)/shard_map/reduce_scatter | solution.py:371
  3722.7 134.8 %reduce-scatter.39.cloned.1.call-done = bf16[1024,32]{0,1:T(8,128)(2,1)} async-done(((bf16[1024,1024]{0,1:T(8,128)(2,1)}), bf16[1024,32]{0,1:T(8,128)(2,1)}) %reduce-scatter.39.cloned.1.call-update) | async-done | bytes 65552 | tf_op jit(solution)/shard_map/reduce_scatter | solution.py:371
  3859.1 132.8 %reduce-scatter.37.cloned.1.call-done = bf16[32,1024]{1,0:T(8,128)(2,1)} async-done(((bf16[1024,1024]{1,0:T(8,128)(2,1)}), bf16[32,1024]{1,0:T(8,128)(2,1)}) %reduce-scatter.37.cloned.1.call-update) | async-done | bytes 65552 | tf_op jit(solution)/shard_map/reduce_scatter | solution.py:368
  3991.9 134.8 %reduce-scatter.35.cloned.1.call-done = bf16[32,1024]{1,0:T(8,128)(2,1)} async-done(((bf16[1024,1024]{1,0:T(8,128)(2,1)}), bf16[32,1024]{1,0:T(8,128)(2,1)}) %reduce-scatter.35.cloned.1.call-update) | async-done | bytes 65552 | tf_op jit(solution)/shard_map/reduce_scatter | solution.py:368
  (1108 shorter events, 1473.9 us)
Async XLA Ops:
  7.2 158.7 %all-gather.24.cloned.1.call-start = ((), (), s32[]{:S(2)}) async-start(), calls=%async_computation.14 | async-start | bytes 1081344 | tf_op jit(solution)/shard_map/all_gather | solution.py:72
  7.9 171.2 %all-gather.26.cloned.1.call-start = ((), (), s32[]{:S(2)}) async-start(), calls=%async_computation.30 | async-start | bytes 1622016 | tf_op jit(solution)/shard_map/all_gather | solution.py:114
  9.4 826.7 %all-gather.32.cloned.1.call-start = ((), (), s32[]{:S(2)}) async-start(), calls=%async_computation.33 | async-start | bytes 1622016 | tf_op jit(solution)/shard_map/all_gather | solution.py:114
  10.2 833.4 %all-reduce.59.cloned.1.call-start = ((), (), s32[]{:S(2)}) async-start(), calls=%async_computation.15 | async-start | bytes 524288 | tf_op jit(solution)/shard_map/psum | solution.py:43
  624.9 220.9 %all-gather.28.cloned.1.call-start = ((), (), s32[]{:S(2)}) async-start(), calls=%async_computation.31 | async-start | bytes 2162688 | tf_op jit(solution)/shard_map/all_gather | solution.py:116
  625.7 224.2 %all-gather.30.cloned.1.call-start = ((), (), s32[]{:S(2)}) async-start(), calls=%async_computation.32 | async-start | bytes 2162688 | tf_op jit(solution)/shard_map/all_gather | solution.py:117
  626.4 266.2 %all-reduce.61.cloned.1.call-start = ((), (), s32[]{:S(2)}) async-start(), calls=%async_computation.16 | async-start | bytes 524288 | tf_op jit(solution)/shard_map/psum | solution.py:43
  853.1 540.1 %all-reduce.63.cloned.1.call-start = ((), (), s32[]{:S(2)}) async-start(), calls=%async_computation.17 | async-start | bytes 524288 | tf_op jit(solution)/shard_map/psum | solution.py:43
  894.9 1012.8 %copy-start.97 = (bf16[1,128,256]{1,2,0:T(8,128)(2,1)}, bf16[1,128,256]{1,2,0:T(8,128)(2,1)S(1)}, u32[]{:S(2)}) copy-start(bf16[1,128,256]{1,2,0:T(8,128)(2,1)S(1)} %fusion.430) | copy-start | bytes 196612
  1244.8 150.0 %all-gather.34.cloned.1.call-start = ((), (), s32[]{:S(2)}) async-start(), calls=%async_computation.34 | async-start | bytes 2162688 | tf_op jit(solution)/shard_map/all_gather | solution.py:116
  1245.5 212.4 %all-gather.36.cloned.1.call-start = ((), (), s32[]{:S(2)}) async-start(), calls=%async_computation.35 | async-start | bytes 2162688 | tf_op jit(solution)/shard_map/all_gather | solution.py:117
  1246.1 258.3 %all-reduce.65.cloned.1.call-start = ((), (), s32[]{:S(2)}) async-start(), calls=%async_computation.18 | async-start | bytes 524288 | tf_op jit(solution)/shard_map/psum | solution.py:43
  1461.1 91.9 %all-reduce.67.cloned.1.call-start = ((), (), s32[]{:S(2)}) async-start(), calls=%async_computation.19 | async-start | bytes 524288 | tf_op jit(solution)/shard_map/psum | solution.py:47
  1510.7 442.1 %reduce-scatter.43.cloned.1.call-start = ((), (), s32[]{:S(2)}) async-start(), calls=%async_computation.36 | async-start | bytes 589824
  1914.4 76.9 %reduce-scatter.45.cloned.1.call-start = ((), (), s32[]{:S(2)}) async-start(), calls=%async_computation.37 | async-start | bytes 589824
  1936.9 101.0 %all-reduce.69.cloned.1.call-start = ((), (), s32[]{:S(2)}) async-start(), calls=%async_computation.20 | async-start | bytes 524288 | tf_op jit(solution)/shard_map/psum | solution.py:47
  1997.4 91.1 %all-reduce.71.cloned.1.call-start = ((), (), s32[]{:S(2)}) async-start(), calls=%async_computation.21 | async-start | bytes 524288 | tf_op jit(solution)/shard_map/psum | solution.py:47
  2046.3 488.0 %reduce-scatter.47.cloned.1.call-start = ((), (), s32[]{:S(2)}) async-start(), calls=%async_computation.38 | async-start | bytes 589824
  2408.4 127.0 %reduce-scatter.49.cloned.1.call-start = ((), (), s32[]{:S(2)}) async-start(), calls=%async_computation.39 | async-start | bytes 589824
  2416.7 201.7 %reduce-scatter.57.cloned.1.call-start = ((), (), s32[]{:S(2)}) async-start(), calls=%async_computation.43 | async-start | bytes 270336
  2418.6 331.0 %reduce-scatter.53.cloned.1.call-start = ((), (), s32[]{:S(2)}) async-start(), calls=%async_computation.41 | async-start | bytes 270336
  2419.6 460.8 %reduce-scatter.55.cloned.1.call-start = ((), (), s32[]{:S(2)}) async-start(), calls=%async_computation.42 | async-start | bytes 270336
  2497.3 514.3 %reduce-scatter.51.cloned.1.call-start = ((), (), s32[]{:S(2)}) async-start(), calls=%async_computation.40 | async-start | bytes 270336
  2498.3 666.0 %all-reduce.75.cloned.1.call-start = ((), (), s32[]{:S(2)}) async-start(), calls=%async_computation.29 | async-start | bytes 4194304 | tf_op jit(solution)/shard_map/psum | solution.py:393
  2506.6 790.8 %reduce-scatter.33.cloned.1.call-start = ((), (), s32[]{:S(2)}) async-start(), calls=%async_computation.24 | async-start | bytes 540672 | tf_op jit(solution)/shard_map/reduce_scatter | solution.py:362
  2508.9 919.6 %reduce-scatter.31.cloned.1.call-start = ((), (), s32[]{:S(2)}) async-start(), calls=%async_computation.23 | async-start | bytes 540672 | tf_op jit(solution)/shard_map/reduce_scatter | solution.py:362
  2527.0 942.7 %all-reduce.73.cloned.1.call-start = ((), (), s32[]{:S(2)}) async-start(), calls=%async_computation.22 | async-start | bytes 524288 | tf_op jit(solution)/shard_map/psum | solution.py:47
  2539.3 1046.2 %all-reduce.77.cloned.1.call-start = ((), (), s32[]{:S(2)}) async-start(), calls=%async_computation.44 | async-start | bytes 8388608
  2547.0 1175.8 %reduce-scatter.41.cloned.1.call-start = ((), (), s32[]{:S(2)}) async-start(), calls=%async_computation.28 | async-start | bytes 2162688 | tf_op jit(solution)/shard_map/reduce_scatter | solution.py:371
  2550.2 1307.3 %reduce-scatter.39.cloned.1.call-start = ((), (), s32[]{:S(2)}) async-start(), calls=%async_computation.27 | async-start | bytes 2162688 | tf_op jit(solution)/shard_map/reduce_scatter | solution.py:371
  2552.5 1439.4 %reduce-scatter.37.cloned.1.call-start = ((), (), s32[]{:S(2)}) async-start(), calls=%async_computation.26 | async-start | bytes 2162688 | tf_op jit(solution)/shard_map/reduce_scatter | solution.py:368
  2554.8 1571.9 %reduce-scatter.35.cloned.1.call-start = ((), (), s32[]{:S(2)}) async-start(), calls=%async_computation.25 | async-start | bytes 2162688 | tf_op jit(solution)/shard_map/reduce_scatter | solution.py:368
  (269 other events, 10718.3 us)
Sparse Core Ops, SparseCore 0:
  9.7 83.1 all-gather.23
  95.2 83.9 all-gather.25
  181.4 84.6 all-gather.31
  625.1 41.6 all-reduce.58
  669.0 83.1 all-gather.27
  754.4 85.1 all-gather.29
  853.2 39.2 all-reduce.60
  1244.9 41.4 all-reduce.62
  1288.7 83.3 all-gather.33
  1374.3 83.5 all-gather.35
  1461.2 43.1 all-reduce.64
  1510.8 42.1 all-reduce.66
  1914.6 38.2 reduce-scatter.42
  1955.0 36.2 reduce-scatter.44
  1997.6 40.2 all-reduce.68
  2046.4 42.1 all-reduce.70
  2408.6 38.2 reduce-scatter.46
  2449.1 36.5 reduce-scatter.48
  2488.1 130.2 reduce-scatter.56
  2621.2 128.3 reduce-scatter.52
  2752.0 128.3 reduce-scatter.54
  2883.3 128.2 reduce-scatter.50
  3017.2 147.0 all-reduce.74
  3166.6 130.7 reduce-scatter.32
  3299.8 128.6 reduce-scatter.30
  3431.3 38.3 all-reduce.72
  3473.0 112.3 all-reduce.76
  3587.8 134.8 reduce-scatter.40
  3725.2 132.2 reduce-scatter.38
  3859.7 132.1 reduce-scatter.36
  3994.4 132.2 reduce-scatter.34
where the time goes:
time: 4160 us; the launch traced here: 4140 us
  waiting for transfers between devices  1860 us (45%)
  local copies, waits for them, and re-layouts  1390 us (33%)
  blocking collectives  581 us (14%)
  matrix products  218 us (5%)
  other arithmetic  57.9 us (1%)
    unnamed x40, waiting for transfers between devices  612 us
    convert_element_type x16, local copies, waits for them, and re-layouts, local(): from_off_grad = from_unskew(score_float)[0].astype(jnp.bfloat16)  448 us
    pad x6, local copies, waits for them, and re-layouts, skew_key(): jnp.pad(values.reshape(sequences, key_count * window), ((0, 0), (0, key_c...  318 us
    reduce_scatter x2, waiting for transfers between devices, local(): lax.psum_scatter(grad_out_w.astype(jnp.bfloat16), ('fsdp', 'ctx'), scatte...  270 us
    reduce_scatter x2, waiting for transfers between devices, local(): lax.psum_scatter(grad_in_w.astype(jnp.bfloat16), ('fsdp', 'ctx'), scatter...  268 us
    reduce_scatter x2, waiting for transfers between devices, local(): lax.psum_scatter(grad_attn_w.astype(jnp.bfloat16), ('fsdp', 'ctx'), scatt...  259 us
    unnamed x636, local copies, waits for them, and re-layouts  207 us
    psum x4, waiting for transfers between devices, back_total(): return lax.psum(values.astype(jnp.bfloat16), 'tp').astype(jnp.float32)  156 us
  transfers between devices with their start and end apart: 31, of which 22 were waited for; matrix products, arithmetic and copies ran while one was open for 16% of the time, Pallas kernels for 0%

commit v1 on v0

v1 whole, which is shorter than its diff:
```python
import functools
import math

import jax
import jax.numpy as jnp
from jax import lax
from jax.experimental import pallas as pl
from jax.experimental.pallas import tpu as pltpu
from jax.sharding import Mesh
from jax.sharding import PartitionSpec as P

HEAD_DIM = 64
EPS = 1e-07
NEG = -1e30
BLOCK = 128
F32 = jnp.float32
BF16 = jnp.bfloat16
VMEM_LIMIT = 56 << 20
CTX = ("x", "zl")
ZED = ("zh", "zl")
PLANE = ("zh", "x", "zl")
OWNERS = ("zh", "core", "x", "zl")


def dot(a, b, ca, cb):
    return lax.dot_general(a, b, (((ca,), (cb,)), ((), ())), preferred_element_type=F32)


def params():
    return pltpu.CompilerParams(vmem_limit_bytes=VMEM_LIMIT)


def head_mask(shape, head):
    lane = lax.broadcasted_iota(jnp.int32, shape, len(shape) - 1)
    return (lane >= head * HEAD_DIM) & (lane < (head + 1) * HEAD_DIM)


def only_head(values, head):
    return jnp.where(head_mask(values.shape, head), values.astype(F32), 0.0).astype(BF16)


def forward_kernel(place_ref, q_ref, *refs):
    count = len(refs) - 10
    blocks = refs[:count]
    pk_ref, pq_ref, doc_i_ref, doc_j_ref = refs[count : count + 4]
    mix_ref, p_ref, k_ref, v_ref, kv_ref, sems = refs[count + 4 :]
    rows, width = q_ref.shape
    keys = k_ref.shape[0]
    win = pk_ref.shape[0]
    mine = place_ref[0]
    copies = []
    for shift, block in enumerate(blocks):
        owner = lax.rem(mine - shift + count, count)
        start = pl.multiple_of(owner * rows, rows)
        copies.append(
            pltpu.make_async_copy(block, kv_ref.at[pl.ds(start, rows), :], sems.at[shift])
        )
    for copy in copies:
        copy.start()
    for copy in copies:
        copy.wait()
    k_ref[...] = kv_ref[:, :width]
    v_ref[...] = kv_ref[:, width:]
    mix = jnp.zeros((rows, width), F32)
    for head in range(width // HEAD_DIM):
        q = only_head(q_ref[...], head)
        to = dot(q, pk_ref[...], 1, 1)
        to = pltpu.roll(to, win + 1 - rows, 1, stride=1, stride_axis=0)
        parts = []
        for start in range(0, keys, BLOCK):
            key_block = k_ref[start : start + BLOCK, :]
            first = win - 2 * BLOCK - start
            pq = only_head(pq_ref[first : first + 2 * BLOCK, :], head)
            off = dot(key_block, pq, 1, 1)
            off = pltpu.roll(off, BLOCK, 1, stride=1, stride_axis=0)
            s = dot(q, key_block, 1, 1) + to[:, start : start + BLOCK] + off[:, :BLOCK].T
            same = doc_i_ref[...] == doc_j_ref[:, start : start + BLOCK]
            parts.append(jnp.where(same, s, NEG))
        s = jnp.concatenate(parts, axis=1)
        e = jnp.exp(s - jnp.max(s, axis=1, keepdims=True))
        p = (e / jnp.sum(e, axis=1, keepdims=True)).astype(BF16)
        p_ref[head] = p
        mix = jnp.where(head_mask(mix.shape, head), dot(p, v_ref[...], 1, 0), mix)
    mix_ref[...] = mix.astype(BF16)


def attention_forward(place, q, blocks, pk_rev, pq_rev, doc_i, doc_j):
    rows, width = q.shape
    keys = rows * len(blocks)
    heads = width // HEAD_DIM
    vmem = pl.BlockSpec(memory_space=pltpu.VMEM)
    return pl.pallas_call(
        forward_kernel,
        in_specs=[pl.BlockSpec(memory_space=pltpu.SMEM), vmem]
        + [pl.BlockSpec(memory_space=pl.ANY)] * len(blocks)
        + [vmem] * 4,
        out_specs=(vmem,) * 4,
        out_shape=(
            jax.ShapeDtypeStruct((rows, width), BF16),
            jax.ShapeDtypeStruct((heads, rows, keys), BF16),
            jax.ShapeDtypeStruct((keys, width), BF16),
            jax.ShapeDtypeStruct((keys, width), BF16),
        ),
        scratch_shapes=[
            pltpu.VMEM((keys, 2 * width), BF16),
            pltpu.SemaphoreType.DMA((len(blocks),)),
        ],
        compiler_params=params(),
        name="attention_forward",
    )(place, q, *blocks, pk_rev, pq_rev, doc_i, doc_j)


def backward_kernel(
    scale,
    q_ref,
    k_ref,
    v_ref,
    pk_ref,
    pq_ref,
    p_ref,
    dm_ref,
    dq_ref,
    dkv_ref,
    dpk_ref,
    dpq_ref,
    ds_all,
    to_all,
    dk_pos,
    dm_all,
    q_all,
    qr_all,
    dpq_sum,
):
    rows, width = q_ref.shape
    keys = k_ref.shape[0]
    heads = width // HEAD_DIM
    win = pk_ref.shape[0]
    row = lax.broadcasted_iota(jnp.int32, (rows, rows), 0)
    col = lax.broadcasted_iota(jnp.int32, (rows, rows), 1)
    flip = jnp.where(row + col == rows - 1, 1.0, 0.0).astype(BF16)
    q_back = dot(flip, q_ref[...], 1, 0)
    content = jnp.zeros((rows, width), F32)
    position = jnp.zeros((rows, width), F32)
    dpq_sum[...] = jnp.zeros_like(dpq_sum)
    for head in range(heads):
        here = slice(head * rows, (head + 1) * rows)
        mask = head_mask((rows, width), head)
        dm = only_head(dm_ref[...], head)
        dm_all[here, :] = dm
        q_all[here, :] = only_head(q_ref[...], head)
        qr_all[here, :] = only_head(q_back, head)
        p = p_ref[head].astype(F32)
        da = dot(dm, v_ref[...], 1, 1)
        ds = (p * (da - jnp.sum(p * da, axis=1, keepdims=True))).astype(BF16)
        ds_all[here, :] = ds
        content = jnp.where(mask, dot(ds, k_ref[...], 1, 0), content)
        ds_back = dot(flip, ds, 1, 0)
        to = jnp.concatenate([ds_back, jnp.zeros((rows, win - keys), F32)], axis=1)
        to = pltpu.roll(to, 0, 1, stride=1, stride_axis=0).astype(BF16)
        to_all[here, :] = to
        position = jnp.where(mask, dot(to, pk_ref[...], 1, 0), position)
        for start in range(0, keys, BLOCK):
            off = ds_back[:, start : start + BLOCK].T
            off = jnp.concatenate([off, jnp.zeros((BLOCK, BLOCK), F32)], axis=1)
            off = pltpu.roll(off, 0, 1, stride=1, stride_axis=0).astype(BF16)
            key_block = only_head(k_ref[start : start + BLOCK, :], head)
            dpq_sum[start : start + 2 * BLOCK, :] += dot(off, key_block, 0, 0)
            more = dot(off, pq_ref[start : start + 2 * BLOCK, :], 1, 0)
            if head:
                more = jnp.where(
                    head_mask(more.shape, head), more, dk_pos[start : start + BLOCK, :]
                )
            dk_pos[start : start + BLOCK, :] = more
    high = position.astype(BF16)
    low = (position - high.astype(F32)).astype(BF16)
    dq = content + dot(flip, high, 1, 0) + dot(flip, low, 1, 0)
    dq_ref[...] = (scale * dq).astype(BF16)
    dkv_ref[:, :width] = (dot(ds_all[...], q_all[...], 0, 0) + dk_pos[...]).astype(BF16)
    p_all = p_ref[...].reshape(heads * rows, keys)
    dkv_ref[:, width:] = dot(p_all, dm_all[...], 0, 0).astype(BF16)
    dpk_ref[...] = dot(to_all[...], qr_all[...], 0, 0).astype(BF16)
    dpq_ref[...] = (scale * dpq_sum[...]).astype(BF16)


def attention_backward(q, k, v, pk_rev, pq_win, p, dm, scale):
    rows, width = q.shape
    keys = k.shape[0]
    heads = width // HEAD_DIM
    win = pk_rev.shape[0]
    return pl.pallas_call(
        functools.partial(backward_kernel, scale),
        out_shape=(
            jax.ShapeDtypeStruct((rows, width), BF16),
            jax.ShapeDtypeStruct((keys, 2 * width), BF16),
            jax.ShapeDtypeStruct((win, width), BF16),
            jax.ShapeDtypeStruct((win, width), BF16),
        ),
        scratch_shapes=[
            pltpu.VMEM((heads * rows, keys), BF16),
            pltpu.VMEM((heads * rows, win), BF16),
            pltpu.VMEM((keys, width), F32),
            pltpu.VMEM((heads * rows, width), BF16),
            pltpu.VMEM((heads * rows, width), BF16),
            pltpu.VMEM((heads * rows, width), BF16),
            pltpu.VMEM((win, width), F32),
        ],
        compiler_params=params(),
        name="attention_backward",
    )(q, k, v, pk_rev, pq_win, p, dm)


def shifted(values, axes, count, shift):
    return lax.ppermute(values, axes, [(i, (i + shift) % count) for i in range(count)])


def assemble_kernel(dims, place_ref, *refs):
    pieces, out_ref, sems = refs[:-2], refs[-2], refs[-1]
    core_count, z_count, x_count, zl_count = dims
    core, z, x = place_ref[0], place_ref[1], place_ref[2]
    rows = out_ref.shape[0] // (core_count * z_count * x_count)
    copies = []
    for c_shift in range(core_count):
        for z_shift in range(z_count):
            piece = pieces[c_shift * z_count + z_shift]
            for x_shift in range(x_count):
                from_c = lax.rem(core - c_shift + core_count, core_count)
                from_z = lax.rem(z - z_shift + z_count, z_count)
                from_x = lax.rem(x - x_shift + x_count, x_count)
                zh, zl = from_z // zl_count, lax.rem(from_z, zl_count)
                owner = ((zh * core_count + from_c) * x_count + from_x) * zl_count + zl
                start = pl.multiple_of(owner * rows, rows)
                copies.append(
                    pltpu.make_async_copy(
                        piece.at[pl.ds(x_shift * rows, rows), :],
                        out_ref.at[pl.ds(start, rows), :],
                        sems.at[len(copies)],
                    )
                )
    for copy in copies:
        copy.start()
    for copy in copies:
        copy.wait()


def gather_rows(values):
    core_count, x_count, zl_count = (lax.axis_size(a) for a in ("core", "x", "zl"))
    z_count = lax.axis_size("zh") * zl_count
    along_x = [values] + [shifted(values, "x", x_count, s) for s in range(1, x_count)]
    along_x = jnp.concatenate(along_x, axis=0)
    along_z = [along_x] + [shifted(along_x, ZED, z_count, s) for s in range(1, z_count)]
    other = [shifted(piece, "core", core_count, 1) for piece in along_z]
    place = jnp.stack([lax.axis_index("core"), lax.axis_index(ZED), lax.axis_index("x")])
    owners = core_count * z_count * x_count
    return pl.pallas_call(
        functools.partial(assemble_kernel, (core_count, z_count, x_count, zl_count)),
        in_specs=[pl.BlockSpec(memory_space=pltpu.SMEM)]
        + [pl.BlockSpec(memory_space=pl.ANY)] * (2 * z_count),
        out_specs=pl.BlockSpec(memory_space=pl.ANY),
        out_shape=jax.ShapeDtypeStruct((owners * values.shape[0], values.shape[1]), BF16),
        scratch_shapes=[pltpu.SemaphoreType.DMA((owners,))],
        compiler_params=params(),
        name="assemble",
    )(place.astype(jnp.int32), *along_z, *other)


def tp_sum(values):
    low = values.astype(BF16)
    count = lax.axis_size("tp")
    parts = [low] + [shifted(low, "tp", count, s) for s in range(1, count)]
    parts = [part.astype(F32) for part in parts]
    return (parts[0] + parts[2]) + (parts[1] + parts[3])


def core_columns(values, core):
    zh = lax.axis_size("zh")
    run = values.shape[1] // (zh * lax.axis_size("core"))
    picked = [
        lax.dynamic_slice_in_dim(values, (2 * part + core) * run, run, 1) for part in range(zh)
    ]
    return jnp.concatenate(picked, axis=1)


def core_rows(values, core):
    zh = lax.axis_size("zh")
    run = values.shape[0] // (zh * lax.axis_size("core"))
    picked = [
        lax.dynamic_slice_in_dim(values, (2 * part + core) * run, run, 0) for part in range(zh)
    ]
    return jnp.concatenate(picked, axis=0)


def scatter_rows(make):
    core = lax.axis_index("core")
    other = make(1 - core).astype(BF16)
    arrived = shifted(other, "core", 2, 1)
    total = (make(core) + arrived.astype(F32)).astype(BF16)
    owners = lax.axis_size(PLANE)
    rows = total.shape[0] // owners
    moved = lax.all_to_all(total.reshape(owners, rows, total.shape[1]), PLANE, 0, 0)
    return jnp.sum(moved.astype(F32), axis=0)


def normalize(values, gain_vec, offset):
    average = jnp.mean(values, axis=-1, keepdims=True)
    centered = values - average
    spread = jnp.mean(centered * centered, axis=-1, keepdims=True)
    return centered * lax.rsqrt(spread + EPS) * gain_vec + offset


def normalize_back(values, gain_vec, grad):
    average = jnp.mean(values, axis=-1, keepdims=True)
    centered = values - average
    spread = jnp.mean(centered * centered, axis=-1, keepdims=True)
    inverse = lax.rsqrt(spread + EPS)
    unit = centered * inverse
    scaled = grad * gain_vec
    back = (
        scaled
        - jnp.mean(scaled, axis=-1, keepdims=True)
        - unit * jnp.mean(scaled * unit, axis=-1, keepdims=True)
    ) * inverse
    return back, grad * unit


def gelu(values):
    return jax.nn.gelu(values, approximate=False)


def local(
    tokens,
    cotangent,
    w_qkv,
    w_attn,
    w_in,
    w_out,
    ln_gain,
    ln_bias,
    rel_emb,
    rel_gain,
    rel_bias,
    doc_ids,
    rel_bucket,
):
    _, rows, model = tokens.shape
    layers = w_qkv.shape[0]
    own = w_qkv.shape[2]
    width = w_qkv.shape[3]
    hidden_units = w_in.shape[2]
    ctx_count = lax.axis_size(CTX)
    length = rows * ctx_count
    ctx = lax.axis_index(CTX)
    row_start = ctx * rows
    scale = 1.0 / math.sqrt(3.0 * HEAD_DIM)
    win = length + rows

    first_qkv = jnp.concatenate([w_qkv[0, i] for i in range(3)], axis=1)
    small = jnp.concatenate(
        [
            ln_gain.reshape(2 * layers, own),
            ln_bias.reshape(2 * layers, own),
            rel_gain[None],
            rel_bias[None],
            doc_ids.astype(BF16).reshape(rows // own, own),
        ],
        axis=0,
    )
    small_rows = small.shape[0]
    small = jnp.pad(small, ((0, 128 - small_rows), (0, 0))).T
    rel_own = rel_emb.shape[0]
    rel_flat = rel_emb.reshape(own, rel_own * model // own)
    rest = [
        jnp.concatenate([w_attn[layer].T, w_in[layer], w_out[layer].T], axis=1)
        for layer in range(layers)
    ]
    start_pack = gather_rows(jnp.concatenate([first_qkv, rel_flat, small], axis=1))
    rest_full = [gather_rows(rest[0])]
    qkv_full = [start_pack[:, : 3 * width]]
    for layer in range(1, layers):
        pack = jnp.concatenate([w_qkv[layer, i] for i in range(3)] + [rest[layer]], axis=1)
        full = gather_rows(pack)
        qkv_full.append(full[:, : 3 * width])
        rest_full.append(full[:, 3 * width :])
    rel_cols = rel_flat.shape[1]
    rel_whole = start_pack[:, 3 * width : 3 * width + rel_cols].reshape(-1, model).astype(F32)
    bucket_count = rel_whole.shape[0]
    small_all = start_pack[:, 3 * width + rel_cols :].T
    gains = small_all[: 2 * layers].astype(F32).reshape(layers, 2, model)
    shifts = small_all[2 * layers : 4 * layers].astype(F32).reshape(layers, 2, model)
    rel_gain_all = small_all[4 * layers].astype(F32)
    rel_bias_all = small_all[4 * layers + 1].astype(F32)
    fsdp = lax.axis_index(("zh", "core"))
    docs = small_all[4 * layers + 2 : small_rows]
    docs = lax.dynamic_slice_in_dim(docs, fsdp * (ctx_count * own), ctx_count * own, 1)
    docs = docs.reshape(rows // own, ctx_count, own).swapaxes(0, 1).reshape(1, length)
    doc_j = docs.astype(jnp.int32)
    doc_i = doc_ids.reshape(rows, 1)

    rel_low = normalize(rel_whole, rel_gain_all, rel_bias_all).astype(BF16)

    padded = jnp.pad(rel_bucket, (1, 1), mode="edge")
    to_index = lax.dynamic_slice_in_dim(padded, row_start, win, 0)[::-1]
    from_index = lax.dynamic_slice_in_dim(padded, length - rows - row_start + 1, win, 0)
    ids = lax.broadcasted_iota(jnp.int32, (win, bucket_count), 1)
    to_table = (to_index[:, None] == ids).astype(BF16)
    from_table = (from_index[:, None] == ids).astype(BF16)
    from_back = (from_index[::-1][:, None] == ids).astype(BF16)
    place = jnp.stack([ctx]).astype(jnp.int32)

    stream = tokens[0].astype(F32)
    kept = []
    for layer in range(layers):
        qkv = qkv_full[layer]
        attn_t = rest_full[layer][:, :width]
        w_in_full = rest_full[layer][:, width : width + hidden_units]
        w_out_t = rest_full[layer][:, width + hidden_units :]
        stream_low = stream.astype(BF16)
        key_value = dot(stream_low, qkv[:, width:], 1, 0).astype(BF16)
        blocks = [key_value] + [shifted(key_value, CTX, ctx_count, s) for s in range(1, ctx_count)]
        q = (scale * dot(stream_low, qkv[:, :width], 1, 0)).astype(BF16)
        pos_q = (scale * dot(rel_low, qkv[:, :width], 1, 0)).astype(BF16)
        pos_k = dot(rel_low, qkv[:, width : 2 * width], 1, 0).astype(BF16)
        pk_rev = dot(to_table, pos_k, 1, 0).astype(BF16)
        pq_rev = dot(from_back, pos_q, 1, 0).astype(BF16)
        pq_win = dot(from_table, pos_q, 1, 0).astype(BF16)
        mixture, p, k_all, v_all = attention_forward(
            place, q, blocks, pk_rev, pq_rev, doc_i, doc_j
        )
        pre_hidden = stream + tp_sum(dot(mixture, attn_t, 1, 1))
        hidden = normalize(pre_hidden, gains[layer, 0], shifts[layer, 0])
        hidden_low = hidden.astype(BF16)
        inner_pre = dot(hidden_low, w_in_full, 1, 0)
        active = gelu(inner_pre).astype(BF16)
        pre_out = hidden + tp_sum(dot(active, w_out_t, 1, 1))
        stream = normalize(pre_out, gains[layer, 1], shifts[layer, 1])
        kept.append(
            (stream_low, q, k_all, v_all, pk_rev, pq_win, p, mixture, pre_hidden, hidden_low)
            + (inner_pre, active, pre_out, qkv, attn_t, w_in_full, w_out_t)
        )
    out_local = stream.astype(BF16)

    gradient = cotangent[0].astype(F32)
    results = [None] * layers
    rel_partial = None
    owner_rows = bucket_count // lax.axis_size(OWNERS)
    for layer in reversed(range(layers)):
        (stream_low, q, k_all, v_all, pk_rev, pq_win, p, mixture, pre_hidden, hidden_low) = kept[
            layer
        ][:10]
        (inner_pre, active, pre_out, qkv, attn_t, w_in_full, w_out_t) = kept[layer][10:]
        d_pre_out, gain_rows_out = normalize_back(pre_out, gains[layer, 1], gradient)
        d_out_low = d_pre_out.astype(BF16)
        d_active = dot(d_out_low, w_out_t, 1, 0)
        d_inner = jax.vjp(gelu, inner_pre)[1](d_active)[0].astype(BF16)
        d_hidden = d_pre_out + tp_sum(dot(d_inner, w_in_full, 1, 1))
        d_pre_hidden, gain_rows_hidden = normalize_back(pre_hidden, gains[layer, 0], d_hidden)
        d_attended = d_pre_hidden.astype(BF16)
        d_mixture = dot(d_attended, attn_t, 1, 0).astype(BF16)
        norm_grads = jnp.stack(
            [
                jnp.sum(gain_rows_hidden, axis=0),
                jnp.sum(gain_rows_out, axis=0),
                jnp.sum(d_hidden, axis=0),
                jnp.sum(gradient, axis=0),
            ]
        )
        norm_grads = jnp.pad(norm_grads, ((0, 124), (0, 0)))

        def early(core):
            return jnp.concatenate(
                [
                    dot(core_columns(d_attended, core), mixture, 0, 0),
                    dot(core_columns(hidden_low, core), d_inner, 0, 0),
                    dot(core_columns(d_out_low, core), active, 0, 0),
                    core_columns(norm_grads, core).T,
                ],
                axis=1,
            )

        early_sum = scatter_rows(early)
        dq, dkv, dpk, dpq = attention_backward(q, k_all, v_all, pk_rev, pq_win, p, d_mixture, scale)
        moved = lax.all_to_all(dkv.reshape(ctx_count, rows, 2 * width), CTX, 0, 0)
        dkv_low = jnp.sum(moved.astype(F32), axis=0).astype(BF16)
        d_pos_k = dot(to_table, dpk, 0, 0)
        d_pos_q = dot(from_table, dpq, 0, 0)
        pos_low = jnp.concatenate([d_pos_q, d_pos_k], axis=1).astype(BF16)
        pos_rows = jnp.concatenate(
            [
                d_pos_q.reshape(-1, owner_rows, width),
                d_pos_k.reshape(-1, owner_rows, width),
            ],
            axis=1,
        ).reshape(-1, width)
        dqkv = jnp.concatenate([dq, dkv_low], axis=1)

        def late(core):
            token_part = dot(core_columns(stream_low, core), dqkv, 0, 0)
            rel_part = dot(core_columns(rel_low, core), pos_low, 0, 0)
            token_part = token_part + jnp.pad(rel_part, ((0, 0), (0, width)))
            return jnp.concatenate([token_part, core_rows(pos_rows, core)], axis=1)

        gradient = d_pre_hidden + tp_sum(dot(dqkv, qkv, 1, 1))
        late_sum = scatter_rows(late)
        pos_sum = late_sum[:, 3 * width :].astype(BF16)
        term = dot(pos_sum[:owner_rows], qkv[:, :width], 1, 1) + dot(
            pos_sum[owner_rows:], qkv[:, width : 2 * width], 1, 1
        )
        rel_partial = term if rel_partial is None else rel_partial + term
        results[layer] = (early_sum, late_sum)

    grad_qkv = jnp.stack(
        [
            jnp.stack([late[:, i * width : (i + 1) * width] for i in range(3)])
            for _, late in results
        ]
    )
    grad_attn = jnp.stack([early[:, :width].T for early, _ in results])
    grad_in = jnp.stack([early[:, width : width + hidden_units] for early, _ in results])
    grad_out = jnp.stack(
        [early[:, width + hidden_units : width + 2 * hidden_units].T for early, _ in results]
    )
    norms = [early[:, width + 2 * hidden_units :].T for early, _ in results]
    grad_gain = jnp.stack([n[:2] for n in norms])
    grad_bias = jnp.stack([n[2:4] for n in norms])

    count = lax.axis_size("tp")
    parts = [rel_partial] + [shifted(rel_partial, "tp", count, s) for s in range(1, count)]
    d_rel = (parts[0] + parts[2]) + (parts[1] + parts[3])
    owner = lax.axis_index(OWNERS)
    grad_rel, gain_rows = normalize_back(rel_emb.astype(F32), rel_gain_all, d_rel)
    ends = jnp.stack([jnp.sum(gain_rows, axis=0), jnp.sum(d_rel, axis=0)])
    ends = ends.reshape(2, -1, own).swapaxes(0, 1)
    ends = lax.all_to_all(ends, OWNERS, 0, 0)
    ends = jnp.sum(ends, axis=0)
    return (
        out_local[None],
        gradient.astype(BF16)[None],
        grad_qkv,
        grad_attn,
        grad_in,
        grad_out,
        grad_gain,
        grad_bias,
        grad_rel,
        ends[0],
        ends[1],
    )


def solution(mesh):
    sizes = mesh.shape
    zh, zl, core = 2, 2, 2
    finer = Mesh(
        mesh.devices.reshape(zh, sizes["fsdp"] // zh, sizes["ctx"] // zl, zl, sizes["tp"]),
        ("zh", "core", "x", "zl", "tp"),
    )
    own = OWNERS
    fsdp = ("zh", "core")
    return jax.shard_map(
        local,
        mesh=finer,
        in_specs=(
            P(fsdp, CTX, None),
            P(fsdp, CTX, None),
            P(None, None, own, "tp"),
            P(None, "tp", own),
            P(None, own, "tp"),
            P(None, "tp", own),
            P(None, None, own),
            P(None, None, own),
            P(own, None),
            P(own),
            P(own),
            P(fsdp, CTX),
            P(),
        ),
        out_specs=(
            P(fsdp, CTX, None),
            P(fsdp, CTX, None),
            P(None, None, own, "tp"),
            P(None, "tp", own),
            P(None, own, "tp"),
            P(None, "tp", own),
            P(None, None, own),
            P(None, None, own),
            P(own, None),
            P(own),
            P(own),
        ),
        check_vma=False,
    )
```

time: 4160 us -> 952 us (0.23)
  waiting for transfers between devices: 1860 us -> 164 us
  local copies, waits for them, and re-layouts: 1390 us -> 43.3 us
  blocking collectives: 581 us -> 0 us
  Pallas kernels: 0 us -> 465 us
  matrix products: 218 us -> 79.5 us
  starting transfers between devices: 1.74 us -> 125 us
    reduce_scatter x6 -> x0, waiting for transfers between devices: 796 us -> none  [the longest x2 270 us: local(): lax.psum_scatter(grad_out_w.astype(jnp.bfloat16), ('fsdp', 'ctx'), scatte...]
    unnamed x40 -> x0, waiting for transfers between devices: 612 us -> none
    all_gather x11 -> x0, blocking collectives: 513 us -> none  [the longest x2 133 us: local(): lax.all_gather(ln_bias[layer_id], ('fsdp', 'ctx'), axis=1, tiled=True)]
    pallas_call x0 -> x7, Pallas kernels: none -> 465 us  [the longest x3 427 us: gather_rows(): pl.pallas_call(functools.partial(assemble_kernel, (core_count, z_count, x...]
    convert_element_type x20 -> x3, local copies, waits for them, and re-layouts: 457 us -> 3.71 us  [the longest x1 2.91 us: local(): start_pack[:, 3 * width:3 * width + rel_cols].reshape(-1, model).astype(F32)]
    psum x9 -> x0, waiting for transfers between devices: 386 us -> none  [the longest x4 156 us: back_total(): return lax.psum(values.astype(jnp.bfloat16), 'tp').astype(jnp.float32)]
    pad x22 -> x0, local copies, waits for them, and re-layouts: 386 us -> none  [the longest x6 318 us: skew_key(): jnp.pad(values.reshape(sequences, key_count * window), ((0, 0), (0, key_c...]
    unnamed x636 -> x274, local copies, waits for them, and re-layouts: 207 us -> 12.5 us
  transfers between devices with their start and end apart: 31 -> 82, of which waited for: 22 -> 33; matrix products, arithmetic and copies ran while one was open for 16% -> 16% of each run, Pallas kernels for 0% -> 47%
where the time goes in v1:
time: 952 us; the launch traced here: 943 us
  Pallas kernels  465 us (49%)
  waiting for transfers between devices  164 us (17%)
  starting transfers between devices  125 us (13%)
  matrix products  79.5 us (8%)
  other arithmetic  63.4 us (7%)
  local copies, waits for them, and re-layouts  43.3 us (5%)
    pallas_call x3, Pallas kernels, gather_rows(): pl.pallas_call(functools.partial(assemble_kernel, (core_count, z_count, x...  427 us
    ppermute x75, starting transfers between devices, shifted(): lax.ppermute(values, axes, [(i, (i + shift) % count) for i in range(count)])  92.9 us
    ppermute x75, waiting for transfers between devices, shifted(): lax.ppermute(values, axes, [(i, (i + shift) % count) for i in range(count)])  90.8 us
    dot_general x54, matrix products, dot(): lax.dot_general(a, b, (((ca,), (cb,)), ((), ())), preferred_element_type=...  79.5 us
    all_to_all x4, waiting for transfers between devices, scatter_rows(): lax.all_to_all(total.reshape(owners, rows, total.shape[1]), PLANE, 0, 0)  64.8 us
    pallas_call x2, Pallas kernels, attention_backward(): pl.pallas_call(functools.partial(backward_kernel, scale), out_shape=(jax....  19.1 us
  transfers between devices with their start and end apart: 82, of which 33 were waited for; matrix products, arithmetic and copies ran while one was open for 16% of the time, Pallas kernels for 47%

profile of v1, /device:TPU:0, one launch (start us, length us, event | category | flops | bytes accessed | tf_op | source)
XLA Modules:
  0.0 942.8 jit_solution(10945173560751526423)
XLA Ops:
  39.0 4.0 collective-permute-start.5
  44.8 5.9 collective-permute-done.33
  66.6 89.4 %assemble.3 = bf16[1024,1408]{1,0:T(8,128)(2,1)} custom-call(s32[3]{0:T(128)} %pad_add_fusion.2.place_ref, bf16[128,1408]{1,0:T(8,128)(2,1)} %copy-done.14, bf16[128,1408]{1,0:T(8,128)(2,1)} %copy-done.41, bf16[128,1408]{1,0:T(8,128)(2,1)} %copy-done.42, bf16[128,1408]{1,0:T(8,128)(2,1)} %copy-done.43, bf16[128,1408]{1,0:T(8,128)(2,1)} %copy-done.44, ...), custom_call_target="tpu_custom_call" | custom-call | tf_op jit(solution)/shard_map/assemble/pallas_call | solution.py:254
  197.4 4.7 collective-permute-start.16
  206.3 4.1 collective-permute-start.38
  211.5 9.2 attention_forward.2
  220.7 145.1 %assemble.4 = bf16[1024,2304]{1,0:T(8,128)(2,1)} custom-call(s32[3]{0:T(128)} %pad_add_fusion.2.place_ref, bf16[128,2304]{1,0:T(8,128)(2,1)} %pad_maximum_fusion.5.refs_0_, bf16[128,2304]{1,0:T(8,128)(2,1)} %collective-permute-done.20.refs_1_, bf16[128,2304]{1,0:T(8,128)(2,1)} %collective-permute-done.21.refs_2_, ...), custom_call_target="tpu_custom_call" | custom-call | tf_op jit(solution)/shard_map/assemble/pallas_call | solution.py:254
  374.5 5.5 collective-permute-done.29
  394.9 192.7 %assemble.5 = bf16[1024,3072]{1,0:T(8,128)(2,1)} custom-call(s32[3]{0:T(128)} %pad_add_fusion.2.place_ref, bf16[128,3072]{1,0:T(8,128)(2,1)} %pad_maximum_fusion.4.refs_0_, bf16[128,3072]{1,0:T(8,128)(2,1)} %collective-permute-done.36.refs_1_, bf16[128,3072]{1,0:T(8,128)(2,1)} %collective-permute-done.37.refs_2_, ...), custom_call_target="tpu_custom_call" | custom-call | tf_op jit(solution)/shard_map/assemble/pallas_call | solution.py:254
  597.3 5.0 collective-permute-start.45
  614.7 9.3 attention_forward.3
  633.6 6.5 collective-permute-done.52
  656.1 5.0 collective-permute-done.54
  681.7 9.6 %attention_backward.2 = (bf16[128,256]{1,0:T(8,128)(2,1)}, bf16[1024,512]{1,0:T(8,128)(2,1)}, bf16[1152,256]{1,0:T(8,128)(2,1)}, bf16[1152,256]{1,0:T(8,128)(2,1)}) custom-call(bf16[128,256]{1,0:T(8,128)(2,1)} %fusion.59.q_ref, bf16[1024,256]{1,0:T(8,128)(2,1)} %get-tuple-element.29.k_ref, bf16[1024,256]{1,0:T(8,128)(2,1)} %get-tuple-element.30.v_ref, ...), custom_call_target="tpu_custom_call" | custom-call | tf_op jit(solution)/shard_map/attention_backward/pallas_call | solution.py:190
  691.3 4.9 all-to-all-start
  720.6 6.8 collective-permute-done.60
  741.7 5.6 collective-permute-done.63
  750.2 9.5 %attention_backward.3 = (bf16[128,256]{1,0:T(8,128)(2,1)}, bf16[1024,512]{1,0:T(8,128)(2,1)}, bf16[1152,256]{1,0:T(8,128)(2,1)}, bf16[1152,256]{1,0:T(8,128)(2,1)}) custom-call(bf16[128,256]{1,0:T(8,128)(2,1)} %fusion.61.q_ref, bf16[1024,256]{1,0:T(8,128)(2,1)} %get-tuple-element.34.k_ref, bf16[1024,256]{1,0:T(8,128)(2,1)} %get-tuple-element.35.v_ref, ...), custom_call_target="tpu_custom_call" | custom-call | tf_op jit(solution)/shard_map/attention_backward/pallas_call | solution.py:190
  759.7 5.8 all-to-all-start.1
  772.7 5.3 all-to-all-done.1
  783.6 4.0 all-to-all-start.3
  795.8 11.3 %all-to-all-done.3 = bf16[16,32,1024]{2,1,0:T(8,128)(2,1)S(1)} async-done(((bf16[16,32,1024]{2,1,0:T(8,128)(2,1)}), bf16[16,32,1024]{2,1,0:T(8,128)(2,1)S(1)}, u32[]{:S(2)}, u32[]{:S(2)}) %all-to-all-start.3) | async-done | bytes 1048608 | tf_op jit(solution)/shard_map/all_to_all | solution.py:299
  807.1 4.3 all-to-all-start.2
  820.4 8.8 all-to-all-done.2
  846.5 4.6 all-to-all-start.6
  851.1 4.5 fusion.1
  858.5 4.4 all-to-all-start.5
  867.7 6.7 collective-permute-done.67
  874.4 6.1 collective-permute-done.66
  884.6 14.8 %all-to-all-done.5 = bf16[16,32,2432]{2,1,0:T(8,128)(2,1)} async-done(((bf16[16,32,2432]{2,1,0:T(8,128)(2,1)}), bf16[16,32,2432]{2,1,0:T(8,128)(2,1)}, u32[]{:S(2)}, u32[]{:S(2)}) %all-to-all-start.5) | async-done | bytes 2490400 | tf_op jit(solution)/shard_map/all_to_all | solution.py:299
  899.4 4.0 all-to-all-start.4
  908.6 29.9 %all-to-all-done.4 = bf16[16,32,2432]{2,1,0:T(8,128)(2,1)S(1)} async-done(((bf16[16,32,2432]{2,1,0:T(8,128)(2,1)}), bf16[16,32,2432]{2,1,0:T(8,128)(2,1)S(1)}, u32[]{:S(2)}, u32[]{:S(2)}) %all-to-all-start.4) | async-done | bytes 2490400 | tf_op jit(solution)/shard_map/all_to_all | solution.py:299
  (633 shorter events, 302.1 us)
Async XLA Ops:
  7.7 20.7 %collective-permute-start.2 = (bf16[32,1408]{1,0:T(8,128)(2,1)S(1)}, bf16[32,1408]{1,0:T(8,128)(2,1)S(1)}, u32[]{:S(2)}, u32[]{:S(2)}) collective-permute-start(bf16[32,1408]{1,0:T(8,128)(2,1)S(1)} %constant_dynamic-update-slice_fusion), channel_id=1, source_target_pairs={{0,24},{8,0},{16,8},{24,16},{1,25},{9,1},{17,9},{25,17},{2,26},{10... | collective-permute-start | bytes 270344 | tf_op jit(solution)/shard_map/ppermute | solution.py:213
  10.6 17.8 %collective-permute-start.1 = (bf16[32,1408]{1,0:T(8,128)(2,1)S(1)}, bf16[32,1408]{1,0:T(8,128)(2,1)S(1)}, u32[]{:S(2)}, u32[]{:S(2)}) collective-permute-start(bf16[32,1408]{1,0:T(8,128)(2,1)S(1)} %constant_dynamic-update-slice_fusion), channel_id=1, source_target_pairs={{0,16},{8,24},{16,0},{24,8},{1,17},{9,25},{17,1},{25,9},{2,18},{10... | collective-permute-start | bytes 270344 | tf_op jit(solution)/shard_map/ppermute | solution.py:213
  11.4 20.2 %collective-permute-start = (bf16[32,1408]{1,0:T(8,128)(2,1)S(1)}, bf16[32,1408]{1,0:T(8,128)(2,1)S(1)}, u32[]{:S(2)}, u32[]{:S(2)}) collective-permute-start(bf16[32,1408]{1,0:T(8,128)(2,1)S(1)} %constant_dynamic-update-slice_fusion), channel_id=1, source_target_pairs={{0,8},{8,16},{16,24},{24,0},{1,9},{9,17},{17,25},{25,1},{2,10},{10... | collective-permute-start | bytes 270344 | tf_op jit(solution)/shard_map/ppermute | solution.py:213
  14.8 17.7 %collective-permute-start.19 = (bf16[32,2304]{1,0:T(8,128)(2,1)S(1)}, bf16[32,2304]{1,0:T(8,128)(2,1)S(1)}, u32[]{:S(2)}, u32[]{:S(2)}) collective-permute-start(bf16[32,2304]{1,0:T(8,128)(2,1)S(1)} %pad_maximum_fusion.24), channel_id=1, source_target_pairs={{0,24},{8,0},{16,8},{24,16},{1,25},{9,1},{17,9},{25,17},{2,26},{10... | collective-permute-start | bytes 442376 | tf_op jit(solution)/shard_map/ppermute | solution.py:213
  17.2 17.3 %collective-permute-start.18 = (bf16[32,2304]{1,0:T(8,128)(2,1)S(1)}, bf16[32,2304]{1,0:T(8,128)(2,1)S(1)}, u32[]{:S(2)}, u32[]{:S(2)}) collective-permute-start(bf16[32,2304]{1,0:T(8,128)(2,1)S(1)} %pad_maximum_fusion.24), channel_id=1, source_target_pairs={{0,16},{8,24},{16,0},{24,8},{1,17},{9,25},{17,1},{25,9},{2,18},{10... | collective-permute-start | bytes 442376 | tf_op jit(solution)/shard_map/ppermute | solution.py:213
  32.5 18.9 %collective-permute-start.3 = (bf16[128,1408]{1,0:T(8,128)(2,1)S(1)}, bf16[128,1408]{1,0:T(8,128)(2,1)S(1)}, u32[]{:S(2)}, u32[]{:S(2)}) collective-permute-start(bf16[128,1408]{1,0:T(8,128)(2,1)S(1)} %pad_maximum_fusion.10.refs_0_), channel_id=1, source_target_pairs={{0,4},{4,64},{64,68},{68,0},{1,5},{5,65},{65,69},{69,1},{2,6},{6,6... | collective-permute-start | bytes 1081352 | tf_op jit(solution)/shard_map/ppermute | solution.py:213
  34.5 20.6 %collective-permute-start.4 = (bf16[128,1408]{1,0:T(8,128)(2,1)S(1)}, bf16[128,1408]{1,0:T(8,128)(2,1)S(1)}, u32[]{:S(2)}, u32[]{:S(2)}) collective-permute-start(bf16[128,1408]{1,0:T(8,128)(2,1)S(1)} %pad_maximum_fusion.10.refs_0_), channel_id=1, source_target_pairs={{0,64},{4,68},{64,0},{68,4},{1,65},{5,69},{65,1},{69,5},{2,66},{6,... | collective-permute-start | bytes 1081352 | tf_op jit(solution)/shard_map/ppermute | solution.py:213
  43.9 19.3 %collective-permute-start.20 = (bf16[128,2304]{1,0:T(8,128)(2,1)}, bf16[128,2304]{1,0:T(8,128)(2,1)}, u32[]{:S(2)}, u32[]{:S(2)}) collective-permute-start(bf16[128,2304]{1,0:T(8,128)(2,1)} %pad_maximum_fusion.5.refs_0_), channel_id=1, source_target_pairs={{0,4},{4,64},{64,68},{68,0},{1,5},{5,65},{65,69},{69,1},{2,6},{6,6... | collective-permute-start | bytes 1769480 | tf_op jit(solution)/shard_map/ppermute | solution.py:213
  60.4 116.4 %collective-permute-start.21 = (bf16[128,2304]{1,0:T(8,128)(2,1)}, bf16[128,2304]{1,0:T(8,128)(2,1)}, u32[]{:S(2)}, u32[]{:S(2)}) collective-permute-start(bf16[128,2304]{1,0:T(8,128)(2,1)} %pad_maximum_fusion.5.refs_0_), channel_id=1, source_target_pairs={{0,64},{4,68},{64,0},{68,4},{1,65},{5,69},{65,1},{69,5},{2,66},{6,... | collective-permute-start | bytes 1769480 | tf_op jit(solution)/shard_map/ppermute | solution.py:213
  63.3 114.1 %collective-permute-start.22 = (bf16[128,2304]{1,0:T(8,128)(2,1)}, bf16[128,2304]{1,0:T(8,128)(2,1)}, u32[]{:S(2)}, u32[]{:S(2)}) collective-permute-start(bf16[128,2304]{1,0:T(8,128)(2,1)} %pad_maximum_fusion.5.refs_0_), channel_id=1, source_target_pairs={{0,68},{4,0},{64,4},{68,64},{1,69},{5,1},{65,5},{69,65},{2,70},{6,... | collective-permute-start | bytes 1769480 | tf_op jit(solution)/shard_map/ppermute | solution.py:213
  65.0 115.4 %collective-permute-start.23 = (bf16[128,2304]{1,0:T(8,128)(2,1)}, bf16[128,2304]{1,0:T(8,128)(2,1)}, u32[]{:S(2)}, u32[]{:S(2)}) collective-permute-start(bf16[128,2304]{1,0:T(8,128)(2,1)} %pad_maximum_fusion.5.refs_0_), channel_id=1, source_target_pairs={{0,32},{32,0},{1,33},{33,1},{2,34},{34,2},{3,35},{35,3},{4,36},{36... | collective-permute-start | bytes 1769480 | tf_op jit(solution)/shard_map/ppermute | solution.py:213
  65.0 141.2 %collective-permute-start.24 = (bf16[128,2304]{1,0:T(8,128)(2,1)}, bf16[128,2304]{1,0:T(8,128)(2,1)}, u32[]{:S(2)}, u32[]{:S(2)}) collective-permute-start(bf16[128,2304]{1,0:T(8,128)(2,1)} %collective-permute-done.20.refs_1_), channel_id=1, source_target_pairs={{0,32},{32,0},{1,33},{33,1},{2,34},{34,2},{3,35},{35,3},{4,36},{36... | collective-permute-start | bytes 1769480 | tf_op jit(solution)/shard_map/ppermute | solution.py:213
  160.8 21.9 %collective-permute-start.10 = (bf16[128,512]{1,0:T(8,128)(2,1)S(1)}, bf16[128,512]{1,0:T(8,128)(2,1)}, u32[]{:S(2)}, u32[]{:S(2)}) collective-permute-start(bf16[128,512]{1,0:T(8,128)(2,1)S(1)} %fusion.58.refs_0_), channel_id=1, source_target_pairs={{0,4},{4,8},{8,12},{12,16},{16,20},{20,24},{24,28},{28,0},{1,5},{5... | collective-permute-start | bytes 393224 | tf_op jit(solution)/shard_map/ppermute | solution.py:213
  185.4 184.9 %collective-permute-start.36 = (bf16[128,3072]{1,0:T(8,128)(2,1)}, bf16[128,3072]{1,0:T(8,128)(2,1)}, u32[]{:S(2)}, u32[]{:S(2)}) collective-permute-start(bf16[128,3072]{1,0:T(8,128)(2,1)} %pad_maximum_fusion.4.refs_0_), channel_id=1, source_target_pairs={{0,4},{4,64},{64,68},{68,0},{1,5},{5,65},{65,69},{69,1},{2,6},{6,6... | collective-permute-start | bytes 2359304 | tf_op jit(solution)/shard_map/ppermute | solution.py:213
  190.0 30.7 %collective-permute-start.25 = (bf16[128,2304]{1,0:T(8,128)(2,1)}, bf16[128,2304]{1,0:T(8,128)(2,1)}, u32[]{:S(2)}, u32[]{:S(2)}) collective-permute-start(bf16[128,2304]{1,0:T(8,128)(2,1)} %collective-permute-done.21.refs_2_), channel_id=1, source_target_pairs={{0,32},{32,0},{1,33},{33,1},{2,34},{34,2},{3,35},{35,3},{4,36},{36... | collective-permute-start | bytes 1769480 | tf_op jit(solution)/shard_map/ppermute | solution.py:213
  190.0 30.6 %collective-permute-start.26 = (bf16[128,2304]{1,0:T(8,128)(2,1)}, bf16[128,2304]{1,0:T(8,128)(2,1)}, u32[]{:S(2)}, u32[]{:S(2)}) collective-permute-start(bf16[128,2304]{1,0:T(8,128)(2,1)} %collective-permute-done.22.refs_3_), channel_id=1, source_target_pairs={{0,32},{32,0},{1,33},{33,1},{2,34},{34,2},{3,35},{35,3},{4,36},{36... | collective-permute-start | bytes 1769480 | tf_op jit(solution)/shard_map/ppermute | solution.py:213
  204.9 169.0 %collective-permute-start.37 = (bf16[128,3072]{1,0:T(8,128)(2,1)}, bf16[128,3072]{1,0:T(8,128)(2,1)}, u32[]{:S(2)}, u32[]{:S(2)}) collective-permute-start(bf16[128,3072]{1,0:T(8,128)(2,1)} %pad_maximum_fusion.4.refs_0_), channel_id=1, source_target_pairs={{0,64},{4,68},{64,0},{68,4},{1,65},{5,69},{65,1},{69,5},{2,66},{6,... | collective-permute-start | bytes 2359304 | tf_op jit(solution)/shard_map/ppermute | solution.py:213
  206.3 167.7 %collective-permute-start.38 = (bf16[128,3072]{1,0:T(8,128)(2,1)}, bf16[128,3072]{1,0:T(8,128)(2,1)}, u32[]{:S(2)}, u32[]{:S(2)}) collective-permute-start(bf16[128,3072]{1,0:T(8,128)(2,1)} %pad_maximum_fusion.4.refs_0_), channel_id=1, source_target_pairs={{0,68},{4,0},{64,4},{68,64},{1,69},{5,1},{65,5},{69,65},{2,70},{6,... | collective-permute-start | bytes 2359304 | tf_op jit(solution)/shard_map/ppermute | solution.py:213
  373.9 17.2 %collective-permute-start.39 = (bf16[128,3072]{1,0:T(8,128)(2,1)}, bf16[128,3072]{1,0:T(8,128)(2,1)S(1)}, u32[]{:S(2)}, u32[]{:S(2)}) collective-permute-start(bf16[128,3072]{1,0:T(8,128)(2,1)} %pad_maximum_fusion.4.refs_0_), channel_id=1, source_target_pairs={{0,32},{32,0},{1,33},{33,1},{2,34},{34,2},{3,35},{35,3},{4,36},{36... | collective-permute-start | bytes 2359304 | tf_op jit(solution)/shard_map/ppermute | solution.py:213
  373.9 18.4 %collective-permute-start.40 = (bf16[128,3072]{1,0:T(8,128)(2,1)}, bf16[128,3072]{1,0:T(8,128)(2,1)S(1)}, u32[]{:S(2)}, u32[]{:S(2)}) collective-permute-start(bf16[128,3072]{1,0:T(8,128)(2,1)} %collective-permute-done.36.refs_1_), channel_id=1, source_target_pairs={{0,32},{32,0},{1,33},{33,1},{2,34},{34,2},{3,35},{35,3},{4,36},{36... | collective-permute-start | bytes 2359304 | tf_op jit(solution)/shard_map/ppermute | solution.py:213
  390.3 202.1 %collective-permute-start.32 = (bf16[128,1024]{1,0:T(8,128)(2,1)S(1)}, bf16[128,1024]{1,0:T(8,128)(2,1)S(1)}, u32[]{:S(2)}, u32[]{:S(2)}) collective-permute-start(bf16[128,1024]{1,0:T(8,128)(2,1)S(1)} %fusion.39), channel_id=1, source_target_pairs={{0,3},{1,0},{2,1},{3,2},{4,7},{5,4},{6,5},{7,6},{8,11},{9,8},{10,9... | collective-permute-start | bytes 786440 | tf_op jit(solution)/shard_map/ppermute | solution.py:213
  391.1 201.2 %collective-permute-start.31 = (bf16[128,1024]{1,0:T(8,128)(2,1)S(1)}, bf16[128,1024]{1,0:T(8,128)(2,1)S(1)}, u32[]{:S(2)}, u32[]{:S(2)}) collective-permute-start(bf16[128,1024]{1,0:T(8,128)(2,1)S(1)} %fusion.39), channel_id=1, source_target_pairs={{0,1},{1,2},{2,3},{3,0},{4,5},{5,6},{6,7},{7,4},{8,9},{9,10},{10,1... | collective-permute-start | bytes 786440 | tf_op jit(solution)/shard_map/ppermute | solution.py:213
  392.4 200.0 %collective-permute-start.30 = (bf16[128,1024]{1,0:T(8,128)(2,1)S(1)}, bf16[128,1024]{1,0:T(8,128)(2,1)}, u32[]{:S(2)}, u32[]{:S(2)}) collective-permute-start(bf16[128,1024]{1,0:T(8,128)(2,1)S(1)} %fusion.39), channel_id=1, source_target_pairs={{0,2},{1,3},{2,0},{3,1},{4,6},{5,7},{6,4},{7,5},{8,10},{9,11},{10,... | collective-permute-start | bytes 786440 | tf_op jit(solution)/shard_map/ppermute | solution.py:213
  691.3 16.6 %all-to-all-start = ((bf16[8,128,512]{2,1,0:T(8,128)(2,1)}), bf16[8,128,512]{2,1,0:T(8,128)(2,1)}, u32[]{:S(2)}, u32[]{:S(2)}) async-start(bf16[8,128,512]{2,1,0:T(8,128)(2,1)} %bitcast.230), calls=%async_computation | async-start | bytes 2097152 | tf_op jit(solution)/shard_map/all_to_all | solution.py:481
  702.3 148.7 %collective-permute-start.71 = (bf16[512,2432]{1,0:T(8,128)(2,1)}, bf16[512,2432]{1,0:T(8,128)(2,1)}, u32[]{:S(2)}, u32[]{:S(2)}) collective-permute-start(bf16[512,2432]{1,0:T(8,128)(2,1)} %pad_maximum_fusion.1), channel_id=1, source_target_pairs={{0,32},{32,0},{1,33},{33,1},{2,34},{34,2},{3,35},{35,3},{4,36},{36... | collective-permute-start | bytes 7471112 | tf_op jit(solution)/shard_map/ppermute | solution.py:213
  717.1 63.9 %collective-permute-start.69 = (bf16[512,1024]{1,0:T(8,128)(2,1)}, bf16[512,1024]{1,0:T(8,128)(2,1)}, u32[]{:S(2)}, u32[]{:S(2)}) collective-permute-start(bf16[512,1024]{1,0:T(8,128)(2,1)} %maximum_maximum_fusion.1), channel_id=1, source_target_pairs={{0,32},{32,0},{1,33},{33,1},{2,34},{34,2},{3,35},{35,3},{4,36},{36... | collective-permute-start | bytes 3145736 | tf_op jit(solution)/shard_map/ppermute | solution.py:213
  759.7 18.2 %all-to-all-start.1 = ((bf16[8,128,512]{2,1,0:T(8,128)(2,1)}), bf16[8,128,512]{2,1,0:T(8,128)(2,1)S(1)}, u32[]{:S(2)}, u32[]{:S(2)}) async-start(bf16[8,128,512]{2,1,0:T(8,128)(2,1)} %bitcast.231), calls=%async_computation.1 | async-start | bytes 2097152 | tf_op jit(solution)/shard_map/all_to_all | solution.py:481
  783.6 23.5 %all-to-all-start.3 = ((bf16[16,32,1024]{2,1,0:T(8,128)(2,1)}), bf16[16,32,1024]{2,1,0:T(8,128)(2,1)S(1)}, u32[]{:S(2)}, u32[]{:S(2)}) async-start(bf16[16,32,1024]{2,1,0:T(8,128)(2,1)} %bitcast.225), calls=%async_computation.3 | async-start | bytes 2097152 | tf_op jit(solution)/shard_map/all_to_all | solution.py:299
  807.1 22.1 %all-to-all-start.2 = ((bf16[16,32,1024]{2,1,0:T(8,128)(2,1)}), bf16[16,32,1024]{2,1,0:T(8,128)(2,1)}, u32[]{:S(2)}, u32[]{:S(2)}) async-start(bf16[16,32,1024]{2,1,0:T(8,128)(2,1)} %bitcast.52), calls=%async_computation.2 | async-start | bytes 2097152 | tf_op jit(solution)/shard_map/all_to_all | solution.py:299
  838.5 43.0 %collective-permute-start.70 = (bf16[512,2432]{1,0:T(8,128)(2,1)}, bf16[512,2432]{1,0:T(8,128)(2,1)}, u32[]{:S(2)}, u32[]{:S(2)}) collective-permute-start(bf16[512,2432]{1,0:T(8,128)(2,1)} %pad_maximum_fusion), channel_id=1, source_target_pairs={{0,32},{32,0},{1,33},{33,1},{2,34},{34,2},{3,35},{35,3},{4,36},{36... | collective-permute-start | bytes 7471112 | tf_op jit(solution)/shard_map/ppermute | solution.py:213
  858.5 40.9 %all-to-all-start.5 = ((bf16[16,32,2432]{2,1,0:T(8,128)(2,1)}), bf16[16,32,2432]{2,1,0:T(8,128)(2,1)}, u32[]{:S(2)}, u32[]{:S(2)}) async-start(bf16[16,32,2432]{2,1,0:T(8,128)(2,1)} %bitcast.220), calls=%async_computation.5 | async-start | bytes 4980736 | tf_op jit(solution)/shard_map/all_to_all | solution.py:299
  899.4 39.1 %all-to-all-start.4 = ((bf16[16,32,2432]{2,1,0:T(8,128)(2,1)}), bf16[16,32,2432]{2,1,0:T(8,128)(2,1)S(1)}, u32[]{:S(2)}, u32[]{:S(2)}) async-start(bf16[16,32,2432]{2,1,0:T(8,128)(2,1)} %bitcast.71), calls=%async_computation.4 | async-start | bytes 4980736 | tf_op jit(solution)/shard_map/all_to_all | solution.py:299
  (184 other events, 3208.2 us)

commit v2 on v1

v2 whole, which is shorter than its diff:
```python
import functools
import math

import jax
import jax.numpy as jnp
from jax import lax
from jax.experimental import pallas as pl
from jax.experimental.pallas import tpu as pltpu
from jax.sharding import Mesh
from jax.sharding import PartitionSpec as P

HEAD_DIM = 64
EPS = 1e-07
NEG = -1e30
BLOCK = 128
LANES = 128
F32 = jnp.float32
BF16 = jnp.bfloat16
CTX = ("x", "zl")
ZED = ("zh", "zl")
PLANE = ("zh", "x", "zl")
OWNERS = ("zh", "core", "x", "zl")


def dot(a, b, ca, cb):
    return lax.dot_general(a, b, (((ca,), (cb,)), ((), ())), preferred_element_type=F32)


def call(body, outs, ins, *, anys=(), smem=(), scratch=(), limit=32, name=None):
    specs = []
    for i in range(len(ins)):
        space = pl.ANY if i in anys else pltpu.SMEM if i in smem else pltpu.VMEM
        specs.append(pl.BlockSpec(memory_space=space))
    return pl.pallas_call(
        body,
        in_specs=specs,
        out_specs=tuple(pl.BlockSpec(memory_space=pltpu.VMEM) for _ in outs),
        out_shape=tuple(jax.ShapeDtypeStruct(shape, dtype) for shape, dtype in outs),
        scratch_shapes=list(scratch),
        compiler_params=pltpu.CompilerParams(vmem_limit_bytes=limit << 20),
        name=name,
    )(*ins)


def head_mask(shape, head, axis=1):
    index = lax.broadcasted_iota(jnp.int32, shape, axis)
    return (index >= head * HEAD_DIM) & (index < (head + 1) * HEAD_DIM)


def only_head(values, head, axis=1):
    mask = head_mask(values.shape, head, axis)
    return jnp.where(mask, values.astype(F32), 0.0).astype(BF16)


def unit_of(values):
    average = jnp.mean(values, axis=-1, keepdims=True)
    centered = values - average
    spread = jnp.mean(centered * centered, axis=-1, keepdims=True)
    inverse = lax.rsqrt(spread + EPS)
    return centered * inverse, inverse


def normalize_back(values, gain_vec, grad):
    unit, inverse = unit_of(values)
    scaled = grad * gain_vec
    back = (
        scaled
        - jnp.mean(scaled, axis=-1, keepdims=True)
        - unit * jnp.mean(scaled * unit, axis=-1, keepdims=True)
    ) * inverse
    return back, grad * unit


def sum_pieces(pieces):
    parts = [piece[...].astype(F32) for piece in pieces]
    return (parts[0] + parts[2]) + (parts[1] + parts[3])


def pack_start_kernel(qkv_ref, rel_ref, gain_ref, bias_ref, rgain_ref, rbias_ref, doc_ref, out_ref, scr):
    own, width = qkv_ref.shape[2], qkv_ref.shape[3]
    layers = qkv_ref.shape[0]
    for i in range(3):
        out_ref[:, i * width : (i + 1) * width] = qkv_ref[0, i]
    at = 3 * width
    half = rel_ref.shape[1] // 2
    rel_rows = rel_ref.shape[0]
    out_ref[:rel_rows, at : at + half] = rel_ref[:, :half]
    out_ref[rel_rows:, at : at + half] = rel_ref[:, half:]
    at += half
    scr[...] = jnp.zeros_like(scr)
    for layer in range(layers):
        scr[2 * layer : 2 * layer + 2, :own] = gain_ref[layer].astype(F32)
        base = 2 * layers + 2 * layer
        scr[base : base + 2, :own] = bias_ref[layer].astype(F32)
    scr[4 * layers : 4 * layers + 1, :own] = rgain_ref[...].astype(F32)
    scr[4 * layers + 1 : 4 * layers + 2, :own] = rbias_ref[...].astype(F32)
    small = scr[...].T[:own, :]
    row = lax.broadcasted_iota(jnp.int32, small.shape, 0)
    upper = lax.broadcasted_iota(jnp.int32, small.shape, 1) >= LANES // 2
    doc = doc_ref[...].astype(F32)
    turned = pltpu.roll(doc, LANES // 2, 1)
    small = jnp.where(upper & (row == 0), turned, small)
    small = jnp.where(upper & (row == 1), doc, small)
    out_ref[:, at : at + LANES] = small.astype(BF16)


def pack_rest_kernel(layer, with_qkv, qkv_ref, attn_ref, in_ref, out_w_ref, pack_ref):
    width = qkv_ref.shape[3]
    hidden = in_ref.shape[2]
    at = 0
    if with_qkv:
        for i in range(3):
            pack_ref[:, i * width : (i + 1) * width] = qkv_ref[layer, i]
        at = 3 * width
    pack_ref[:, at : at + width] = attn_ref[layer].astype(F32).T.astype(BF16)
    at += width
    pack_ref[:, at : at + hidden] = in_ref[layer]
    at += hidden
    pack_ref[:, at : at + hidden] = out_w_ref[layer].astype(F32).T.astype(BF16)


def assemble(dims, place_ref, pieces, moves, sems):
    core_count, z_count, x_count, zl_count, own = dims
    core, z, x = place_ref[0], place_ref[1], place_ref[2]
    copies = []
    for c_shift in range(core_count):
        for z_shift in range(z_count):
            piece = pieces[c_shift * z_count + z_shift]
            for x_shift in range(x_count):
                from_c = lax.rem(core - c_shift + core_count, core_count)
                from_z = lax.rem(z - z_shift + z_count, z_count)
                from_x = lax.rem(x - x_shift + x_count, x_count)
                zh, zl = lax.div(from_z, zl_count), lax.rem(from_z, zl_count)
                owner = ((zh * core_count + from_c) * x_count + from_x) * zl_count + zl
                for row, rows, col, cols, target, step, to_col in moves:
                    start = pl.multiple_of(owner * step, step)
                    copies.append(
                        pltpu.make_async_copy(
                            piece.at[pl.ds(x_shift * own + row, rows), pl.ds(col, cols)],
                            target.at[pl.ds(start, rows), pl.ds(to_col, cols)],
                            sems.at[len(copies)],
                        )
                    )
    for copy in copies:
        copy.start()
    for copy in copies:
        copy.wait()


def start_kernel(dims, scale, place_ref, *refs):
    pieces, (tokens_ref, qkv_ref, rel_ref, small_ref, q_ref, kv_ref, sems) = refs[:-7], refs[-7:]
    own = dims[-1]
    wide = qkv_ref.shape[1]
    width = wide // 3
    half = rel_ref.shape[1] // 2
    part = own // 2
    moves = (
        (0, own, 0, wide, qkv_ref, own, 0),
        (0, part, wide, half, rel_ref, part, 0),
        (part, part, wide, half, rel_ref, part, half),
        (0, own, wide + half, LANES, small_ref, own, 0),
    )
    assemble(dims, place_ref, pieces, moves, sems)
    low = tokens_ref[...]
    kv_ref[...] = dot(low, qkv_ref[:, width:], 1, 0).astype(BF16)
    q_ref[...] = (scale * dot(low, qkv_ref[:, :width], 1, 0)).astype(BF16)


def rest_kernel(dims, outs, place_ref, *refs):
    pieces, targets, sems = refs[: -outs - 1], refs[-outs - 1 : -1], refs[-1]
    own = dims[-1]
    moves, at = [], 0
    for target in targets:
        cols = target.shape[1]
        moves.append((0, own, at, cols, target, own, 0))
        at += cols
    assemble(dims, place_ref, pieces, moves, sems)


def relative_kernel(layers, owners, place_ref, rel_ref, small_ref, low_ref, vec_ref, doc_ref):
    turned = small_ref[...].astype(F32).T[: vec_ref.shape[0], :]
    vec_ref[...] = turned
    unit, _ = unit_of(rel_ref[...].astype(F32))
    gain, bias = turned[4 * layers : 4 * layers + 1], turned[4 * layers + 1 : 4 * layers + 2]
    low_ref[...] = (unit * gain + bias).astype(BF16)
    length = doc_ref.shape[1]
    blocks = length // LANES
    fsdp = place_ref[0]
    own = small_ref.shape[0] // owners
    span = blocks * own
    mine = small_ref[pl.ds(pl.multiple_of(fsdp * span, span), span), :].astype(F32)
    upper = lax.broadcasted_iota(jnp.int32, (1, LANES), 1) >= LANES // 2
    for block in range(blocks):
        first = pltpu.roll(mine[block * own : block * own + 1, :], LANES // 2, 1)
        second = mine[block * own + 1 : block * own + 2, :]
        doc_ref[:, block * LANES : (block + 1) * LANES] = jnp.where(upper, second, first)


def table_kernel(index_ref, table_ref):
    count, buckets, win = table_ref.shape
    bucket = lax.broadcasted_iota(jnp.int32, (buckets, win), 0)
    for i in range(count):
        same = bucket == index_ref[i : i + 1, :]
        table_ref[i] = jnp.where(same, 1.0, 0.0).astype(BF16)


def position_kernel(scale, rel_ref, qkv_ref, table_ref, pk_ref, pq_rev_ref, pq_ref):
    width = qkv_ref.shape[1] // 3
    pos_q = (scale * dot(rel_ref[...], qkv_ref[:, :width], 1, 0)).astype(BF16)
    pos_k = dot(rel_ref[...], qkv_ref[:, width : 2 * width], 1, 0).astype(BF16)
    pk_ref[...] = dot(pos_k, table_ref[0], 0, 0).astype(BF16)
    pq_rev_ref[...] = dot(pos_q, table_ref[1], 0, 0).astype(BF16)
    pq_ref[...] = dot(pos_q, table_ref[2], 0, 0).astype(BF16)


def project_kernel(scale, rows_of, hidden_ref, *refs):
    pieces, rest = refs[:4], refs[4:]
    vec_ref, qkv_ref, pre_ref, stream_ref, low_ref, q_ref, kv_ref = rest
    width = qkv_ref.shape[1] // 3
    gain, bias = rows_of
    pre = hidden_ref[...] + sum_pieces(pieces)
    pre_ref[...] = pre
    unit, _ = unit_of(pre)
    stream = unit * vec_ref[gain : gain + 1, :] + vec_ref[bias : bias + 1, :]
    stream_ref[...] = stream
    low = stream.astype(BF16)
    low_ref[...] = low
    kv_ref[...] = dot(low, qkv_ref[:, width:], 1, 0).astype(BF16)
    q_ref[...] = (scale * dot(low, qkv_ref[:, :width], 1, 0)).astype(BF16)


def attention_kernel(place_ref, q_ref, *refs):
    blocks, rest = refs[:-12], refs[-12:]
    pk_ref, pq_ref, doc_i_ref, doc_j_ref, attn_ref = rest[:5]
    part_ref, mix_ref, p_ref, kv_ref, to_ref, q_all, sems = rest[5:]
    count = len(blocks)
    rows, width = q_ref.shape
    keys = kv_ref.shape[0]
    win = pk_ref.shape[1]
    heads = width // HEAD_DIM
    mine = place_ref[1]
    copies = []
    for shift, block in enumerate(blocks):
        owner = lax.rem(mine - shift + count, count)
        start = pl.multiple_of(owner * rows, rows)
        copies.append(
            pltpu.make_async_copy(block, kv_ref.at[pl.ds(start, rows), :], sems.at[shift])
        )
    for copy in copies:
        copy.start()
    for head in range(heads):
        q = only_head(q_ref[...], head)
        q_all[head] = q
        to = dot(q, pk_ref[...], 1, 0)
        to = pltpu.roll(to, win + 1 - rows, 1, stride=1, stride_axis=0)
        to_ref[head] = to[:, :keys]
    doc_i = jnp.broadcast_to(doc_i_ref[...].astype(F32), (rows, rows)).T
    for copy in copies:
        copy.wait()
    mix = jnp.zeros((rows, width), F32)
    for head in range(heads):
        q = q_all[head]
        parts = []
        for start in range(0, keys, BLOCK):
            key_block = kv_ref[start : start + BLOCK, :width]
            first = win - 2 * BLOCK - start
            pq = only_head(pq_ref[:, first : first + 2 * BLOCK], head, 0)
            off = dot(key_block, pq, 1, 0)
            off = pltpu.roll(off, BLOCK, 1, stride=1, stride_axis=0)
            s = dot(q, key_block, 1, 1) + to_ref[head, :, start : start + BLOCK]
            s = s + off[:, :BLOCK].T
            same = doc_i == doc_j_ref[:, start : start + BLOCK]
            parts.append(jnp.where(same, s, NEG))
        s = jnp.concatenate(parts, axis=1)
        e = jnp.exp(s - jnp.max(s, axis=1, keepdims=True))
        p = (e / jnp.sum(e, axis=1, keepdims=True)).astype(BF16)
        p_ref[head] = p
        mix = jnp.where(head_mask(mix.shape, head), dot(p, kv_ref[:, width:], 1, 0), mix)
    mix = mix.astype(BF16)
    mix_ref[...] = mix
    part_ref[...] = dot(mix, attn_ref[...], 1, 1).astype(BF16)


def feed_kernel(rows_of, stream_ref, *refs):
    pieces, rest = refs[:4], refs[4:]
    vec_ref, in_ref, out_ref = rest[:3]
    pre_ref, hidden_ref, low_ref, slope_ref, active_ref, part_ref = rest[3:]
    gain, bias = rows_of
    pre = stream_ref[...].astype(F32) + sum_pieces(pieces)
    pre_ref[...] = pre
    unit, _ = unit_of(pre)
    hidden = unit * vec_ref[gain : gain + 1, :] + vec_ref[bias : bias + 1, :]
    hidden_ref[...] = hidden
    low = hidden.astype(BF16)
    low_ref[...] = low
    inner = dot(low, in_ref[...], 1, 0)
    below = 0.5 * (1.0 + lax.erf(inner * math.sqrt(0.5)))
    bell = jnp.exp(-0.5 * inner * inner) * (1.0 / math.sqrt(2.0 * math.pi))
    slope_ref[...] = below + inner * bell
    active = (inner * below).astype(BF16)
    active_ref[...] = active
    part_ref[...] = dot(active, out_ref[...], 1, 1).astype(BF16)


def end_kernel(rows_of, hidden_ref, *refs):
    pieces, (vec_ref, pre_ref, out_ref) = refs[:4], refs[4:]
    gain, bias = rows_of
    pre = hidden_ref[...] + sum_pieces(pieces)
    pre_ref[...] = pre
    unit, _ = unit_of(pre)
    stream = unit * vec_ref[gain : gain + 1, :] + vec_ref[bias : bias + 1, :]
    out_ref[...] = stream.astype(BF16)


def column_sums(ref, first, second):
    ref[...] = jnp.zeros_like(ref)
    ref[0:1, :] = jnp.sum(first, axis=0, keepdims=True)
    ref[1:2, :] = jnp.sum(second, axis=0, keepdims=True)


def feed_back_kernel(gain, has_pieces, grad_ref, *refs):
    pieces, rest = (refs[:4], refs[4:]) if has_pieces else ((), refs)
    pre_ref, vec_ref, slope_ref, in_ref, out_ref = rest[:5]
    d_pre_ref, d_low_ref, d_inner_ref, part_ref, norm_ref = rest[5:]
    grad = grad_ref[...].astype(F32)
    if has_pieces:
        grad = grad + sum_pieces(pieces)
    back, gain_terms = normalize_back(pre_ref[...], vec_ref[gain : gain + 1, :], grad)
    column_sums(norm_ref, gain_terms, grad)
    d_pre_ref[...] = back
    low = back.astype(BF16)
    d_low_ref[...] = low
    inner = (dot(low, out_ref[...], 1, 0) * slope_ref[...]).astype(BF16)
    d_inner_ref[...] = inner
    part_ref[...] = dot(inner, in_ref[...], 1, 1).astype(BF16)


def attention_back_kernel(gain, scale, place_ref, *refs):
    pieces, rest = refs[:4], refs[4:]
    d_out_ref, pre_ref, vec_ref, attn_ref, q_ref, kv_ref, pk_ref, pq_ref, p_ref = rest[:9]
    d_pre_ref, d_low_ref, dq_ref, dpk_ref, dpq_ref, norm_ref = rest[9:15]
    ds_all, to_all, dk_pos, dm_all, q_all, qr_all, dpq_sum, dkv = rest[-8:]
    dkv_refs = rest[15:-8]
    rows, width = q_ref.shape
    keys = kv_ref.shape[0]
    heads = width // HEAD_DIM
    win = pk_ref.shape[1]

    grad = d_out_ref[...] + sum_pieces(pieces)
    back, gain_terms = normalize_back(pre_ref[...], vec_ref[gain : gain + 1, :], grad)
    column_sums(norm_ref, gain_terms, grad)
    d_pre_ref[...] = back
    d_low = back.astype(BF16)
    d_low_ref[...] = d_low
    d_mixture = dot(d_low, attn_ref[...], 1, 0)

    row = lax.broadcasted_iota(jnp.int32, (rows, rows), 0)
    col = lax.broadcasted_iota(jnp.int32, (rows, rows), 1)
    flip = jnp.where(row + col == rows - 1, 1.0, 0.0).astype(BF16)
    q_back = dot(flip, q_ref[...], 1, 0)
    content = jnp.zeros((rows, width), F32)
    position = jnp.zeros((rows, width), F32)
    dpq_sum[...] = jnp.zeros_like(dpq_sum)
    for head in range(heads):
        here = slice(head * rows, (head + 1) * rows)
        mask = head_mask((rows, width), head)
        dm = only_head(d_mixture, head)
        dm_all[here, :] = dm
        q_all[here, :] = only_head(q_ref[...], head)
        qr_all[here, :] = only_head(q_back, head)
        p = p_ref[head].astype(F32)
        da = dot(dm, kv_ref[:, width:], 1, 1)
        ds = (p * (da - jnp.sum(p * da, axis=1, keepdims=True))).astype(BF16)
        ds_all[here, :] = ds
        content = jnp.where(mask, dot(ds, kv_ref[:, :width], 1, 0), content)
        ds_back = dot(flip, ds, 1, 0)
        to = jnp.concatenate([ds_back, jnp.zeros((rows, win - keys), F32)], axis=1)
        to = pltpu.roll(to, 0, 1, stride=1, stride_axis=0).astype(BF16)
        to_all[here, :] = to
        position = jnp.where(mask, dot(to, pk_ref[...], 1, 1), position)
        for start in range(0, keys, BLOCK):
            off = ds_back[:, start : start + BLOCK].T
            off = jnp.concatenate([off, jnp.zeros((BLOCK, BLOCK), F32)], axis=1)
            off = pltpu.roll(off, 0, 1, stride=1, stride_axis=0).astype(BF16)
            key_block = only_head(kv_ref[start : start + BLOCK, :width], head)
            dpq_sum[start : start + 2 * BLOCK, :] += dot(off, key_block, 0, 0)
            more = dot(off, pq_ref[:, start : start + 2 * BLOCK], 1, 1)
            if head:
                more = jnp.where(
                    head_mask(more.shape, head), more, dk_pos[start : start + BLOCK, :]
                )
            dk_pos[start : start + BLOCK, :] = more
    high = position.astype(BF16)
    low = (position - high.astype(F32)).astype(BF16)
    dq = content + dot(flip, high, 1, 0) + dot(flip, low, 1, 0)
    dq_ref[...] = (scale * dq).astype(BF16)
    dkv[:, :width] = (dot(ds_all[...], q_all[...], 0, 0) + dk_pos[...]).astype(BF16)
    p_all = p_ref[...].reshape(heads * rows, keys)
    dkv[:, width:] = dot(p_all, dm_all[...], 0, 0).astype(BF16)
    count = len(dkv_refs)
    for shift, target in enumerate(dkv_refs):
        owner = lax.rem(place_ref[1] + shift, count)
        target[...] = dkv[pl.ds(pl.multiple_of(owner * rows, rows), rows), :]
    dpk_ref[...] = dot(to_all[...], qr_all[...], 0, 0).astype(BF16)
    dpq_ref[...] = (scale * dpq_sum[...]).astype(BF16)


def position_back_kernel(table_ref, dpk_ref, dpq_ref, low_ref, rows_ref):
    width = dpk_ref.shape[1]
    d_k = dot(table_ref[0], dpk_ref[...], 1, 0).astype(BF16)
    d_q = dot(table_ref[2], dpq_ref[...], 1, 0).astype(BF16)
    low_ref[:, :width] = d_q
    low_ref[:, width:] = d_k
    owners, step = rows_ref.shape[0], rows_ref.shape[1] // 2
    for owner in range(owners):
        rows_ref[owner, :step, :] = d_q[owner * step : (owner + 1) * step, :]
        rows_ref[owner, step:, :] = d_k[owner * step : (owner + 1) * step, :]


def picked_columns(ref, core, parts=2):
    run = ref.shape[1] // (2 * parts)
    picked = [ref[:, pl.ds(pl.multiple_of((2 * i + core) * run, run), run)] for i in range(parts)]
    return jnp.concatenate(picked, axis=1)


def early_kernel(own_core, place_ref, *refs):
    d_att_ref, mix_ref, hid_ref, d_inner_ref, d_out_ref, act_ref, norm_h_ref, norm_o_ref = refs[:8]
    out_ref, scr = refs[-2:]
    core = place_ref[2] if own_core else 1 - place_ref[2]
    at = 0
    for left, right in ((d_att_ref, mix_ref), (hid_ref, d_inner_ref), (d_out_ref, act_ref)):
        cols = right.shape[1]
        value = dot(picked_columns(left, core), right[...], 0, 0)
        if own_core:
            value = value + refs[8][:, at : at + cols].astype(F32)
        out_ref[:, at : at + cols] = value.astype(BF16)
        at += cols
    hid = picked_columns(norm_h_ref, core)
    out = picked_columns(norm_o_ref, core)
    scr[...] = jnp.zeros_like(scr)
    scr[0:1, :] = hid[0:1]
    scr[1:2, :] = out[0:1]
    scr[2:3, :] = hid[1:2]
    scr[3:4, :] = out[1:2]
    value = scr[...].T
    if own_core:
        value = value + refs[8][:, at : at + LANES].astype(F32)
    out_ref[:, at : at + LANES] = value.astype(BF16)


def stream_back_kernel(dq_ref, *refs):
    pieces, (qkv_ref, all_ref, part_ref) = refs[:-3], refs[-3:]
    total = pieces[0][...].astype(F32)
    for piece in pieces[1:]:
        total = total + piece[...].astype(F32)
    both = jnp.concatenate([dq_ref[...], total.astype(BF16)], axis=1)
    all_ref[...] = both
    part_ref[...] = dot(both, qkv_ref[...], 1, 1).astype(BF16)


def late_kernel(own_core, place_ref, low_ref, all_ref, rel_ref, pos_ref, *refs):
    out_ref = refs[-1]
    core = place_ref[2] if own_core else 1 - place_ref[2]
    wide = pos_ref.shape[1]
    value = dot(picked_columns(low_ref, core), all_ref[...], 0, 0)
    terms = dot(picked_columns(rel_ref, core), pos_ref[...], 0, 0)
    first = value[:, :wide] + terms
    second = value[:, wide:]
    if own_core:
        first = first + refs[0][:, :wide].astype(F32)
        second = second + refs[0][:, wide:].astype(F32)
    out_ref[:, :wide] = first.astype(BF16)
    out_ref[:, wide:] = second.astype(BF16)


def total_of(ref):
    total = ref[0].astype(F32)
    for i in range(1, ref.shape[0]):
        total = total + ref[i].astype(F32)
    return total


def early_end_kernel(*refs):
    layers = len(refs) - 5
    attn_ref, in_ref, out_ref, gain_ref, bias_ref = refs[layers:]
    width, hidden = attn_ref.shape[1], in_ref.shape[2]
    for layer in range(layers):
        total = total_of(refs[layer])
        attn_ref[layer] = total[:, :width].T
        in_ref[layer] = total[:, width : width + hidden]
        out_ref[layer] = total[:, width + hidden : width + 2 * hidden].T
        norms = total[:, width + 2 * hidden :].T
        gain_ref[layer] = norms[0:2, :]
        bias_ref[layer] = norms[2:4, :]


def late_end_kernel(*refs):
    layers = len(refs) - 1
    out_ref = refs[-1]
    width = out_ref.shape[3]
    for layer in range(layers):
        total = total_of(refs[layer])
        for i in range(3):
            out_ref[layer, i] = total[:, i * width : (i + 1) * width]


def relative_term_kernel(*refs):
    layers = (len(refs) - 1) // 2
    out_ref = refs[-1]
    width = refs[0].shape[2]
    step = refs[0].shape[1] // 2
    total = None
    for layer in range(layers):
        moved = total_of(refs[2 * layer]).astype(BF16)
        qkv_ref = refs[2 * layer + 1]
        term = dot(moved[:step], qkv_ref[:, :width], 1, 1)
        term = term + dot(moved[step:], qkv_ref[:, width : 2 * width], 1, 1)
        total = term if total is None else total + term
    out_ref[...] = total


def relative_end_kernel(gain, *refs):
    pieces, (rel_ref, vec_ref, grad_ref, ends_ref) = refs[:4], refs[4:]
    d_rel = sum_pieces(pieces)
    back, gain_terms = normalize_back(
        rel_ref[...].astype(F32), vec_ref[gain : gain + 1, :], d_rel
    )
    grad_ref[...] = back
    owners, _, own = ends_ref.shape
    for k, terms in enumerate((gain_terms, d_rel)):
        sums = jnp.sum(terms, axis=0, keepdims=True)
        for owner in range(owners):
            first = owner * own // LANES * LANES
            chunk = sums[:, first : first + LANES]
            offset = owner * own - first
            if offset:
                chunk = pltpu.roll(chunk, LANES - offset, 1)
            ends_ref[owner, k : k + 1, :] = chunk[:, :own]


def shifted(values, axes, shift):
    count = lax.axis_size(axes)
    return lax.ppermute(values, axes, [(i, (i + shift) % count) for i in range(count)])


def gather_pieces(values):
    x_count, z_count = lax.axis_size("x"), lax.axis_size(ZED)
    along_x = [values] + [shifted(values, "x", s) for s in range(1, x_count)]
    along_x = jnp.concatenate(along_x, axis=0)
    along_z = [along_x] + [shifted(along_x, ZED, s) for s in range(1, z_count)]
    return along_z + [shifted(piece, "core", 1) for piece in along_z]


def tp_pieces(low):
    return [low] + [shifted(low, "tp", s) for s in range(1, lax.axis_size("tp"))]


def plane_blocks(values):
    owners = lax.axis_size(PLANE)
    blocks = values.reshape(owners, values.shape[0] // owners, values.shape[1])
    return lax.all_to_all(blocks, PLANE, 0, 0)


def local(
    tokens,
    cotangent,
    w_qkv,
    w_attn,
    w_in,
    w_out,
    ln_gain,
    ln_bias,
    rel_emb,
    rel_gain,
    rel_bias,
    doc_ids,
    rel_bucket,
):
    _, rows, model = tokens.shape
    layers, _, own, width = w_qkv.shape
    hidden_units = w_in.shape[2]
    heads = width // HEAD_DIM
    ctx_count = lax.axis_size(CTX)
    owners = lax.axis_size(OWNERS)
    length = rows * ctx_count
    row_start = lax.axis_index(CTX) * rows
    scale = 1.0 / math.sqrt(3.0 * HEAD_DIM)
    win = length + rows
    rel_own = rel_emb.shape[0]
    buckets = rel_own * owners
    wide = 3 * width

    dims = (
        lax.axis_size("core"),
        lax.axis_size(ZED),
        lax.axis_size("x"),
        lax.axis_size("zl"),
        own,
    )
    whence = jnp.stack([lax.axis_index("core"), lax.axis_index(ZED), lax.axis_index("x")])
    whence = whence.astype(jnp.int32)
    place = jnp.stack(
        [lax.axis_index(("zh", "core")), lax.axis_index(CTX), lax.axis_index("core")]
    ).astype(jnp.int32)

    start_cols = wide + model // 2 + LANES
    (start_pack,) = call(
        pack_start_kernel,
        [((own, start_cols), BF16)],
        [w_qkv, rel_emb, ln_gain, ln_bias, rel_gain[None], rel_bias[None], doc_ids],
        scratch=[pltpu.VMEM((LANES, LANES), F32)],
        limit=8,
        name="pack_start",
    )
    rest_packs = []
    for layer in range(layers):
        cols = width + 2 * hidden_units + (wide if layer else 0)
        rest_packs.extend(
            call(
                functools.partial(pack_rest_kernel, layer, layer > 0),
                [((own, cols), BF16)],
                [w_qkv, w_attn, w_in, w_out],
                limit=16,
                name="pack_rest",
            )
        )
    start_pieces = gather_pieces(start_pack)
    rest_pieces = [gather_pieces(pack) for pack in rest_packs]

    padded = jnp.pad(rel_bucket, (1, 1), mode="edge")
    to_index = lax.dynamic_slice_in_dim(padded, row_start, win, 0)
    from_index = lax.dynamic_slice_in_dim(padded, length - rows - row_start + 1, win, 0)
    index = jnp.stack([to_index[::-1], from_index[::-1], from_index])
    (tables,) = call(
        table_kernel, [((3, buckets, win), BF16)], [index], limit=16, name="tables"
    )

    copies = 4 * owners
    qkv, rel_raw, small, q, key_value = call(
        functools.partial(start_kernel, dims, scale),
        [
            ((model, wide), BF16),
            ((buckets, model), BF16),
            ((model, LANES), BF16),
            ((rows, width), BF16),
            ((rows, 2 * width), BF16),
        ],
        [whence, *start_pieces, tokens[0]],
        smem=(0,),
        anys=range(1, 1 + len(start_pieces)),
        scratch=[pltpu.SemaphoreType.DMA((copies,))],
        limit=24,
        name="start",
    )
    rel_low, vecs, doc_j = call(
        functools.partial(relative_kernel, layers, owners),
        [((buckets, model), BF16), ((16, model), F32), ((1, length), F32)],
        [place, rel_raw, small],
        smem=(0,),
        limit=24,
        name="relative",
    )
    qkvs, rests = [qkv], []
    for layer in range(layers):
        shapes = [((model, c), BF16) for c in (width, hidden_units, hidden_units)]
        if layer:
            shapes = [((model, wide), BF16)] + shapes
        outs = call(
            functools.partial(rest_kernel, dims, len(shapes)),
            shapes,
            [whence, *rest_pieces[layer]],
            smem=(0,),
            anys=range(1, 1 + len(rest_pieces[layer])),
            scratch=[pltpu.SemaphoreType.DMA((len(shapes) * owners,))],
            limit=24,
            name="rest",
        )
        if layer:
            qkvs.append(outs[0])
        rests.append(outs[-3:])

    token_low = tokens[0]
    stream = token_low
    kept = []
    hidden, pieces = None, None
    tile = (rows, model)
    for layer in range(layers):
        qkv = qkvs[layer]
        attn_t, in_full, out_t = rests[layer]
        if layer:
            pre_out, stream, stream_low, q, key_value = call(
                functools.partial(
                    project_kernel, scale, (2 * layer - 1, 2 * layers + 2 * layer - 1)
                ),
                [
                    (tile, F32),
                    (tile, F32),
                    (tile, BF16),
                    ((rows, width), BF16),
                    ((rows, 2 * width), BF16),
                ],
                [hidden, *pieces, vecs, qkv],
                name="project",
            )
            kept[-1]["pre_out"] = pre_out
        else:
            stream_low = token_low
        blocks = [key_value] + [shifted(key_value, CTX, s) for s in range(1, ctx_count)]
        pk, pq_rev, pq = call(
            functools.partial(position_kernel, scale),
            [((width, win), BF16)] * 3,
            [rel_low, qkv, tables],
            name="position",
        )
        part, mixture, p, kv = call(
            attention_kernel,
            [
                (tile, BF16),
                ((rows, width), BF16),
                ((heads, rows, length), BF16),
                ((length, 2 * width), BF16),
            ],
            [place, q, *blocks, pk, pq_rev, doc_ids, doc_j, attn_t],
            smem=(0,),
            anys=range(2, 2 + ctx_count),
            scratch=[
                pltpu.VMEM((heads, rows, length), F32),
                pltpu.VMEM((heads, rows, width), BF16),
                pltpu.SemaphoreType.DMA((ctx_count,)),
            ],
            name="attention",
        )
        pre_hidden, hidden, hidden_low, slope, active, part = call(
            functools.partial(feed_kernel, (2 * layer, 2 * layers + 2 * layer)),
            [
                (tile, F32),
                (tile, F32),
                (tile, BF16),
                ((rows, hidden_units), F32),
                ((rows, hidden_units), BF16),
                (tile, BF16),
            ],
            [stream, *tp_pieces(part), vecs, in_full, out_t],
            name="feed",
        )
        pieces = tp_pieces(part)
        kept.append(
            dict(
                stream_low=stream_low,
                q=q,
                kv=kv,
                pk=pk,
                pq=pq,
                p=p,
                mixture=mixture,
                pre_hidden=pre_hidden,
                hidden_low=hidden_low,
                slope=slope,
                active=active,
            )
        )
    last = layers - 1
    pre_out, out_local = call(
        functools.partial(end_kernel, (2 * last + 1, 2 * layers + 2 * last + 1)),
        [(tile, F32), (tile, BF16)],
        [hidden, *pieces, vecs],
        name="end",
    )
    kept[-1]["pre_out"] = pre_out

    grad_parts = [cotangent[0]]
    early_blocks, late_blocks, pos_blocks = [None] * layers, [None] * layers, [None] * layers
    for layer in reversed(range(layers)):
        k = kept[layer]
        qkv = qkvs[layer]
        attn_t, in_full, out_t = rests[layer]
        d_pre_out, d_out_low, d_inner, part, norm_out = call(
            functools.partial(feed_back_kernel, 2 * layer + 1, len(grad_parts) > 1),
            [
                (tile, F32),
                (tile, BF16),
                ((rows, hidden_units), BF16),
                (tile, BF16),
                ((8, model), F32),
            ],
            [*grad_parts, k["pre_out"], vecs, k["slope"], in_full, out_t],
            name="feed_back",
        )
        backs = call(
            functools.partial(attention_back_kernel, 2 * layer, scale),
            [
                (tile, F32),
                (tile, BF16),
                ((rows, width), BF16),
                ((win, width), BF16),
                ((win, width), BF16),
                ((8, model), F32),
            ]
            + [((rows, 2 * width), BF16)] * ctx_count,
            [place, *tp_pieces(part), d_pre_out, k["pre_hidden"], vecs, attn_t]
            + [k["q"], k["kv"], k["pk"], k["pq"], k["p"]],
            smem=(0,),
            scratch=[
                pltpu.VMEM((heads * rows, length), BF16),
                pltpu.VMEM((heads * rows, win), BF16),
                pltpu.VMEM((length, width), F32),
                pltpu.VMEM((heads * rows, width), BF16),
                pltpu.VMEM((heads * rows, width), BF16),
                pltpu.VMEM((heads * rows, width), BF16),
                pltpu.VMEM((win, width), F32),
                pltpu.VMEM((length, 2 * width), BF16),
            ],
            name="attention_back",
        )
        d_pre_hidden, d_attended, dq, dpk, dpq, norm_hidden = backs[:6]
        dkv = [backs[6]] + [shifted(backs[6 + s], CTX, s) for s in range(1, ctx_count)]

        early_in = [place, d_attended, k["mixture"], k["hidden_low"], d_inner]
        early_in += [d_out_low, k["active"], norm_hidden, norm_out]
        early_cols = width + 2 * hidden_units + LANES
        early = [((model // 2, early_cols), BF16)]
        early_scratch = [pltpu.VMEM((LANES, model // 2), F32)]
        (other,) = call(
            functools.partial(early_kernel, False),
            early,
            early_in,
            smem=(0,),
            scratch=early_scratch,
            name="early_other",
        )
        (mine,) = call(
            functools.partial(early_kernel, True),
            early,
            [*early_in, shifted(other, "core", 1)],
            smem=(0,),
            scratch=early_scratch,
            name="early_own",
        )
        early_blocks[layer] = plane_blocks(mine)

        pos_low, pos_rows = call(
            position_back_kernel,
            [((buckets, 2 * width), BF16), ((owners, 2 * rel_own, width), BF16)],
            [tables, dpk, dpq],
            name="position_back",
        )
        pos_blocks[layer] = lax.all_to_all(pos_rows, OWNERS, 0, 0)

        dqkv, part = call(
            stream_back_kernel,
            [((rows, wide), BF16), (tile, BF16)],
            [dq, *dkv, qkv],
            name="stream_back",
        )
        grad_parts = [d_pre_hidden] + tp_pieces(part)
        late_in = [place, k["stream_low"], dqkv, rel_low, pos_low]
        late = [((model // 2, wide), BF16)]
        (other,) = call(
            functools.partial(late_kernel, False), late, late_in, smem=(0,), name="late_other"
        )
        (mine,) = call(
            functools.partial(late_kernel, True),
            late,
            [*late_in, shifted(other, "core", 1)],
            smem=(0,),
            name="late_own",
        )
        late_blocks[layer] = plane_blocks(mine)

    total = (grad_parts[1].astype(F32) + grad_parts[3].astype(F32)) + (
        grad_parts[2].astype(F32) + grad_parts[4].astype(F32)
    )
    grad_tokens = (grad_parts[0] + total).astype(BF16)

    grad_attn, grad_in, grad_out, grad_gain, grad_bias = call(
        early_end_kernel,
        [
            ((layers, width, own), F32),
            ((layers, own, hidden_units), F32),
            ((layers, hidden_units, own), F32),
            ((layers, 2, own), F32),
            ((layers, 2, own), F32),
        ],
        early_blocks,
        name="early_end",
    )
    (grad_qkv,) = call(
        late_end_kernel, [((layers, 3, own, width), F32)], late_blocks, name="late_end"
    )

    term_in = []
    for layer in range(layers):
        term_in += [pos_blocks[layer], qkvs[layer]]
    (term,) = call(relative_term_kernel, [((rel_own, model), F32)], term_in, name="relative_term")
    grad_rel, ends = call(
        functools.partial(relative_end_kernel, 4 * layers),
        [((rel_own, model), F32), ((owners, 2, own), F32)],
        [*tp_pieces(term), rel_emb, vecs],
        name="relative_end",
    )
    ends = jnp.sum(lax.all_to_all(ends, OWNERS, 0, 0), axis=0)
    return (
        out_local[None],
        grad_tokens[None],
        grad_qkv,
        grad_attn,
        grad_in,
        grad_out,
        grad_gain,
        grad_bias,
        grad_rel,
        ends[0],
        ends[1],
    )


def solution(mesh):
    sizes = mesh.shape
    zh, zl = 2, 2
    finer = Mesh(
        mesh.devices.reshape(zh, sizes["fsdp"] // zh, sizes["ctx"] // zl, zl, sizes["tp"]),
        ("zh", "core", "x", "zl", "tp"),
    )
    own = OWNERS
    fsdp = ("zh", "core")
    return jax.shard_map(
        local,
        mesh=finer,
        in_specs=(
            P(fsdp, CTX, None),
            P(fsdp, CTX, None),
            P(None, None, own, "tp"),
            P(None, "tp", own),
            P(None, own, "tp"),
            P(None, "tp", own),
            P(None, None, own),
            P(None, None, own),
            P(own, None),
            P(own),
            P(own),
            P(fsdp, CTX),
            P(),
        ),
        out_specs=(
            P(fsdp, CTX, None),
            P(fsdp, CTX, None),
            P(None, None, own, "tp"),
            P(None, "tp", own),
            P(None, own, "tp"),
            P(None, "tp", own),
            P(None, None, own),
            P(None, None, own),
            P(own, None),
            P(own),
            P(own),
        ),
        check_vma=False,
    )
```

time: 952 us -> 556 us (0.58)
  Pallas kernels: 465 us -> 91.1 us
  matrix products: 79.5 us -> 0 us
  waiting for transfers between devices: 164 us -> 229 us
  other arithmetic: 63.4 us -> 5.44 us
  local copies, waits for them, and re-layouts: 43.3 us -> 72.7 us
  starting transfers between devices: 125 us -> 144 us
    pallas_call x7 -> x36, Pallas kernels: 465 us -> 91.1 us  [call(): pl.pallas_call(body, in_specs=specs, out_specs=tuple((pl.BlockSpec(memory...]
    dot_general x54 -> x0, matrix products: 79.5 us -> none  [dot(): lax.dot_general(a, b, (((ca,), (cb,)), ((), ())), preferred_element_type=...]
    ppermute x75 -> x89, waiting for transfers between devices: 90.8 us -> 168 us  [shifted(): lax.ppermute(values, axes, [(i, (i + shift) % count) for i in range(count)])]
    unnamed x274 -> x346, local copies, waits for them, and re-layouts: 12.5 us -> 70 us
    convert_element_type x15 -> x0, other arithmetic: 21.6 us -> none  [the longest x4 12.8 us: scatter_rows(): total = (make(core) + arrived.astype(F32)).astype(BF16)]
    reduce_sum x27 -> x1, other arithmetic: 21.1 us -> 0.8 us  [local(): ends = jnp.sum(lax.all_to_all(ends, OWNERS, 0, 0), axis=0)]
    ppermute x75 -> x89, starting transfers between devices: 92.9 us -> 110 us  [shifted(): lax.ppermute(values, axes, [(i, (i + shift) % count) for i in range(count)])]
    all_to_all x7, waiting for transfers between devices: 72.9 us -> 61.1 us  [the longest x4 56.4 us: plane_blocks(): return lax.all_to_all(blocks, PLANE, 0, 0)]
  transfers between devices with their start and end apart: 82 -> 96, of which waited for: 33 -> 43; matrix products, arithmetic and copies ran while one was open for 16% -> 2% of each run, Pallas kernels for 47% -> 12%
where the time goes in v2:
time: 556 us; the launch traced here: 545 us
  waiting for transfers between devices  229 us (41%)
  starting transfers between devices  144 us (26%)
  Pallas kernels  91.1 us (16%)
  local copies, waits for them, and re-layouts  72.7 us (13%)
    ppermute x89, waiting for transfers between devices, shifted(): lax.ppermute(values, axes, [(i, (i + shift) % count) for i in range(count)])  168 us
    ppermute x89, starting transfers between devices, shifted(): lax.ppermute(values, axes, [(i, (i + shift) % count) for i in range(count)])  110 us
    pallas_call x36, Pallas kernels, call(): pl.pallas_call(body, in_specs=specs, out_specs=tuple((pl.BlockSpec(memory...  91.1 us
    unnamed x346, local copies, waits for them, and re-layouts  70 us
    all_to_all x4, waiting for transfers between devices, plane_blocks(): return lax.all_to_all(blocks, PLANE, 0, 0)  56.4 us
    all_to_all x4, starting transfers between devices, plane_blocks(): return lax.all_to_all(blocks, PLANE, 0, 0)  15.5 us
    all_to_all x2, starting transfers between devices, local(): pos_blocks[layer] = lax.all_to_all(pos_rows, OWNERS, 0, 0)  12.2 us
  transfers between devices with their start and end apart: 96, of which 43 were waited for; matrix products, arithmetic and copies ran while one was open for 2% of the time, Pallas kernels for 12%

profile of v2, /device:TPU:0, one launch (start us, length us, event | category | flops | bytes accessed | tf_op | source)
XLA Modules:
  0.0 545.0 jit_solution(11684393621816519690)
XLA Ops:
  16.1 4.1 collective-permute-start.5
  39.3 8.9 %collective-permute-done.3.refs_1_ = bf16[128,1408]{1,0:T(8,128)(2,1)S(1)} collective-permute-done((bf16[128,1408]{1,0:T(8,128)(2,1)S(1)}, bf16[128,1408]{1,0:T(8,128)(2,1)S(1)}, u32[]{:S(2)}, u32[]{:S(2)}) %collective-permute-start.3) | collective-permute-done | bytes 360480 | tf_op jit(solution)/shard_map/ppermute | solution.py:543
  62.6 4.9 start.1
  72.1 9.5 %collective-permute-done.20.refs_1_ = bf16[128,2304]{1,0:T(8,128)(2,1)} collective-permute-done((bf16[128,2304]{1,0:T(8,128)(2,1)S(1)}, bf16[128,2304]{1,0:T(8,128)(2,1)}, u32[]{:S(2)}, u32[]{:S(2)}) %collective-permute-start.20) | collective-permute-done | bytes 589856 | tf_op jit(solution)/shard_map/ppermute | solution.py:543
  96.7 7.0 %collective-permute-done.12.refs_3_ = bf16[128,512]{1,0:T(8,128)(2,1)S(1)} collective-permute-done((bf16[128,512]{1,0:T(8,128)(2,1)}, bf16[128,512]{1,0:T(8,128)(2,1)S(1)}, u32[]{:S(2)}, u32[]{:S(2)}) %collective-permute-start.12) | collective-permute-done | bytes 131104 | tf_op jit(solution)/shard_map/ppermute | solution.py:543
  124.3 17.8 %collective-permute-done.10.refs_1_ = bf16[128,512]{1,0:T(8,128)(2,1)} collective-permute-done((bf16[128,512]{1,0:T(8,128)(2,1)}, bf16[128,512]{1,0:T(8,128)(2,1)}, u32[]{:S(2)}, u32[]{:S(2)}) %collective-permute-start.10) | collective-permute-done | bytes 131104 | tf_op jit(solution)/shard_map/ppermute | solution.py:543
  142.2 7.2 %attention.2 = (bf16[128,1024]{1,0:T(8,128)(2,1)S(1)}, bf16[128,256]{1,0:T(8,128)(2,1)S(1)}, bf16[4,128,1024]{2,1,0:T(8,128)(2,1)S(1)}, bf16[1024,512]{1,0:T(8,128)(2,1)S(1)}) custom-call(s32[3]{0:T(128)S(1)} %pad_add_fusion.1.place_ref, bf16[128,256]{1,0:T(8,128)(2,1)S(1)} %copy-done.115, bf16[128,512]{1,0:T(8,128)(2,1)} %get-tuple-element.113.refs_0_, ...), custom_call_target="tpu_custom_call" | custom-call | tf_op jit(solution)/shard_map/attention/pallas_call | solution.py:34
  155.4 8.2 %collective-permute-done.29.refs_3_ = bf16[128,1024]{1,0:T(8,128)(2,1)S(1)} collective-permute-done((bf16[128,1024]{1,0:T(8,128)(2,1)S(1)}, bf16[128,1024]{1,0:T(8,128)(2,1)S(1)}, u32[]{:S(2)}, u32[]{:S(2)}) %collective-permute-start.29) | collective-permute-done | bytes 262176 | tf_op jit(solution)/shard_map/ppermute | solution.py:543
  165.6 8.6 %collective-permute-done.27.refs_1_ = bf16[128,1024]{1,0:T(8,128)(2,1)S(1)} collective-permute-done((bf16[128,1024]{1,0:T(8,128)(2,1)S(1)}, bf16[128,1024]{1,0:T(8,128)(2,1)S(1)}, u32[]{:S(2)}, u32[]{:S(2)}) %collective-permute-start.27) | collective-permute-done | bytes 262176 | tf_op jit(solution)/shard_map/ppermute | solution.py:543
  183.1 6.3 %collective-permute-done.32.refs_3_ = bf16[128,1024]{1,0:T(8,128)(2,1)S(1)} collective-permute-done((bf16[128,1024]{1,0:T(8,128)(2,1)S(1)}, bf16[128,1024]{1,0:T(8,128)(2,1)S(1)}, u32[]{:S(2)}, u32[]{:S(2)}) %collective-permute-start.32) | collective-permute-done | bytes 262176 | tf_op jit(solution)/shard_map/ppermute | solution.py:543
  205.5 6.3 %collective-permute-start.43 = (bf16[128,512]{1,0:T(8,128)(2,1)S(1)}, bf16[128,512]{1,0:T(8,128)(2,1)S(1)}, u32[]{:S(2)}, u32[]{:S(2)}) collective-permute-start(bf16[128,512]{1,0:T(8,128)(2,1)S(1)} %get-tuple-element.131.refs_0_), channel_id=1, source_target_pairs={{0,4},{4,8},{8,12},{12,16},{16,20},{20,24},{24,28},{28,0},{1,5},{5... | collective-permute-start | bytes 393224 | tf_op jit(solution)/shard_map/ppermute | solution.py:543
  216.0 7.8 %attention.3 = (bf16[128,1024]{1,0:T(8,128)(2,1)S(1)}, bf16[128,256]{1,0:T(8,128)(2,1)S(1)}, bf16[4,128,1024]{2,1,0:T(8,128)(2,1)S(1)}, bf16[1024,512]{1,0:T(8,128)(2,1)S(1)}) custom-call(s32[3]{0:T(128)S(1)} %pad_add_fusion.1.place_ref, bf16[128,256]{1,0:T(8,128)(2,1)S(1)} %get-tuple-element.130.q_ref.refs_8_, ...), custom_call_target="tpu_custom_call" | custom-call | tf_op jit(solution)/shard_map/attention/pallas_call | solution.py:34
  226.0 7.1 %collective-permute-done.52.refs_3_ = bf16[128,1024]{1,0:T(8,128)(2,1)S(1)} collective-permute-done((bf16[128,1024]{1,0:T(8,128)(2,1)S(1)}, bf16[128,1024]{1,0:T(8,128)(2,1)S(1)}, u32[]{:S(2)}, u32[]{:S(2)}) %collective-permute-start.52) | collective-permute-done | bytes 262176 | tf_op jit(solution)/shard_map/ppermute | solution.py:543
  242.8 6.8 %collective-permute-done.55.refs_3_ = bf16[128,1024]{1,0:T(8,128)(2,1)S(1)} collective-permute-done((bf16[128,1024]{1,0:T(8,128)(2,1)S(1)}, bf16[128,1024]{1,0:T(8,128)(2,1)S(1)}, u32[]{:S(2)}, u32[]{:S(2)}) %collective-permute-start.55) | collective-permute-done | bytes 262176 | tf_op jit(solution)/shard_map/ppermute | solution.py:543
  262.7 6.4 %collective-permute-done.58.refs_3_ = bf16[128,1024]{1,0:T(8,128)(2,1)S(1)} collective-permute-done((bf16[128,1024]{1,0:T(8,128)(2,1)S(1)}, bf16[128,1024]{1,0:T(8,128)(2,1)S(1)}, u32[]{:S(2)}, u32[]{:S(2)}) %collective-permute-start.58) | collective-permute-done | bytes 262176 | tf_op jit(solution)/shard_map/ppermute | solution.py:543
  275.2 8.9 %attention_back.2 = (f32[128,1024]{1,0:T(8,128)S(1)}, bf16[128,1024]{1,0:T(8,128)(2,1)S(1)}, bf16[128,256]{1,0:T(8,128)(2,1)S(1)}, bf16[1152,256]{1,0:T(8,128)(2...) custom-call(s32[3]{0:T(128)S(1)} %pad_add_fusion.1.place_ref, ...), custom_call_target="tpu_custom_call" | custom-call | tf_op jit(solution)/shard_map/attention_back/pallas_call | solution.py:34
  285.1 5.5 %collective-permute-start.62 = (bf16[128,512]{1,0:T(8,128)(2,1)S(1)}, bf16[128,512]{1,0:T(8,128)(2,1)S(1)}, u32[]{:S(2)}, u32[]{:S(2)}) collective-permute-start(bf16[128,512]{1,0:T(8,128)(2,1)S(1)} %get-tuple-element.155), channel_id=1, source_target_pairs={{0,16},{4,20},{8,24},{12,28},{16,0},{20,4},{24,8},{28,12},{1,17},{... | collective-permute-start | bytes 393224 | tf_op jit(solution)/shard_map/ppermute | solution.py:543
  293.7 6.0 %collective-permute-start.65 = (bf16[128,512]{1,0:T(8,128)(2,1)S(1)}, bf16[128,512]{1,0:T(8,128)(2,1)S(1)}, u32[]{:S(2)}, u32[]{:S(2)}) collective-permute-start(bf16[128,512]{1,0:T(8,128)(2,1)S(1)} %get-tuple-element.158), channel_id=1, source_target_pairs={{0,28},{4,0},{8,4},{12,8},{16,12},{20,16},{24,20},{28,24},{1,29},{... | collective-permute-start | bytes 393224 | tf_op jit(solution)/shard_map/ppermute | solution.py:543
  310.6 4.9 all-to-all-start.5
  338.6 6.5 %collective-permute-done.71.refs_3_ = bf16[128,1024]{1,0:T(8,128)(2,1)S(1)} collective-permute-done((bf16[128,1024]{1,0:T(8,128)(2,1)S(1)}, bf16[128,1024]{1,0:T(8,128)(2,1)S(1)}, u32[]{:S(2)}, u32[]{:S(2)}) %collective-permute-start.71) | collective-permute-done | bytes 262176 | tf_op jit(solution)/shard_map/ppermute | solution.py:543
  348.9 9.0 %attention_back.3 = (f32[128,1024]{1,0:T(8,128)S(1)}, bf16[128,1024]{1,0:T(8,128)(2,1)S(1)}, bf16[128,256]{1,0:T(8,128)(2,1)S(1)}, bf16[1152,256]{1,0:T(8,128)(2...) custom-call(s32[3]{0:T(128)S(1)} %pad_add_fusion.1.place_ref, ...), custom_call_target="tpu_custom_call" | custom-call | tf_op jit(solution)/shard_map/attention_back/pallas_call | solution.py:34
  368.3 7.3 %all-to-all-start.4 = ((bf16[32,32,256]{2,1,0:T(8,128)(2,1)}), bf16[32,32,256]{2,1,0:T(8,128)(2,1)S(1)}, u32[]{:S(2)}, u32[]{:S(2)}) async-start(bf16[32,32,256]{2,1,0:T(8,128)(2,1)} %copy-done.90), calls=%async_computation.4 | async-start | bytes 1048576 | tf_op jit(solution)/shard_map/all_to_all | solution.py:847
  381.0 8.3 %collective-permute-done.72.refs_1_ = bf16[128,512]{1,0:T(8,128)(2,1)S(1)} collective-permute-done((bf16[128,512]{1,0:T(8,128)(2,1)}, bf16[128,512]{1,0:T(8,128)(2,1)S(1)}, u32[]{:S(2)}, u32[]{:S(2)}) %collective-permute-start.72) | collective-permute-done | bytes 131104 | tf_op jit(solution)/shard_map/ppermute | solution.py:543
  393.7 4.3 collective-permute-done.74.refs_3_
  413.5 6.2 %all-to-all-start.6 = ((f32[32,2,32]{2,1,0:T(2,128)}), f32[32,2,32]{2,1,0:T(2,128)S(1)}, u32[]{:S(2)}, u32[]{:S(2)}) async-start(f32[32,2,32]{2,1,0:T(2,128)} %get-tuple-element.212), calls=%async_computation.6 | async-start | bytes 65536 | tf_op jit(solution)/shard_map/all_to_all | solution.py:901
  422.4 4.7 all-to-all-done.6
  433.5 12.6 %all-to-all-done.1.refs_1_ = bf16[16,32,768]{2,1,0:T(8,128)(2,1)S(1)} async-done(((bf16[16,32,768]{2,1,0:T(8,128)(2,1)}), bf16[16,32,768]{2,1,0:T(8,128)(2,1)S(1)}, u32[]{:S(2)}, u32[]{:S(2)}) %all-to-all-start.1) | async-done | bytes 786464 | tf_op jit(solution)/shard_map/all_to_all | solution.py:561
  456.8 6.8 %all-to-all-done.refs_0_ = bf16[16,32,768]{2,1,0:T(8,128)(2,1)S(1)} async-done(((bf16[16,32,768]{2,1,0:T(8,128)(2,1)}), bf16[16,32,768]{2,1,0:T(8,128)(2,1)S(1)}, u32[]{:S(2)}, u32[]{:S(2)}) %all-to-all-start) | async-done | bytes 786464 | tf_op jit(solution)/shard_map/all_to_all | solution.py:561
  478.3 23.6 %all-to-all-done.3.refs_1_ = bf16[16,32,2432]{2,1,0:T(8,128)(2,1)S(1)} async-done(((bf16[16,32,2432]{2,1,0:T(8,128)(2,1)}), bf16[16,32,2432]{2,1,0:T(8,128)(2,1)S(1)}, u32[]{:S(2)}, u32[]{:S(2)}) %all-to-all-start.3) | async-done | bytes 2490400 | tf_op jit(solution)/shard_map/all_to_all | solution.py:561
  501.9 4.6 all-to-all-start.2
  514.4 5.0 collective-permute-done.80
  524.8 13.5 %all-to-all-done.2.refs_0_ = bf16[16,32,2432]{2,1,0:T(8,128)(2,1)} async-done(((bf16[16,32,2432]{2,1,0:T(8,128)(2,1)}), bf16[16,32,2432]{2,1,0:T(8,128)(2,1)}, u32[]{:S(2)}, u32[]{:S(2)}) %all-to-all-start.2) | async-done | bytes 2490400 | tf_op jit(solution)/shard_map/all_to_all | solution.py:561
  (559 shorter events, 287.7 us)
Async XLA Ops:
  16.1 21.3 %collective-permute-start.5 = (bf16[128,1408]{1,0:T(8,128)(2,1)S(1)}, bf16[128,1408]{1,0:T(8,128)(2,1)S(1)}, u32[]{:S(2)}, u32[]{:S(2)}) collective-permute-start(bf16[128,1408]{1,0:T(8,128)(2,1)S(1)} %pad_maximum_fusion.2.refs_0_), channel_id=1, source_target_pairs={{0,68},{4,0},{64,4},{68,64},{1,69},{5,1},{65,5},{69,65},{2,70},{6,... | collective-permute-start | bytes 1081352 | tf_op jit(solution)/shard_map/ppermute | solution.py:543
  20.3 17.4 %collective-permute-start.4 = (bf16[128,1408]{1,0:T(8,128)(2,1)S(1)}, bf16[128,1408]{1,0:T(8,128)(2,1)S(1)}, u32[]{:S(2)}, u32[]{:S(2)}) collective-permute-start(bf16[128,1408]{1,0:T(8,128)(2,1)S(1)} %pad_maximum_fusion.2.refs_0_), channel_id=1, source_target_pairs={{0,64},{4,68},{64,0},{68,4},{1,65},{5,69},{65,1},{69,5},{2,66},{6,... | collective-permute-start | bytes 1081352 | tf_op jit(solution)/shard_map/ppermute | solution.py:543
  39.3 32.2 %collective-permute-start.23 = (bf16[128,2304]{1,0:T(8,128)(2,1)S(1)}, bf16[128,2304]{1,0:T(8,128)(2,1)S(1)}, u32[]{:S(2)}, u32[]{:S(2)}) collective-permute-start(bf16[128,2304]{1,0:T(8,128)(2,1)S(1)} %pad_maximum_fusion.1.refs_0_), channel_id=1, source_target_pairs={{0,32},{32,0},{1,33},{33,1},{2,34},{34,2},{3,35},{35,3},{4,36},{36... | collective-permute-start | bytes 1769480 | tf_op jit(solution)/shard_map/ppermute | solution.py:543
  49.8 21.7 %collective-permute-start.22 = (bf16[128,2304]{1,0:T(8,128)(2,1)S(1)}, bf16[128,2304]{1,0:T(8,128)(2,1)S(1)}, u32[]{:S(2)}, u32[]{:S(2)}) collective-permute-start(bf16[128,2304]{1,0:T(8,128)(2,1)S(1)} %pad_maximum_fusion.1.refs_0_), channel_id=1, source_target_pairs={{0,68},{4,0},{64,4},{68,64},{1,69},{5,1},{65,5},{69,65},{2,70},{6,... | collective-permute-start | bytes 1769480 | tf_op jit(solution)/shard_map/ppermute | solution.py:543
  51.6 20.0 %collective-permute-start.21 = (bf16[128,2304]{1,0:T(8,128)(2,1)S(1)}, bf16[128,2304]{1,0:T(8,128)(2,1)}, u32[]{:S(2)}, u32[]{:S(2)}) collective-permute-start(bf16[128,2304]{1,0:T(8,128)(2,1)S(1)} %pad_maximum_fusion.1.refs_0_), channel_id=1, source_target_pairs={{0,64},{4,68},{64,0},{68,4},{1,65},{5,69},{65,1},{69,5},{2,66},{6,... | collective-permute-start | bytes 1769480 | tf_op jit(solution)/shard_map/ppermute | solution.py:543
  53.5 28.0 %collective-permute-start.20 = (bf16[128,2304]{1,0:T(8,128)(2,1)S(1)}, bf16[128,2304]{1,0:T(8,128)(2,1)}, u32[]{:S(2)}, u32[]{:S(2)}) collective-permute-start(bf16[128,2304]{1,0:T(8,128)(2,1)S(1)} %pad_maximum_fusion.1.refs_0_), channel_id=1, source_target_pairs={{0,4},{4,64},{64,68},{68,0},{1,5},{5,65},{65,69},{69,1},{2,6},{6,6... | collective-permute-start | bytes 1769480 | tf_op jit(solution)/shard_map/ppermute | solution.py:543
  71.5 34.9 %collective-permute-start.26 = (bf16[128,2304]{1,0:T(8,128)(2,1)S(1)}, bf16[128,2304]{1,0:T(8,128)(2,1)S(1)}, u32[]{:S(2)}, u32[]{:S(2)}) collective-permute-start(bf16[128,2304]{1,0:T(8,128)(2,1)S(1)} %collective-permute-done.22.refs_3_), channel_id=1, source_target_pairs={{0,32},{32,0},{1,33},{33,1},{2,34},{34,2},{3,35},{35,3},{4,36},{36... | collective-permute-start | bytes 1769480 | tf_op jit(solution)/shard_map/ppermute | solution.py:543
  71.6 37.9 %collective-permute-start.25 = (bf16[128,2304]{1,0:T(8,128)(2,1)}, bf16[128,2304]{1,0:T(8,128)(2,1)}, u32[]{:S(2)}, u32[]{:S(2)}) collective-permute-start(bf16[128,2304]{1,0:T(8,128)(2,1)} %collective-permute-done.21.refs_2_), channel_id=1, source_target_pairs={{0,32},{32,0},{1,33},{33,1},{2,34},{34,2},{3,35},{35,3},{4,36},{36... | collective-permute-start | bytes 1769480 | tf_op jit(solution)/shard_map/ppermute | solution.py:543
  81.5 29.8 %collective-permute-start.24 = (bf16[128,2304]{1,0:T(8,128)(2,1)}, bf16[128,2304]{1,0:T(8,128)(2,1)S(1)}, u32[]{:S(2)}, u32[]{:S(2)}) collective-permute-start(bf16[128,2304]{1,0:T(8,128)(2,1)} %collective-permute-done.20.refs_1_), channel_id=1, source_target_pairs={{0,32},{32,0},{1,33},{33,1},{2,34},{34,2},{3,35},{35,3},{4,36},{36... | collective-permute-start | bytes 1769480 | tf_op jit(solution)/shard_map/ppermute | solution.py:543
  91.3 62.8 %collective-permute-start.38 = (bf16[128,3072]{1,0:T(8,128)(2,1)}, bf16[128,3072]{1,0:T(8,128)(2,1)}, u32[]{:S(2)}, u32[]{:S(2)}) collective-permute-start(bf16[128,3072]{1,0:T(8,128)(2,1)} %pad_maximum_fusion.refs_0_), channel_id=1, source_target_pairs={{0,68},{4,0},{64,4},{68,64},{1,69},{5,1},{65,5},{69,65},{2,70},{6,... | collective-permute-start | bytes 2359304 | tf_op jit(solution)/shard_map/ppermute | solution.py:543
  104.4 50.2 %collective-permute-start.37 = (bf16[128,3072]{1,0:T(8,128)(2,1)}, bf16[128,3072]{1,0:T(8,128)(2,1)}, u32[]{:S(2)}, u32[]{:S(2)}) collective-permute-start(bf16[128,3072]{1,0:T(8,128)(2,1)} %pad_maximum_fusion.refs_0_), channel_id=1, source_target_pairs={{0,64},{4,68},{64,0},{68,4},{1,65},{5,69},{65,1},{69,5},{2,66},{6,... | collective-permute-start | bytes 2359304 | tf_op jit(solution)/shard_map/ppermute | solution.py:543
  107.2 48.0 %collective-permute-start.36 = (bf16[128,3072]{1,0:T(8,128)(2,1)}, bf16[128,3072]{1,0:T(8,128)(2,1)}, u32[]{:S(2)}, u32[]{:S(2)}) collective-permute-start(bf16[128,3072]{1,0:T(8,128)(2,1)} %pad_maximum_fusion.refs_0_), channel_id=1, source_target_pairs={{0,4},{4,64},{64,68},{68,0},{1,5},{5,65},{65,69},{69,1},{2,6},{6,6... | collective-permute-start | bytes 2359304 | tf_op jit(solution)/shard_map/ppermute | solution.py:543
  112.2 29.9 %collective-permute-start.10 = (bf16[128,512]{1,0:T(8,128)(2,1)}, bf16[128,512]{1,0:T(8,128)(2,1)}, u32[]{:S(2)}, u32[]{:S(2)}) collective-permute-start(bf16[128,512]{1,0:T(8,128)(2,1)} %get-tuple-element.113.refs_0_), channel_id=1, source_target_pairs={{0,4},{4,8},{8,12},{12,16},{16,20},{20,24},{24,28},{28,0},{1,5},{5... | collective-permute-start | bytes 393224 | tf_op jit(solution)/shard_map/ppermute | solution.py:543
  154.0 24.3 %collective-permute-start.39 = (bf16[128,3072]{1,0:T(8,128)(2,1)}, bf16[128,3072]{1,0:T(8,128)(2,1)S(1)}, u32[]{:S(2)}, u32[]{:S(2)}) collective-permute-start(bf16[128,3072]{1,0:T(8,128)(2,1)} %pad_maximum_fusion.refs_0_), channel_id=1, source_target_pairs={{0,32},{32,0},{1,33},{33,1},{2,34},{34,2},{3,35},{35,3},{4,36},{36... | collective-permute-start | bytes 2359304 | tf_op jit(solution)/shard_map/ppermute | solution.py:543
  154.1 24.3 %collective-permute-start.42 = (bf16[128,3072]{1,0:T(8,128)(2,1)}, bf16[128,3072]{1,0:T(8,128)(2,1)S(1)}, u32[]{:S(2)}, u32[]{:S(2)}) collective-permute-start(bf16[128,3072]{1,0:T(8,128)(2,1)} %collective-permute-done.38.refs_3_), channel_id=1, source_target_pairs={{0,32},{32,0},{1,33},{33,1},{2,34},{34,2},{3,35},{35,3},{4,36},{36... | collective-permute-start | bytes 2359304 | tf_op jit(solution)/shard_map/ppermute | solution.py:543
  155.2 24.1 %collective-permute-start.41 = (bf16[128,3072]{1,0:T(8,128)(2,1)}, bf16[128,3072]{1,0:T(8,128)(2,1)S(1)}, u32[]{:S(2)}, u32[]{:S(2)}) collective-permute-start(bf16[128,3072]{1,0:T(8,128)(2,1)} %collective-permute-done.37.refs_2_), channel_id=1, source_target_pairs={{0,32},{32,0},{1,33},{33,1},{2,34},{34,2},{3,35},{35,3},{4,36},{36... | collective-permute-start | bytes 2359304 | tf_op jit(solution)/shard_map/ppermute | solution.py:543
  163.6 15.8 %collective-permute-start.40 = (bf16[128,3072]{1,0:T(8,128)(2,1)}, bf16[128,3072]{1,0:T(8,128)(2,1)S(1)}, u32[]{:S(2)}, u32[]{:S(2)}) collective-permute-start(bf16[128,3072]{1,0:T(8,128)(2,1)} %collective-permute-done.36.refs_1_), channel_id=1, source_target_pairs={{0,32},{32,0},{1,33},{33,1},{2,34},{34,2},{3,35},{35,3},{4,36},{36... | collective-permute-start | bytes 2359304 | tf_op jit(solution)/shard_map/ppermute | solution.py:543
  197.8 15.9 %collective-permute-start.47 = (bf16[128,512]{1,0:T(8,128)(2,1)S(1)}, bf16[128,512]{1,0:T(8,128)(2,1)S(1)}, u32[]{:S(2)}, u32[]{:S(2)}) collective-permute-start(bf16[128,512]{1,0:T(8,128)(2,1)S(1)} %get-tuple-element.131.refs_0_), channel_id=1, source_target_pairs={{0,20},{4,24},{8,28},{12,0},{16,4},{20,8},{24,12},{28,16},{1,21},{... | collective-permute-start | bytes 393224 | tf_op jit(solution)/shard_map/ppermute | solution.py:543
  305.7 20.0 %collective-permute-start.68 = (bf16[128,1024]{1,0:T(8,128)(2,1)}, bf16[128,1024]{1,0:T(8,128)(2,1)}, u32[]{:S(2)}, u32[]{:S(2)}) collective-permute-start(bf16[128,1024]{1,0:T(8,128)(2,1)} %get-tuple-element.159.refs_0_), channel_id=1, source_target_pairs={{0,3},{1,0},{2,1},{3,2},{4,7},{5,4},{6,5},{7,6},{8,11},{9,8},{10,9... | collective-permute-start | bytes 786440 | tf_op jit(solution)/shard_map/ppermute | solution.py:543
  306.3 19.5 %collective-permute-start.67 = (bf16[128,1024]{1,0:T(8,128)(2,1)}, bf16[128,1024]{1,0:T(8,128)(2,1)}, u32[]{:S(2)}, u32[]{:S(2)}) collective-permute-start(bf16[128,1024]{1,0:T(8,128)(2,1)} %get-tuple-element.159.refs_0_), channel_id=1, source_target_pairs={{0,2},{1,3},{2,0},{3,1},{4,6},{5,7},{6,4},{7,5},{8,10},{9,11},{10,... | collective-permute-start | bytes 786440 | tf_op jit(solution)/shard_map/ppermute | solution.py:543
  306.7 19.1 %collective-permute-start.66 = (bf16[128,1024]{1,0:T(8,128)(2,1)}, bf16[128,1024]{1,0:T(8,128)(2,1)}, u32[]{:S(2)}, u32[]{:S(2)}) collective-permute-start(bf16[128,1024]{1,0:T(8,128)(2,1)} %get-tuple-element.159.refs_0_), channel_id=1, source_target_pairs={{0,1},{1,2},{2,3},{3,0},{4,5},{5,6},{6,7},{7,4},{8,9},{9,10},{10,1... | collective-permute-start | bytes 786440 | tf_op jit(solution)/shard_map/ppermute | solution.py:543
  310.6 57.7 %all-to-all-start.5 = ((bf16[32,32,256]{2,1,0:T(8,128)(2,1)}), bf16[32,32,256]{2,1,0:T(8,128)(2,1)}, u32[]{:S(2)}, u32[]{:S(2)}) async-start(bf16[32,32,256]{2,1,0:T(8,128)(2,1)} %copy-done.89), calls=%async_computation.5 | async-start | bytes 1048576 | tf_op jit(solution)/shard_map/all_to_all | solution.py:847
  325.5 127.1 %collective-permute-start.85 = (bf16[512,2432]{1,0:T(8,128)(2,1)}, bf16[512,2432]{1,0:T(8,128)(2,1)}, u32[]{:S(2)}, u32[]{:S(2)}) collective-permute-start(bf16[512,2432]{1,0:T(8,128)(2,1)} %early_other.3), channel_id=1, source_target_pairs={{0,32},{32,0},{1,33},{33,1},{2,34},{34,2},{3,35},{35,3},{4,36},{36... | collective-permute-start | bytes 7471112 | tf_op jit(solution)/shard_map/ppermute | solution.py:543
  338.4 81.2 %collective-permute-start.83 = (bf16[512,768]{1,0:T(8,128)(2,1)}, bf16[512,768]{1,0:T(8,128)(2,1)}, u32[]{:S(2)}, u32[]{:S(2)}) collective-permute-start(bf16[512,768]{1,0:T(8,128)(2,1)} %late_other.3), channel_id=1, source_target_pairs={{0,32},{32,0},{1,33},{33,1},{2,34},{34,2},{3,35},{35,3},{4,36},{36... | collective-permute-start | bytes 2359304 | tf_op jit(solution)/shard_map/ppermute | solution.py:543
  368.3 29.7 %all-to-all-start.4 = ((bf16[32,32,256]{2,1,0:T(8,128)(2,1)}), bf16[32,32,256]{2,1,0:T(8,128)(2,1)S(1)}, u32[]{:S(2)}, u32[]{:S(2)}) async-start(bf16[32,32,256]{2,1,0:T(8,128)(2,1)} %copy-done.90), calls=%async_computation.4 | async-start | bytes 1048576 | tf_op jit(solution)/shard_map/all_to_all | solution.py:847
  379.0 19.1 %collective-permute-start.74 = (bf16[128,512]{1,0:T(8,128)(2,1)}, bf16[128,512]{1,0:T(8,128)(2,1)S(1)}, u32[]{:S(2)}, u32[]{:S(2)}) collective-permute-start(bf16[128,512]{1,0:T(8,128)(2,1)} %copy-done.164), channel_id=1, source_target_pairs={{0,12},{4,16},{8,20},{12,24},{16,28},{20,0},{24,4},{28,8},{1,13},{... | collective-permute-start | bytes 393224 | tf_op jit(solution)/shard_map/ppermute | solution.py:543
  410.9 19.8 %collective-permute-start.82 = (bf16[512,768]{1,0:T(8,128)(2,1)}, bf16[512,768]{1,0:T(8,128)(2,1)}, u32[]{:S(2)}, u32[]{:S(2)}) collective-permute-start(bf16[512,768]{1,0:T(8,128)(2,1)} %late_other.2), channel_id=1, source_target_pairs={{0,32},{32,0},{1,33},{33,1},{2,34},{34,2},{3,35},{35,3},{4,36},{36... | collective-permute-start | bytes 2359304 | tf_op jit(solution)/shard_map/ppermute | solution.py:543
  427.1 19.0 %all-to-all-start.1 = ((bf16[16,32,768]{2,1,0:T(8,128)(2,1)}), bf16[16,32,768]{2,1,0:T(8,128)(2,1)S(1)}, u32[]{:S(2)}, u32[]{:S(2)}) async-start(bf16[16,32,768]{2,1,0:T(8,128)(2,1)} %bitcast.12), calls=%async_computation.1 | async-start | bytes 1572864 | tf_op jit(solution)/shard_map/all_to_all | solution.py:561
  446.1 17.5 %all-to-all-start = ((bf16[16,32,768]{2,1,0:T(8,128)(2,1)}), bf16[16,32,768]{2,1,0:T(8,128)(2,1)S(1)}, u32[]{:S(2)}, u32[]{:S(2)}) async-start(bf16[16,32,768]{2,1,0:T(8,128)(2,1)} %bitcast.11), calls=%async_computation | async-start | bytes 1572864 | tf_op jit(solution)/shard_map/all_to_all | solution.py:561
  452.7 15.5 %collective-permute-start.84 = (bf16[512,2432]{1,0:T(8,128)(2,1)}, bf16[512,2432]{1,0:T(8,128)(2,1)}, u32[]{:S(2)}, u32[]{:S(2)}) collective-permute-start(bf16[512,2432]{1,0:T(8,128)(2,1)} %early_other.2), channel_id=1, source_target_pairs={{0,32},{32,0},{1,33},{33,1},{2,34},{34,2},{3,35},{35,3},{4,36},{36... | collective-permute-start | bytes 7471112 | tf_op jit(solution)/shard_map/ppermute | solution.py:543
  464.4 37.5 %all-to-all-start.3 = ((bf16[16,32,2432]{2,1,0:T(8,128)(2,1)}), bf16[16,32,2432]{2,1,0:T(8,128)(2,1)S(1)}, u32[]{:S(2)}, u32[]{:S(2)}) async-start(bf16[16,32,2432]{2,1,0:T(8,128)(2,1)} %bitcast.21), calls=%async_computation.3 | async-start | bytes 4980736 | tf_op jit(solution)/shard_map/all_to_all | solution.py:561
  501.9 36.3 %all-to-all-start.2 = ((bf16[16,32,2432]{2,1,0:T(8,128)(2,1)}), bf16[16,32,2432]{2,1,0:T(8,128)(2,1)}, u32[]{:S(2)}, u32[]{:S(2)}) async-start(bf16[16,32,2432]{2,1,0:T(8,128)(2,1)} %bitcast.20), calls=%async_computation.2 | async-start | bytes 4980736 | tf_op jit(solution)/shard_map/all_to_all | solution.py:561
  (235 other events, 2479.0 us)

commit v3 on v2

v3 whole, which is shorter than its diff:
```python
import functools
import math

import jax
import jax.numpy as jnp
from jax import lax
from jax.experimental import pallas as pl
from jax.experimental.pallas import tpu as pltpu
from jax.sharding import Mesh
from jax.sharding import PartitionSpec as P

HEAD_DIM = 64
EPS = 1e-07
NEG = -1e30
BLOCK = 128
LANES = 128
F32 = jnp.float32
BF16 = jnp.bfloat16
CTX = ("x", "zl")
ZED = ("zh", "zl")
PLANE = ("zh", "x", "zl")
OWNERS = ("zh", "core", "x", "zl")


def dot(a, b, ca, cb):
    return lax.dot_general(a, b, (((ca,), (cb,)), ((), ())), preferred_element_type=F32)


def call(body, outs, ins, *, anys=(), hbm=(), smem=(), scratch=(), after=(), limit=8, name=None):
    specs = []
    for i in range(len(ins)):
        space = pltpu.VMEM
        if i in anys:
            space = pl.ANY
        if i in hbm:
            space = pltpu.HBM
        if i in smem:
            space = pltpu.SMEM
        specs.append(pl.BlockSpec(memory_space=space))
    count, late = len(ins), len(after)
    specs += [pl.BlockSpec(memory_space=pl.ANY)] * late
    ins = [
        pltpu.with_memory_space_constraint(value, pltpu.HBM) if i in hbm else value
        for i, value in enumerate(ins)
    ]

    def without(*refs):
        body(*refs[:count], *refs[count + late :])

    return pl.pallas_call(
        without,
        in_specs=specs,
        out_specs=tuple(pl.BlockSpec(memory_space=pltpu.VMEM) for _ in outs),
        out_shape=tuple(jax.ShapeDtypeStruct(shape, dtype) for shape, dtype in outs),
        scratch_shapes=list(scratch),
        compiler_params=pltpu.CompilerParams(vmem_limit_bytes=limit << 20),
        name=name,
    )(*ins, *after)


def ctx_shifts(x_count, zl_count):
    pairs = [(dx, dz) for dx in range(x_count) for dz in range(zl_count)]
    return sorted(pairs, key=lambda p: (min(p[0], x_count - p[0]) + p[1], p[1], p[0]))


def ctx_owner(place_ref, shift, sign, x_count, zl_count):
    x = lax.rem(place_ref[1] + (sign * shift[0]) % x_count, x_count)
    zl = lax.rem(place_ref[2] + (sign * shift[1]) % zl_count, zl_count)
    return x * zl_count + zl


def head_mask(shape, head, axis=1):
    index = lax.broadcasted_iota(jnp.int32, shape, axis)
    return (index >= head * HEAD_DIM) & (index < (head + 1) * HEAD_DIM)


def only_head(values, head, axis=1):
    mask = head_mask(values.shape, head, axis)
    return jnp.where(mask, values.astype(F32), 0.0).astype(BF16)


def unit_of(values):
    average = jnp.mean(values, axis=-1, keepdims=True)
    centered = values - average
    spread = jnp.mean(centered * centered, axis=-1, keepdims=True)
    inverse = lax.rsqrt(spread + EPS)
    return centered * inverse, inverse


def normalize_back(values, gain_vec, grad):
    unit, inverse = unit_of(values)
    scaled = grad * gain_vec
    back = (
        scaled
        - jnp.mean(scaled, axis=-1, keepdims=True)
        - unit * jnp.mean(scaled * unit, axis=-1, keepdims=True)
    ) * inverse
    return back, grad * unit


def sum_pieces(pieces):
    parts = [piece[...].astype(F32) for piece in pieces]
    return (parts[0] + parts[2]) + (parts[1] + parts[3])


def run_copies(pairs, sems):
    copies = [
        pltpu.make_async_copy(source, target, sems.at[i])
        for i, (source, target) in enumerate(pairs)
    ]
    for copy in copies:
        copy.start()
    for copy in copies:
        copy.wait()


def pack_start_kernel(qkv_ref, attn_ref, rel_ref, gain_ref, bias_ref, rgain_ref, rbias_ref, doc_ref, *refs):
    out_ref, scr, gain, bias, rgain, rbias, doc, sems = refs
    own, width = qkv_ref.shape[2], qkv_ref.shape[3]
    layers = qkv_ref.shape[0]
    at = 4 * width
    half = rel_ref.shape[1] // 2
    part = rel_ref.shape[0]
    pairs = [(gain_ref, gain), (bias_ref, bias), (rgain_ref, rgain), (rbias_ref, rbias)]
    pairs += [(doc_ref, doc), (attn_ref.at[0], out_ref.at[:, pl.ds(3 * width, width)])]
    pairs += [(qkv_ref.at[0, i], out_ref.at[:, pl.ds(i * width, width)]) for i in range(3)]
    pairs += [
        (rel_ref.at[:, pl.ds(i * half, half)], out_ref.at[pl.ds(i * part, part), pl.ds(at, half)])
        for i in range(2)
    ]
    run_copies(pairs, sems)
    at += half
    scr[...] = jnp.zeros_like(scr)
    for layer in range(layers):
        scr[2 * layer : 2 * layer + 2, :own] = gain[layer].astype(F32)
        base = 2 * layers + 2 * layer
        scr[base : base + 2, :own] = bias[layer].astype(F32)
    scr[4 * layers : 4 * layers + 1, :own] = rgain[...].astype(F32)
    scr[4 * layers + 1 : 4 * layers + 2, :own] = rbias[...].astype(F32)
    small = scr[...].T[:own, :]
    row = lax.broadcasted_iota(jnp.int32, small.shape, 0)
    upper = lax.broadcasted_iota(jnp.int32, small.shape, 1) >= LANES // 2
    doc_row = doc[...].astype(F32)
    turned = pltpu.roll(doc_row, LANES // 2, 1)
    small = jnp.where(upper & (row == 0), turned, small)
    small = jnp.where(upper & (row == 1), doc_row, small)
    out_ref[:, at : at + LANES] = small.astype(BF16)


def pack_kernel(index, *refs):
    ins, (out_ref, sems) = refs[: len(index)], refs[-2:]
    pairs, at = [], 0
    for ref, lead in zip(ins, index):
        cols = ref.shape[-1]
        pairs.append((ref.at[lead], out_ref.at[:, pl.ds(at, cols)]))
        at += cols
    run_copies(pairs, sems)


def stack_kernel(count, *refs):
    out_ref = refs[-1]
    rows = refs[0].shape[0]
    for i in range(count):
        out_ref[i * rows : (i + 1) * rows, :] = refs[i][...]


def assemble(dims, x_inner, place_ref, pieces, moves, sems):
    core_count, z_count, x_count, zl_count, own = dims
    x, core, z = place_ref[1], place_ref[3], place_ref[4]
    pairs = []
    for c_shift in range(core_count):
        for z_shift in range(z_count):
            for x_shift in range(x_count):
                place = z_shift * x_count + x_shift if x_inner else x_shift * z_count + z_shift
                from_c = lax.rem(core - c_shift + core_count, core_count)
                from_z = lax.rem(z - z_shift + z_count, z_count)
                from_x = lax.rem(x - x_shift + x_count, x_count)
                zh, zl = lax.div(from_z, zl_count), lax.rem(from_z, zl_count)
                owner = ((zh * core_count + from_c) * x_count + from_x) * zl_count + zl
                for row, rows, col, cols, target, step, to_col in moves:
                    start = pl.multiple_of(owner * step, step)
                    pairs.append(
                        (
                            pieces[c_shift].at[pl.ds(place * own + row, rows), pl.ds(col, cols)],
                            target.at[pl.ds(start, rows), pl.ds(to_col, cols)],
                        )
                    )
    run_copies(pairs, sems)


def start_kernel(dims, scale, place_ref, one_ref, two_ref, tokens_ref, *refs):
    qkv_ref, attn_ref, small_ref, q_ref, kv_ref, sems = refs
    own = dims[-1]
    wide = qkv_ref.shape[1]
    width = wide // 3
    moves = (
        (0, own, 0, wide, qkv_ref, own, 0),
        (0, own, wide, width, attn_ref, own, 0),
        (0, own, one_ref.shape[1] - LANES, LANES, small_ref, own, 0),
    )
    assemble(dims, True, place_ref, (one_ref, two_ref), moves, sems)
    low = tokens_ref[...]
    kv_ref[...] = dot(low, qkv_ref[:, width:], 1, 0).astype(BF16)
    q_ref[...] = (scale * dot(low, qkv_ref[:, :width], 1, 0)).astype(BF16)


def rest_kernel(dims, x_inner, outs, place_ref, one_ref, two_ref, *refs):
    targets, sems = refs[-outs - 1 : -1], refs[-1]
    own = dims[-1]
    moves, at = [], 0
    for target in targets:
        cols = target.shape[1]
        moves.append((0, own, at, cols, target, own, 0))
        at += cols
    assemble(dims, x_inner, place_ref, (one_ref, two_ref), moves, sems)


def relative_kernel(dims, layers, place_ref, one_ref, two_ref, small_ref, *refs):
    low_ref, vec_ref, doc_ref, rel_ref, sems = refs
    own = dims[-1]
    part = own // 2
    half = rel_ref.shape[1] // 2
    at = one_ref.shape[1] - LANES - half
    moves = (
        (0, part, at, half, rel_ref, part, 0),
        (part, part, at, half, rel_ref, part, half),
    )
    assemble(dims, True, place_ref, (one_ref, two_ref), moves, sems)
    turned = small_ref[...].astype(F32).T[: vec_ref.shape[0], :]
    vec_ref[...] = turned
    unit, _ = unit_of(rel_ref[...].astype(F32))
    gain, bias = turned[4 * layers : 4 * layers + 1], turned[4 * layers + 1 : 4 * layers + 2]
    low_ref[...] = (unit * gain + bias).astype(BF16)
    blocks = doc_ref.shape[1] // LANES
    span = blocks * own
    start = pl.multiple_of(place_ref[0] * span, span)
    mine = small_ref[pl.ds(start, span), :].astype(F32)
    upper = lax.broadcasted_iota(jnp.int32, (1, LANES), 1) >= LANES // 2
    for block in range(blocks):
        first = pltpu.roll(mine[block * own : block * own + 1, :], LANES // 2, 1)
        second = mine[block * own + 1 : block * own + 2, :]
        doc_ref[:, block * LANES : (block + 1) * LANES] = jnp.where(upper, second, first)


def table_kernel(index_ref, table_ref):
    count, buckets, win = table_ref.shape
    bucket = lax.broadcasted_iota(jnp.int32, (buckets, win), 0)
    for i in range(count):
        same = bucket == index_ref[i : i + 1, :]
        table_ref[i] = jnp.where(same, 1.0, 0.0).astype(BF16)


def position_kernel(scale, skip, rel_ref, qkv_ref, table_ref, pk_ref, pq_rev_ref, pq_ref):
    width = pk_ref.shape[0]
    pos_q = (scale * dot(rel_ref[...], qkv_ref[:, skip : skip + width], 1, 0)).astype(BF16)
    pos_k = dot(rel_ref[...], qkv_ref[:, skip + width : skip + 2 * width], 1, 0).astype(BF16)
    pk_ref[...] = dot(pos_k, table_ref[0], 0, 0).astype(BF16)
    pq_rev_ref[...] = dot(pos_q, table_ref[1], 0, 0).astype(BF16)
    pq_ref[...] = dot(pos_q, table_ref[2], 0, 0).astype(BF16)


def project_kernel(scale, rows_of, skip, hidden_ref, *refs):
    pieces, rest = refs[:4], refs[4:]
    vec_ref, qkv_ref, pre_ref, stream_ref, low_ref, q_ref, kv_ref = rest
    width = q_ref.shape[1]
    gain, bias = rows_of
    pre = hidden_ref[...] + sum_pieces(pieces)
    pre_ref[...] = pre
    unit, _ = unit_of(pre)
    stream = unit * vec_ref[gain : gain + 1, :] + vec_ref[bias : bias + 1, :]
    stream_ref[...] = stream
    low = stream.astype(BF16)
    low_ref[...] = low
    kv_ref[...] = dot(low, qkv_ref[:, skip + width : skip + 3 * width], 1, 0).astype(BF16)
    q_ref[...] = (scale * dot(low, qkv_ref[:, skip : skip + width], 1, 0)).astype(BF16)


def gather_kernel(shape, place_ref, *refs):
    blocks, kv_ref, sems = refs[:-2], refs[-2], refs[-1]
    rows = blocks[0].shape[0]
    pairs = []
    for block, shift in zip(blocks, ctx_shifts(*shape)):
        owner = ctx_owner(place_ref, shift, -1, *shape)
        start = pl.multiple_of(owner * rows, rows)
        pairs.append((block, kv_ref.at[pl.ds(start, rows), :]))
    run_copies(pairs, sems)


def attention_kernel(q_ref, kv_ref, *refs):
    pk_ref, pq_ref, doc_i_ref, doc_j_ref = refs[:4]
    mix_ref, p_ref, to_ref, q_all = refs[4:]
    rows, width = q_ref.shape
    keys = kv_ref.shape[0]
    win = pk_ref.shape[1]
    heads = width // HEAD_DIM
    for head in range(heads):
        q = only_head(q_ref[...], head)
        q_all[head] = q
        to = dot(q, pk_ref[...], 1, 0)
        to = pltpu.roll(to, win + 1 - rows, 1, stride=1, stride_axis=0)
        to_ref[head] = to[:, :keys]
    doc_i = jnp.broadcast_to(doc_i_ref[...].astype(F32), (rows, rows)).T
    mix = jnp.zeros((rows, width), F32)
    for head in range(heads):
        q = q_all[head]
        parts = []
        for start in range(0, keys, BLOCK):
            key_block = kv_ref[start : start + BLOCK, :width]
            first = win - 2 * BLOCK - start
            pq = only_head(pq_ref[:, first : first + 2 * BLOCK], head, 0)
            off = dot(key_block, pq, 1, 0)
            off = pltpu.roll(off, BLOCK, 1, stride=1, stride_axis=0)
            s = dot(q, key_block, 1, 1) + to_ref[head, :, start : start + BLOCK]
            s = s + off[:, :BLOCK].T
            same = doc_i == doc_j_ref[:, start : start + BLOCK]
            parts.append(jnp.where(same, s, NEG))
        s = jnp.concatenate(parts, axis=1)
        e = jnp.exp(s - jnp.max(s, axis=1, keepdims=True))
        p = (e / jnp.sum(e, axis=1, keepdims=True)).astype(BF16)
        p_ref[head] = p
        mix = jnp.where(head_mask(mix.shape, head), dot(p, kv_ref[:, width:], 1, 0), mix)
    mix_ref[...] = mix.astype(BF16)


def attended_kernel(skip, mix_ref, full_ref, part_ref):
    attn = full_ref[:, skip : skip + mix_ref.shape[1]]
    part_ref[...] = dot(mix_ref[...], attn, 1, 1).astype(BF16)


def feed_kernel(rows_of, skip, stream_ref, *refs):
    pieces, rest = refs[:4], refs[4:]
    vec_ref, full_ref = rest[:2]
    pre_ref, hidden_ref, low_ref, slope_ref, active_ref, part_ref = rest[2:]
    units = active_ref.shape[1]
    gain, bias = rows_of
    pre = stream_ref[...].astype(F32) + sum_pieces(pieces)
    pre_ref[...] = pre
    unit, _ = unit_of(pre)
    hidden = unit * vec_ref[gain : gain + 1, :] + vec_ref[bias : bias + 1, :]
    hidden_ref[...] = hidden
    low = hidden.astype(BF16)
    low_ref[...] = low
    inner = dot(low, full_ref[:, skip : skip + units], 1, 0)
    below = 0.5 * (1.0 + lax.erf(inner * math.sqrt(0.5)))
    bell = jnp.exp(-0.5 * inner * inner) * (1.0 / math.sqrt(2.0 * math.pi))
    slope_ref[...] = below + inner * bell
    active = (inner * below).astype(BF16)
    active_ref[...] = active
    out = full_ref[:, skip + units : skip + 2 * units]
    part_ref[...] = dot(active, out, 1, 1).astype(BF16)


def end_kernel(rows_of, hidden_ref, *refs):
    pieces, (vec_ref, pre_ref, out_ref) = refs[:4], refs[4:]
    gain, bias = rows_of
    pre = hidden_ref[...] + sum_pieces(pieces)
    pre_ref[...] = pre
    unit, _ = unit_of(pre)
    stream = unit * vec_ref[gain : gain + 1, :] + vec_ref[bias : bias + 1, :]
    out_ref[...] = stream.astype(BF16)


def column_sums(ref, first, second):
    ref[...] = jnp.zeros_like(ref)
    ref[0:1, :] = jnp.sum(first, axis=0, keepdims=True)
    ref[1:2, :] = jnp.sum(second, axis=0, keepdims=True)


def feed_back_kernel(gain, skip, has_pieces, grad_ref, *refs):
    pieces, rest = (refs[:4], refs[4:]) if has_pieces else ((), refs)
    pre_ref, vec_ref, slope_ref, full_ref = rest[:4]
    d_pre_ref, d_low_ref, d_inner_ref, part_ref, norm_ref = rest[4:]
    units = slope_ref.shape[1]
    grad = grad_ref[...].astype(F32)
    if has_pieces:
        grad = grad + sum_pieces(pieces)
    back, gain_terms = normalize_back(pre_ref[...], vec_ref[gain : gain + 1, :], grad)
    column_sums(norm_ref, gain_terms, grad)
    d_pre_ref[...] = back
    low = back.astype(BF16)
    d_low_ref[...] = low
    out = full_ref[:, skip + units : skip + 2 * units]
    inner = (dot(low, out, 1, 0) * slope_ref[...]).astype(BF16)
    d_inner_ref[...] = inner
    part_ref[...] = dot(inner, full_ref[:, skip : skip + units], 1, 1).astype(BF16)


def attention_back_kernel(gain, skip, scale, place_ref, *refs):
    pieces, rest = refs[:4], refs[4:]
    d_out_ref, pre_ref, vec_ref, full_ref, q_ref, kv_ref, pk_ref, pq_ref, p_ref = rest[:9]
    d_pre_ref, d_low_ref, dq_ref, dpk_ref, dpq_ref, norm_ref = rest[9:15]
    ds_all, to_all, dk_pos, dm_all, q_all, qr_all, dpq_sum, dkv = rest[-8:]
    dkv_refs = rest[15:-8]
    rows, width = q_ref.shape
    keys = kv_ref.shape[0]
    heads = width // HEAD_DIM
    win = pk_ref.shape[1]

    grad = d_out_ref[...] + sum_pieces(pieces)
    back, gain_terms = normalize_back(pre_ref[...], vec_ref[gain : gain + 1, :], grad)
    column_sums(norm_ref, gain_terms, grad)
    d_pre_ref[...] = back
    d_low = back.astype(BF16)
    d_low_ref[...] = d_low
    d_mixture = dot(d_low, full_ref[:, skip : skip + width], 1, 0)

    row = lax.broadcasted_iota(jnp.int32, (rows, rows), 0)
    col = lax.broadcasted_iota(jnp.int32, (rows, rows), 1)
    flip = jnp.where(row + col == rows - 1, 1.0, 0.0).astype(BF16)
    q_back = dot(flip, q_ref[...], 1, 0)
    content = jnp.zeros((rows, width), F32)
    position = jnp.zeros((rows, width), F32)
    dpq_sum[...] = jnp.zeros_like(dpq_sum)
    for head in range(heads):
        here = slice(head * rows, (head + 1) * rows)
        mask = head_mask((rows, width), head)
        dm = only_head(d_mixture, head)
        dm_all[here, :] = dm
        q_all[here, :] = only_head(q_ref[...], head)
        qr_all[here, :] = only_head(q_back, head)
        p = p_ref[head].astype(F32)
        da = dot(dm, kv_ref[:, width:], 1, 1)
        ds = (p * (da - jnp.sum(p * da, axis=1, keepdims=True))).astype(BF16)
        ds_all[here, :] = ds
        content = jnp.where(mask, dot(ds, kv_ref[:, :width], 1, 0), content)
        ds_back = dot(flip, ds, 1, 0)
        to = jnp.concatenate([ds_back, jnp.zeros((rows, win - keys), F32)], axis=1)
        to = pltpu.roll(to, 0, 1, stride=1, stride_axis=0).astype(BF16)
        to_all[here, :] = to
        position = jnp.where(mask, dot(to, pk_ref[...], 1, 1), position)
        for start in range(0, keys, BLOCK):
            off = ds_back[:, start : start + BLOCK].T
            off = jnp.concatenate([off, jnp.zeros((BLOCK, BLOCK), F32)], axis=1)
            off = pltpu.roll(off, 0, 1, stride=1, stride_axis=0).astype(BF16)
            key_block = only_head(kv_ref[start : start + BLOCK, :width], head)
            dpq_sum[start : start + 2 * BLOCK, :] += dot(off, key_block, 0, 0)
            more = dot(off, pq_ref[:, start : start + 2 * BLOCK], 1, 1)
            if head:
                more = jnp.where(
                    head_mask(more.shape, head), more, dk_pos[start : start + BLOCK, :]
                )
            dk_pos[start : start + BLOCK, :] = more
    high = position.astype(BF16)
    low = (position - high.astype(F32)).astype(BF16)
    dq = content + dot(flip, high, 1, 0) + dot(flip, low, 1, 0)
    dq_ref[...] = (scale * dq).astype(BF16)
    dkv[:, :width] = (dot(ds_all[...], q_all[...], 0, 0) + dk_pos[...]).astype(BF16)
    p_all = p_ref[...].reshape(heads * rows, keys)
    dkv[:, width:] = dot(p_all, dm_all[...], 0, 0).astype(BF16)
    x_count = len(dkv_refs)
    zl_count = keys // (rows * x_count)
    for shift, target in enumerate(dkv_refs):
        x = lax.rem(place_ref[1] + shift, x_count)
        for side in range(zl_count):
            zl = lax.rem(place_ref[2] + side, zl_count)
            start = pl.multiple_of((x * zl_count + zl) * rows, rows)
            target[side * rows : (side + 1) * rows, :] = dkv[pl.ds(start, rows), :]
    dpk_ref[...] = dot(to_all[...], qr_all[...], 0, 0).astype(BF16)
    dpq_ref[...] = (scale * dpq_sum[...]).astype(BF16)


def position_back_kernel(table_ref, dpk_ref, dpq_ref, low_ref, rows_ref):
    width = dpk_ref.shape[1]
    d_k = dot(table_ref[0], dpk_ref[...], 1, 0).astype(BF16)
    d_q = dot(table_ref[2], dpq_ref[...], 1, 0).astype(BF16)
    low_ref[:, :width] = d_q
    low_ref[:, width:] = d_k
    owners, step = rows_ref.shape[0], rows_ref.shape[1] // 2
    for owner in range(owners):
        rows_ref[owner, :step, :] = d_q[owner * step : (owner + 1) * step, :]
        rows_ref[owner, step:, :] = d_k[owner * step : (owner + 1) * step, :]


def picked_columns(ref, core, parts=2):
    run = ref.shape[1] // (2 * parts)
    picked = [ref[:, pl.ds(pl.multiple_of((2 * i + core) * run, run), run)] for i in range(parts)]
    return jnp.concatenate(picked, axis=1)


def scatter_kernel(own_core, names, place_ref, *refs):
    refs = list(refs)
    core = place_ref[3] if own_core else 1 - place_ref[3]
    parts = []
    for name in names:
        if name == "qkv":
            low_ref, all_ref, rel_ref, pos_ref = refs[:4]
            del refs[:4]
            value = dot(picked_columns(low_ref, core), all_ref[...], 0, 0)
            terms = dot(picked_columns(rel_ref, core), pos_ref[...], 0, 0)
            wide = pos_ref.shape[1]
            parts += [value[:, :wide] + terms, value[:, wide:]]
        elif name == "norm":
            hid = picked_columns(refs.pop(0), core)
            out = picked_columns(refs.pop(0), core)
            rows = jnp.concatenate([hid[0:1], out[0:1], hid[1:2], out[1:2]], axis=0)
            rows = jnp.concatenate([rows, jnp.zeros((LANES - 4, rows.shape[1]), F32)], axis=0)
            parts.append(rows.T)
        elif name == "pos":
            rows_ref = refs.pop(0)
            run = rows_ref.shape[0] // 4
            picked = [rows_ref[pl.ds((2 * i + core) * run, run)] for i in range(2)]
            picked = jnp.concatenate(picked, axis=0).astype(F32)
            parts.append(picked.reshape(-1, rows_ref.shape[2]))
        else:
            left, right = refs[:2]
            del refs[:2]
            parts.append(dot(picked_columns(left, core), right[...], 0, 0))
    if not own_core:
        out_ref = refs[0]
        at = 0
        for part in parts:
            out_ref[:, at : at + part.shape[1]] = part.astype(BF16)
            at += part.shape[1]
        return
    if len(refs) == 2:
        arrived, outs, scr = refs[0], (), refs[1]
    else:
        arrived, outs, scr = refs[0], refs[1:-1], refs[-1]
    at = 0
    for part in parts:
        cols = part.shape[1]
        scr[:, at : at + cols] = (part + arrived[:, at : at + cols].astype(F32)).astype(BF16)
        at += cols
    if not outs:
        return
    z_count = len(outs)
    own = scr.shape[0] // 16
    x_count = outs[0].shape[0] // own
    zl_count = scr.shape[0] // (own * x_count * 2)
    for shift, out_ref in enumerate(outs):
        z = lax.rem(place_ref[4] + shift, z_count)
        zh, zl = lax.div(z, zl_count), lax.rem(z, zl_count)
        for x in range(x_count):
            start = pl.multiple_of(((zh * x_count + x) * zl_count + zl) * own, own)
            out_ref[x * own : (x + 1) * own, :] = scr[pl.ds(start, own), :]


def middle_kernel(count, place_ref, *refs):
    pieces, outs, scr = refs[:count], refs[count:-1], refs[-1]
    total = pieces[0][...].astype(F32)
    for piece in pieces[1:]:
        total = total + piece[...].astype(F32)
    scr[...] = total.astype(BF16)
    own = outs[0].shape[0]
    for shift, out_ref in enumerate(outs):
        x = lax.rem(place_ref[1] + shift, len(outs))
        out_ref[...] = scr[pl.ds(pl.multiple_of(x * own, own), own), :]


def halves_kernel(count, *refs):
    pieces, (mine_ref, other_ref) = refs[:count], refs[count:]
    total = pieces[0][...].astype(F32)
    for piece in pieces[1:]:
        total = total + piece[...].astype(F32)
    rows = mine_ref.shape[0]
    mine_ref[...] = total[:rows, :]
    other_ref[...] = total[rows:, :].astype(BF16)


def stream_back_kernel(skip, dq_ref, mine_ref, other_ref, qkv_ref, all_ref, part_ref):
    total = mine_ref[...] + other_ref[...].astype(F32)
    both = jnp.concatenate([dq_ref[...], total.astype(BF16)], axis=1)
    all_ref[...] = both
    qkv = qkv_ref[:, skip : skip + both.shape[1]]
    part_ref[...] = dot(both, qkv, 1, 1).astype(BF16)


def total_of(refs, first, cols):
    total = refs[0][:, first : first + cols].astype(F32)
    for ref in refs[1:]:
        total = total + ref[:, first : first + cols].astype(F32)
    return total


def total_kernel(*refs):
    refs[-1][...] = total_of(refs[:-1], 0, refs[-1].shape[1])


def groups_of(counts, refs):
    return [refs[sum(counts[:i]) : sum(counts[: i + 1])] for i in range(len(counts))]


def early_end_kernel(counts, firsts, *refs):
    in_ref, out_ref = refs[-2:]
    hidden = in_ref.shape[2]
    for layer, pieces in enumerate(groups_of(counts, refs)):
        in_ref[layer] = total_of(pieces, firsts[layer], hidden)
        out_ref[layer] = total_of(pieces, firsts[layer] + hidden, hidden)


def middle_end_kernel(counts, firsts, *refs):
    attn_ref, gain_ref, bias_ref = refs[-3:]
    width = attn_ref.shape[2]
    for layer, pieces in enumerate(groups_of(counts, refs)):
        attn_ref[layer] = total_of(pieces, firsts[layer], width)
        norms = total_of(pieces, firsts[layer] + width, LANES).T
        gain_ref[layer] = norms[0:2, :]
        bias_ref[layer] = norms[2:4, :]


def late_end_kernel(counts, *refs):
    out_ref = refs[-1]
    width = out_ref.shape[3]
    for layer, pieces in enumerate(groups_of(counts, refs)):
        for i in range(3):
            out_ref[layer, i] = total_of(pieces, i * width, width)


def relative_term_kernel(counts, firsts, skips, width, *refs):
    out_ref = refs[-1]
    layers = len(counts)
    total = None
    for layer, pieces in enumerate(groups_of(counts, refs)):
        qkv_ref, skip = refs[sum(counts) + layer], skips[layer]
        moved = total_of(pieces, firsts[layer], width).astype(BF16)
        step = moved.shape[0] // 2
        term = dot(moved[:step], qkv_ref[:, skip : skip + width], 1, 1)
        term = term + dot(moved[step:], qkv_ref[:, skip + width : skip + 2 * width], 1, 1)
        total = term if total is None else total + term
    out_ref[...] = total


def token_end_kernel(grad_ref, *refs):
    refs[-1][...] = (grad_ref[...] + sum_pieces(refs[:-1])).astype(BF16)


def relative_end_kernel(gain, *refs):
    pieces, (rel_ref, vec_ref, grad_ref, ends_ref) = refs[:4], refs[4:]
    d_rel = sum_pieces(pieces)
    back, gain_terms = normalize_back(
        rel_ref[...].astype(F32), vec_ref[gain : gain + 1, :], d_rel
    )
    grad_ref[...] = back
    owners, _, own = ends_ref.shape
    for k, terms in enumerate((gain_terms, d_rel)):
        sums = jnp.sum(terms, axis=0, keepdims=True)
        for owner in range(owners):
            first = owner * own // LANES * LANES
            chunk = sums[:, first : first + LANES]
            offset = owner * own - first
            if offset:
                chunk = pltpu.roll(chunk, LANES - offset, 1)
            ends_ref[owner, k : k + 1, :] = chunk[:, :own]


def shifted(values, axes, shift):
    count = lax.axis_size(axes)
    return lax.ppermute(values, axes, [(i, (i + shift) % count) for i in range(count)])


def along(run, values, axes):
    pieces = moved_on([values] * lax.axis_size(axes), axes)
    rows, cols = values.shape
    (out,) = run(
        functools.partial(stack_kernel, len(pieces)),
        [((len(pieces) * rows, cols), BF16)],
        pieces,
        name="stack",
    )
    return out


def ctx_shifted(values):
    x_count, zl_count = lax.axis_size("x"), lax.axis_size("zl")
    shifts = ctx_shifts(x_count, zl_count)
    moved = [values[0]]
    for i in reversed(range(1, len(shifts))):
        dx, dz = shifts[i]
        pairs = []
        for x in range(x_count):
            for z in range(zl_count):
                target = (x + dx) % x_count * zl_count + (z + dz) % zl_count
                pairs.append((x * zl_count + z, target))
        moved.insert(1, lax.ppermute(values[i], CTX, pairs))
    return moved


def tp_pieces(low):
    count = lax.axis_size("tp")
    order = sorted(range(1, count), key=lambda s: -min(s, count - s))
    moved = {s: shifted(low, "tp", s) for s in order}
    return [low] + [moved[s] for s in range(1, count)]


def moved_on(pieces, axes):
    count = len(pieces)
    order = sorted(range(1, count), key=lambda s: -min(s, count - s))
    moved = {s: shifted(pieces[s], axes, s) for s in order}
    return [pieces[0]] + [moved[s] for s in range(1, count)]


def local(
    tokens,
    cotangent,
    w_qkv,
    w_attn,
    w_in,
    w_out,
    ln_gain,
    ln_bias,
    rel_emb,
    rel_gain,
    rel_bias,
    doc_ids,
    rel_bucket,
):
    _, rows, model = tokens.shape
    layers, _, own, width = w_qkv.shape
    hidden_units = w_in.shape[2]
    heads = width // HEAD_DIM
    ctx_count = lax.axis_size(CTX)
    owners = lax.axis_size(OWNERS)
    length = rows * ctx_count
    row_start = lax.axis_index(CTX) * rows
    scale = 1.0 / math.sqrt(3.0 * HEAD_DIM)
    win = length + rows
    rel_own = rel_emb.shape[0]
    buckets = rel_own * owners
    wide = 3 * width

    shape = (lax.axis_size("x"), lax.axis_size("zl"))
    dims = (lax.axis_size("core"), lax.axis_size(ZED), *shape, own)
    place = [("zh", "core"), "x", "zl", "core", ZED]
    place = jnp.stack([lax.axis_index(axes) for axes in place]).astype(jnp.int32)
    dma = pltpu.SemaphoreType.DMA

    previous = []

    def run(*args, **kwargs):
        outs = call(*args, after=tuple(previous), **kwargs)
        previous[:] = [outs[-1]]
        return outs

    attn_rows, out_rows = jnp.swapaxes(w_attn, 1, 2), jnp.swapaxes(w_out, 1, 2)
    start_cols = wide + width + model // 2 + LANES
    (start_pack,) = run(
        pack_start_kernel,
        [((own, start_cols), BF16)],
        [w_qkv, attn_rows, rel_emb, ln_gain, ln_bias, rel_gain[None], rel_bias[None], doc_ids],
        hbm=range(8),
        scratch=[
            pltpu.VMEM((LANES, LANES), F32),
            pltpu.VMEM(ln_gain.shape, BF16),
            pltpu.VMEM(ln_bias.shape, BF16),
            pltpu.VMEM((1, own), BF16),
            pltpu.VMEM((1, own), BF16),
            pltpu.VMEM((1, rows), jnp.int32),
            dma((11,)),
        ],
        name="pack_start",
    )
    arrays, index = [w_in, out_rows], [0, 0]
    feed_at, qkv_at, attn_at = [0], [0], [0]
    at = 2 * hidden_units
    for layer in range(1, layers):
        arrays += [w_qkv, w_qkv, w_qkv, attn_rows, w_in, out_rows]
        index += [(layer, 0), (layer, 1), (layer, 2), layer, layer, layer]
        qkv_at.append(at)
        attn_at.append(at + wide)
        feed_at.append(at + wide + width)
        at += wide + width + 2 * hidden_units
    (rest,) = run(
        functools.partial(pack_kernel, index),
        [((own, at), BF16)],
        arrays,
        hbm=range(len(arrays)),
        scratch=[dma((len(arrays),))],
        name="pack",
    )
    full = lax.all_gather(rest, OWNERS, axis=0, tiled=True)

    padded = jnp.pad(rel_bucket, (1, 1), mode="edge")
    to_index = lax.dynamic_slice_in_dim(padded, row_start, win, 0)
    from_index = lax.dynamic_slice_in_dim(padded, length - rows - row_start + 1, win, 0)
    index = jnp.stack([to_index[::-1], from_index[::-1], from_index])
    (tables,) = run(table_kernel, [((3, buckets, win), BF16)], [index], limit=8, name="tables")

    start_x = along(run, start_pack, "x")
    start_z = along(run, start_x, ZED)
    start_pieces = [start_z, shifted(start_z, "core", 1)]
    qkv, attn, small, q, key_value = run(
        functools.partial(start_kernel, dims, scale),
        [
            ((model, wide), BF16),
            ((model, width), BF16),
            ((model, LANES), BF16),
            ((rows, width), BF16),
            ((rows, 2 * width), BF16),
        ],
        [place, *start_pieces, tokens[0]],
        smem=(0,),
        anys=(1, 2),
        scratch=[dma((3 * owners,))],
        name="start",
    )
    rel_low, vecs, doc_j = run(
        functools.partial(relative_kernel, dims, layers),
        [((buckets, model), BF16), ((16, model), F32), ((1, length), F32)],
        [place, *start_pieces, small],
        smem=(0,),
        anys=(1, 2),
        scratch=[pltpu.VMEM((buckets, model), BF16), dma((2 * owners,))],
        name="relative",
    )
    qkvs = [qkv] + [full] * (layers - 1)
    attns = [attn] + [full] * (layers - 1)

    token_low = tokens[0]
    stream = token_low
    kept = []
    hidden, pieces = None, None
    tile = (rows, model)
    for layer in range(layers):
        if layer:
            pre_out, stream, stream_low, q, key_value = run(
                functools.partial(
                    project_kernel,
                    scale,
                    (2 * layer - 1, 2 * layers + 2 * layer - 1),
                    qkv_at[layer],
                ),
                [
                    (tile, F32),
                    (tile, F32),
                    (tile, BF16),
                    ((rows, width), BF16),
                    ((rows, 2 * width), BF16),
                ],
                [hidden, *pieces, vecs, qkvs[layer]],
                name="project",
            )
            kept[-1]["pre_out"] = pre_out
        else:
            stream_low = token_low
        blocks = ctx_shifted([key_value] * ctx_count)
        pk, pq_rev, pq = run(
            functools.partial(position_kernel, scale, qkv_at[layer]),
            [((width, win), BF16)] * 3,
            [rel_low, qkvs[layer], tables],
            name="position",
        )
        (kv,) = run(
            functools.partial(gather_kernel, shape),
            [((length, 2 * width), BF16)],
            [place, *blocks],
            smem=(0,),
            anys=range(1, 1 + ctx_count),
            scratch=[dma((ctx_count,))],
            name="gather",
        )
        mixture, p = run(
            attention_kernel,
            [((rows, width), BF16), ((heads, rows, length), BF16)],
            [q, kv, pk, pq_rev, doc_ids, doc_j],
            scratch=[
                pltpu.VMEM((heads, rows, length), F32),
                pltpu.VMEM((heads, rows, width), BF16),
            ],
            limit=16,
            name="attention",
        )
        (part,) = run(
            functools.partial(attended_kernel, attn_at[layer]),
            [(tile, BF16)],
            [mixture, attns[layer]],
            name="attended",
        )
        pre_hidden, hidden, hidden_low, slope, active, part = run(
            functools.partial(feed_kernel, (2 * layer, 2 * layers + 2 * layer), feed_at[layer]),
            [
                (tile, F32),
                (tile, F32),
                (tile, BF16),
                ((rows, hidden_units), F32),
                ((rows, hidden_units), BF16),
                (tile, BF16),
            ],
            [stream, *tp_pieces(part), vecs, full],
            name="feed",
        )
        pieces = tp_pieces(part)
        kept.append(
            dict(
                stream_low=stream_low,
                q=q,
                kv=kv,
                pk=pk,
                pq=pq,
                p=p,
                mixture=mixture,
                pre_hidden=pre_hidden,
                hidden_low=hidden_low,
                slope=slope,
                active=active,
            )
        )
    last = layers - 1
    pre_out, out_local = run(
        functools.partial(end_kernel, (2 * last + 1, 2 * layers + 2 * last + 1)),
        [(tile, F32), (tile, BF16)],
        [hidden, *pieces, vecs],
        name="end",
    )
    kept[-1]["pre_out"] = pre_out

    grad_parts = [cotangent[0]]
    z_count, x_count = lax.axis_size(ZED), lax.axis_size("x")

    def scatter_other(names, ins, cols, label):
        (other,) = run(
            functools.partial(scatter_kernel, False, names),
            [((model // 2, cols), BF16)],
            [place, *ins],
            smem=(0,),
            limit=12,
            name=label + "_other",
        )
        return shifted(other, "core", 1)

    def scatter_own(names, ins, arrived, label):
        half, cols = arrived.shape
        pieces = run(
            functools.partial(scatter_kernel, True, names),
            [((half // z_count, cols), BF16)] * z_count,
            [place, *ins, arrived],
            smem=(0,),
            scratch=[pltpu.VMEM((half, cols), BF16)],
            limit=12,
            name=label + "_own",
        )
        return moved_on(pieces, ZED)

    def scatter_middle(pieces, label):
        rows_here, cols = pieces[0].shape
        pieces = run(
            functools.partial(middle_kernel, len(pieces)),
            [((rows_here // x_count, cols), BF16)] * x_count,
            [place, *pieces],
            smem=(0,),
            scratch=[pltpu.VMEM((rows_here, cols), BF16)],
            name=label + "_middle",
        )
        return moved_on(pieces, "x")

    def scatter_total(pieces, label):
        return list(run(total_kernel, [(pieces[0].shape, F32)], pieces, name=label + "_total"))

    early_names, early_cols = ("in", "out"), 2 * hidden_units
    middle_names, middle_cols = ("attn", "norm", "pos"), 2 * width + LANES
    late_names, late_cols = ("qkv",), wide
    both_names, both_cols = late_names + middle_names, late_cols + middle_cols
    early_sums, middle_sums, late_sums = [None] * layers, [None] * layers, [None] * layers
    both = None
    for layer in reversed(range(layers)):
        k = kept[layer]
        d_pre_out, d_out_low, d_inner, part, norm_out = run(
            functools.partial(
                feed_back_kernel, 2 * layer + 1, feed_at[layer], len(grad_parts) > 1
            ),
            [
                (tile, F32),
                (tile, BF16),
                ((rows, hidden_units), BF16),
                (tile, BF16),
                ((8, model), F32),
            ],
            [*grad_parts, k["pre_out"], vecs, k["slope"], full],
            name="feed_back",
        )
        pieces = tp_pieces(part)
        early_in = [k["hidden_low"], d_inner, d_out_low, k["active"]]
        arrived = scatter_other(early_names, early_in, early_cols, "early")
        if both is not None:
            both = scatter_middle(both, "late")
        early = scatter_own(early_names, early_in, arrived, "early")
        backs = run(
            functools.partial(attention_back_kernel, 2 * layer, attn_at[layer], scale),
            [
                (tile, F32),
                (tile, BF16),
                ((rows, width), BF16),
                ((win, width), BF16),
                ((win, width), BF16),
                ((8, model), F32),
            ]
            + [((length // x_count, 2 * width), BF16)] * x_count,
            [place, *pieces, d_pre_out, k["pre_hidden"], vecs, attns[layer]]
            + [k["q"], k["kv"], k["pk"], k["pq"], k["p"]],
            smem=(0,),
            scratch=[
                pltpu.VMEM((heads * rows, length), BF16),
                pltpu.VMEM((heads * rows, win), BF16),
                pltpu.VMEM((length, width), F32),
                pltpu.VMEM((heads * rows, width), BF16),
                pltpu.VMEM((heads * rows, width), BF16),
                pltpu.VMEM((heads * rows, width), BF16),
                pltpu.VMEM((win, width), F32),
                pltpu.VMEM((length, 2 * width), BF16),
            ],
            limit=20,
            name="attention_back",
        )
        d_pre_hidden, d_attended, dq, dpk, dpq, norm_hidden = backs[:6]
        dkv = moved_on(backs[6:], "x")
        pos_low, pos_rows = run(
            position_back_kernel,
            [((buckets, 2 * width), BF16), ((owners, 2 * rel_own, width), BF16)],
            [tables, dpk, dpq],
            name="position_back",
        )
        middle_in = [d_attended, k["mixture"], norm_hidden, norm_out, pos_rows]
        if both is not None:
            both = scatter_total(both, "late")
            middle_sums[layer + 1] = late_sums[layer + 1] = both
        if layer:
            early = scatter_middle(early, "early")
        else:
            arrived = scatter_other(middle_names, middle_in, middle_cols, "middle")
            middle = scatter_own(middle_names, middle_in, arrived, "middle")
            early = scatter_middle(early, "early")
        mine, other = run(
            functools.partial(halves_kernel, x_count),
            [((rows, 2 * width), F32), ((rows, 2 * width), BF16)],
            dkv,
            name="halves",
        )
        other = shifted(other, "zl", 1)
        if not layer:
            middle_sums[layer] = scatter_middle(middle, "middle")
        dqkv, part = run(
            functools.partial(stream_back_kernel, qkv_at[layer]),
            [((rows, wide), BF16), (tile, BF16)],
            [dq, mine, other, qkvs[layer]],
            name="stream_back",
        )
        grad_parts = [d_pre_hidden] + tp_pieces(part)
        late_in = [k["stream_low"], dqkv, rel_low, pos_low]
        if layer:
            arrived = scatter_other(both_names, late_in + middle_in, both_cols, "late")
            early_sums[layer] = scatter_total(early, "early")
            both = scatter_own(both_names, late_in + middle_in, arrived, "late")
        else:
            arrived = scatter_other(late_names, late_in, late_cols, "late")
            early_sums[layer] = early
            late = scatter_own(late_names, late_in, arrived, "late")

    counts = [len(pieces) for pieces in middle_sums]
    (term,) = run(
        functools.partial(
            relative_term_kernel,
            counts,
            [width + LANES] + [wide + width + LANES] * (layers - 1),
            qkv_at,
            width,
        ),
        [((rel_own, model), F32)],
        sum(middle_sums, []) + qkvs,
        name="relative_term",
    )
    terms = tp_pieces(term)
    late_sums[0] = scatter_middle(late, "late")
    grad_rel, ends = run(
        functools.partial(relative_end_kernel, 4 * layers),
        [((rel_own, model), F32), ((owners, 2, own), F32)],
        [*terms, rel_emb, vecs],
        name="relative_end",
    )
    ends = lax.all_to_all(ends, OWNERS, 0, 0)
    (grad_tokens,) = run(token_end_kernel, [(tile, BF16)], grad_parts, name="token_end")
    grad_in, grad_out = run(
        functools.partial(early_end_kernel, [len(p) for p in early_sums], [0] * layers),
        [((layers, own, hidden_units), F32)] * 2,
        sum(early_sums, []),
        name="early_end",
    )
    grad_attn, grad_gain, grad_bias = run(
        functools.partial(middle_end_kernel, counts, [0] + [wide] * (layers - 1)),
        [((layers, own, width), F32), ((layers, 2, own), F32), ((layers, 2, own), F32)],
        sum(middle_sums, []),
        name="middle_end",
    )
    (grad_qkv,) = run(
        functools.partial(late_end_kernel, [len(p) for p in late_sums]),
        [((layers, 3, own, width), F32)],
        sum(late_sums, []),
        name="late_end",
    )
    grad_attn, grad_out = jnp.swapaxes(grad_attn, 1, 2), jnp.swapaxes(grad_out, 1, 2)
    ends = jnp.sum(ends, axis=0)
    return (
        out_local[None],
        grad_tokens[None],
        grad_qkv,
        grad_attn,
        grad_in,
        grad_out,
        grad_gain,
        grad_bias,
        grad_rel,
        ends[0],
        ends[1],
    )


def solution(mesh):
    sizes = mesh.shape
    zh, zl = 2, 2
    finer = Mesh(
        mesh.devices.reshape(zh, sizes["fsdp"] // zh, sizes["ctx"] // zl, zl, sizes["tp"]),
        ("zh", "core", "x", "zl", "tp"),
    )
    own = OWNERS
    fsdp = ("zh", "core")
    return jax.shard_map(
        local,
        mesh=finer,
        in_specs=(
            P(fsdp, CTX, None),
            P(fsdp, CTX, None),
            P(None, None, own, "tp"),
            P(None, "tp", own),
            P(None, own, "tp"),
            P(None, "tp", own),
            P(None, None, own),
            P(None, None, own),
            P(own, None),
            P(own),
            P(own),
            P(fsdp, CTX),
            P(),
        ),
        out_specs=(
            P(fsdp, CTX, None),
            P(fsdp, CTX, None),
            P(None, None, own, "tp"),
            P(None, "tp", own),
            P(None, own, "tp"),
            P(None, "tp", own),
            P(None, None, own),
            P(None, None, own),
            P(own, None),
            P(own),
            P(own),
        ),
        check_vma=False,
    )
```

time: 556 us -> 442 us (0.79)
  waiting for transfers between devices: 229 us -> 174 us
  local copies, waits for them, and re-layouts: 72.7 us -> 21.2 us
  between operations: 2.56 us -> 15.3 us
  Pallas kernels: 91.1 us -> 82 us
    all_to_all x7 -> x1, waiting for transfers between devices: 61.1 us -> 0.01 us  [local(): ends = lax.all_to_all(ends, OWNERS, 0, 0)]
    unnamed x346 -> x90, local copies, waits for them, and re-layouts: 70 us -> 17 us
    all_to_all x7 -> x1, starting transfers between devices: 34 us -> 3.9 us  [local(): ends = lax.all_to_all(ends, OWNERS, 0, 0)]
    ppermute x89 -> x77, waiting for transfers between devices: 168 us -> 138 us  [shifted(): lax.ppermute(values, axes, [(i, (i + shift) % count) for i in range(count)])]
    all_gather x0 -> x1, waiting for transfers between devices: none -> 25.4 us  [local(): full = lax.all_gather(rest, OWNERS, axis=0, tiled=True)]
    ppermute x0 -> x14, starting transfers between devices: none -> 20.2 us  [ctx_shifted(): moved.insert(1, lax.ppermute(values[i], CTX, pairs))]
    ppermute x0 -> x14, waiting for transfers between devices: none -> 10.3 us  [ctx_shifted(): moved.insert(1, lax.ppermute(values[i], CTX, pairs))]
    pallas_call x36 -> x52, Pallas kernels: 91.1 us -> 82 us  [call(): pl.pallas_call(without, in_specs=specs, out_specs=tuple((pl.BlockSpec(mem...]
  transfers between devices with their start and end apart: 96 -> 93, of which waited for: 43 -> 34; matrix products, arithmetic and copies ran while one was open for 2% -> 1% of each run, Pallas kernels for 12% -> 13%
where the time goes in v3:
time: 442 us; the launch traced here: 435 us
  waiting for transfers between devices  174 us (39%)
  starting transfers between devices  143 us (32%)
  Pallas kernels  82 us (19%)
  local copies, waits for them, and re-layouts  21.2 us (5%)
  between operations  15.3 us (3%)
    ppermute x77, waiting for transfers between devices, shifted(): lax.ppermute(values, axes, [(i, (i + shift) % count) for i in range(count)])  138 us
    ppermute x77, starting transfers between devices, shifted(): lax.ppermute(values, axes, [(i, (i + shift) % count) for i in range(count)])  119 us
    pallas_call x52, Pallas kernels, call(): pl.pallas_call(without, in_specs=specs, out_specs=tuple((pl.BlockSpec(mem...  82 us
    all_gather x1, waiting for transfers between devices, local(): full = lax.all_gather(rest, OWNERS, axis=0, tiled=True)  25.4 us
    ppermute x14, starting transfers between devices, ctx_shifted(): moved.insert(1, lax.ppermute(values[i], CTX, pairs))  20.2 us
    unnamed x90, local copies, waits for them, and re-layouts  17 us
    ppermute x14, waiting for transfers between devices, ctx_shifted(): moved.insert(1, lax.ppermute(values[i], CTX, pairs))  10.3 us
  transfers between devices with their start and end apart: 93, of which 34 were waited for; matrix products, arithmetic and copies ran while one was open for 1% of the time, Pallas kernels for 13%

profile of v3, /device:TPU:0, one launch (start us, length us, event | category | flops | bytes accessed | tf_op | source)
XLA Modules:
  0.0 435.4 jit_solution(7471683427410452546)
XLA Ops:
  24.0 3.6 collective-permute-start.4
  28.6 10.2 %collective-permute-done.3.refs_1_ = bf16[128,1664]{1,0:T(8,128)(2,1)S(1)} collective-permute-done((bf16[128,1664]{1,0:T(8,128)(2,1)S(1)}, bf16[128,1664]{1,0:T(8,128)(2,1)S(1)}, u32[]{:S(2)}, u32[]{:S(2)}) %collective-permute-start.3) | collective-permute-done | bytes 426016 | tf_op jit(solution)/shard_map/ppermute | solution.py:648
  38.8 16.2 %collective-permute-done.4.refs_2_ = bf16[128,1664]{1,0:T(8,128)(2,1)S(1)} collective-permute-done((bf16[128,1664]{1,0:T(8,128)(2,1)S(1)}, bf16[128,1664]{1,0:T(8,128)(2,1)S(1)}, u32[]{:S(2)}, u32[]{:S(2)}) %collective-permute-start.4) | collective-permute-done | bytes 426016 | tf_op jit(solution)/shard_map/ppermute | solution.py:648
  56.4 4.0 collective-permute-done.6.refs_2_
  61.3 3.6 start.1
  86.6 4.8 %attention.2 = (bf16[128,256]{1,0:T(8,128)(2,1)S(1)}, bf16[4,128,1024]{2,1,0:T(8,128)(2,1)S(1)}) custom-call(bf16[128,256]{1,0:T(8,128)(2,1)S(1)} %get-tuple-element.137.refs_0_.refs_9_, bf16[1024,512]{1,0:T(8,128)(2,1)S(1)} %gather.2.refs_1_.refs_6_.refs_10_, bf16[256,1152]{1,0:T(8,128)(2,1)S(1)} %get-tuple-element.144.refs_2_.refs_11_, ...), custom_call_target="tpu_custom_call" | custom-call | tf_op jit(solution)/shard_map/attention/pallas_call | solution.py:50
  101.9 6.1 %collective-permute-done.15.refs_3_ = bf16[128,1024]{1,0:T(8,128)(2,1)S(1)} collective-permute-done((bf16[128,1024]{1,0:T(8,128)(2,1)S(1)}, bf16[128,1024]{1,0:T(8,128)(2,1)S(1)}, u32[]{:S(2)}, u32[]{:S(2)}) %collective-permute-start.15) | collective-permute-done | bytes 262176 | tf_op jit(solution)/shard_map/ppermute | solution.py:648
  109.4 25.4 %all-gather.2.cloned.1.call-done.refs_6_.refs_1_.refs_4_.refs_8_.refs_3_ = bf16[1024,5120]{1,0:T(8,128)(2,1)} async-done(((bf16[32,5120]{1,0:T(8,128)(2,1)}), bf16[1024,5120]{1,0:T(8,128)(2,1)}) %all-gather.2.cloned.1.call-update) | async-done | bytes 10485776 | tf_op jit(solution)/shard_map/all_gather | solution.py:770
  134.8 4.0 copy-done
  151.4 4.1 collective-permute-done.17.refs_2_
  155.5 6.3 %collective-permute-done.18.refs_3_ = bf16[128,1024]{1,0:T(8,128)(2,1)S(1)} collective-permute-done((bf16[128,1024]{1,0:T(8,128)(2,1)S(1)}, bf16[128,1024]{1,0:T(8,128)(2,1)S(1)}, u32[]{:S(2)}, u32[]{:S(2)}) %collective-permute-start.18) | collective-permute-done | bytes 262176 | tf_op jit(solution)/shard_map/ppermute | solution.py:648
  162.6 3.2 collective-permute-start.21
  169.2 3.4 collective-permute-start.25
  176.0 4.3 collective-permute-done.24.refs_6_
  182.4 4.8 %attention.3 = (bf16[128,256]{1,0:T(8,128)(2,1)S(1)}, bf16[4,128,1024]{2,1,0:T(8,128)(2,1)S(1)}) custom-call(bf16[128,256]{1,0:T(8,128)(2,1)S(1)} %get-tuple-element.153.refs_0_.refs_9_, bf16[1024,512]{1,0:T(8,128)(2,1)S(1)} %gather.3.refs_1_.refs_6_.refs_10_, bf16[256,1152]{1,0:T(8,128)(2,1)S(1)} %get-tuple-element.156.refs_2_.refs_11_, ...), custom_call_target="tpu_custom_call" | custom-call | tf_op jit(solution)/shard_map/attention/pallas_call | solution.py:50
  192.7 4.1 collective-permute-done.27.refs_2_
  196.8 5.3 %collective-permute-done.28.refs_3_ = bf16[128,1024]{1,0:T(8,128)(2,1)S(1)} collective-permute-done((bf16[128,1024]{1,0:T(8,128)(2,1)S(1)}, bf16[128,1024]{1,0:T(8,128)(2,1)S(1)}, u32[]{:S(2)}, u32[]{:S(2)}) %collective-permute-start.28) | collective-permute-done | bytes 262176 | tf_op jit(solution)/shard_map/ppermute | solution.py:648
  208.3 3.9 collective-permute-done.30.refs_2_
  212.2 6.1 %collective-permute-done.31.refs_3_ = bf16[128,1024]{1,0:T(8,128)(2,1)S(1)} collective-permute-done((bf16[128,1024]{1,0:T(8,128)(2,1)S(1)}, bf16[128,1024]{1,0:T(8,128)(2,1)S(1)}, u32[]{:S(2)}, u32[]{:S(2)}) %collective-permute-start.31) | collective-permute-done | bytes 262176 | tf_op jit(solution)/shard_map/ppermute | solution.py:648
  239.3 5.1 %collective-permute-done.35.refs_4_ = bf16[128,1024]{1,0:T(8,128)(2,1)S(1)} collective-permute-done((bf16[128,1024]{1,0:T(8,128)(2,1)S(1)}, bf16[128,1024]{1,0:T(8,128)(2,1)S(1)}, u32[]{:S(2)}, u32[]{:S(2)}) %collective-permute-start.35) | collective-permute-done | bytes 262176 | tf_op jit(solution)/shard_map/ppermute | solution.py:648
  244.5 9.0 %attention_back.2 = (f32[128,1024]{1,0:T(8,128)S(1)}, bf16[128,1024]{1,0:T(8,128)(2,1)S(1)}, bf16[128,256]{1,0:T(8,128)(2,1)S(1)}, bf16[1152,256]{1,0:T(8,128)(2...) custom-call(s32[5]{0:T(128)S(1)} %stack.37.refs_0_, ...), custom_call_target="tpu_custom_call" | custom-call | tf_op jit(solution)/shard_map/attention_back/pallas_call | solution.py:50
  260.5 7.1 %collective-permute-done.37.refs_1_ = bf16[256,512]{1,0:T(8,128)(2,1)S(1)} collective-permute-done((bf16[256,512]{1,0:T(8,128)(2,1)S(1)}, bf16[256,512]{1,0:T(8,128)(2,1)S(1)}, u32[]{:S(2)}, u32[]{:S(2)}) %collective-permute-start.37) | collective-permute-done | bytes 262176 | tf_op jit(solution)/shard_map/ppermute | solution.py:648
  288.6 3.6 collective-permute-done.50.refs_3_
  306.2 5.7 %collective-permute-done.55.refs_2_ = bf16[128,1408]{1,0:T(8,128)(2,1)S(1)} collective-permute-done((bf16[128,1408]{1,0:T(8,128)(2,1)S(1)}, bf16[128,1408]{1,0:T(8,128)(2,1)S(1)}, u32[]{:S(2)}, u32[]{:S(2)}) %collective-permute-start.55) | collective-permute-done | bytes 360480 | tf_op jit(solution)/shard_map/ppermute | solution.py:648
  313.8 6.5 %collective-permute-done.56.refs_3_ = bf16[128,1408]{1,0:T(8,128)(2,1)S(1)} collective-permute-done((bf16[128,1408]{1,0:T(8,128)(2,1)S(1)}, bf16[128,1408]{1,0:T(8,128)(2,1)S(1)}, u32[]{:S(2)}, u32[]{:S(2)}) %collective-permute-start.56) | collective-permute-done | bytes 360480 | tf_op jit(solution)/shard_map/ppermute | solution.py:648
  328.7 9.1 %attention_back.3 = (f32[128,1024]{1,0:T(8,128)S(1)}, bf16[128,1024]{1,0:T(8,128)(2,1)S(1)}, bf16[128,256]{1,0:T(8,128)(2,1)S(1)}, bf16[1152,256]{1,0:T(8,128)(2...) custom-call(s32[5]{0:T(128)S(1)} %stack.37.refs_0_, ...), custom_call_target="tpu_custom_call" | custom-call | tf_op jit(solution)/shard_map/attention_back/pallas_call | solution.py:50
  344.4 8.2 %collective-permute-done.58.refs_1_ = bf16[256,512]{1,0:T(8,128)(2,1)S(1)} collective-permute-done((bf16[256,512]{1,0:T(8,128)(2,1)S(1)}, bf16[256,512]{1,0:T(8,128)(2,1)S(1)}, u32[]{:S(2)}, u32[]{:S(2)}) %collective-permute-start.58) | collective-permute-done | bytes 262176 | tf_op jit(solution)/shard_map/ppermute | solution.py:648
  355.9 10.6 %collective-permute-done.61.refs_2_ = bf16[128,2048]{1,0:T(8,128)(2,1)S(1)} collective-permute-done((bf16[128,2048]{1,0:T(8,128)(2,1)S(1)}, bf16[128,2048]{1,0:T(8,128)(2,1)S(1)}, u32[]{:S(2)}, u32[]{:S(2)}) %collective-permute-start.61) | collective-permute-done | bytes 524320 | tf_op jit(solution)/shard_map/ppermute | solution.py:648
  372.2 4.8 %collective-permute-done.69.refs_2_ = bf16[128,640]{1,0:T(8,128)(2,1)S(1)} collective-permute-done((bf16[128,640]{1,0:T(8,128)(2,1)S(1)}, bf16[128,640]{1,0:T(8,128)(2,1)S(1)}, u32[]{:S(2)}, u32[]{:S(2)}) %collective-permute-start.69) | collective-permute-done | bytes 163872 | tf_op jit(solution)/shard_map/ppermute | solution.py:648
  391.2 3.8 collective-permute-start.80
  400.7 4.4 %collective-permute-start.74 = (bf16[128,1024]{1,0:T(8,128)(2,1)S(1)}, bf16[128,1024]{1,0:T(8,128)(2,1)S(1)}, u32[]{:S(2)}, u32[]{:S(2)}) collective-permute-start(bf16[128,1024]{1,0:T(8,128)(2,1)S(1)} %get-tuple-element.239.refs_5_.refs_1_), channel_id=1, source_target_pairs={{0,3},{1,0},{2,1},{3,2},{4,7},{5,4},{6,5},{7,6},{8,11},{9,8},{10,9... | collective-permute-start | bytes 786440 | tf_op jit(solution)/shard_map/ppermute | solution.py:648
  412.8 3.9 all-to-all-start
  (309 shorter events, 214.9 us)
Async XLA Ops:
  7.2 127.6 %all-gather.2.cloned.1.call-start = ((), (), s32[]{:S(2)}) async-start(), calls=%async_computation.1 | async-start | bytes 10813440 | tf_op jit(solution)/shard_map/all_gather | solution.py:770
  22.0 16.7 %collective-permute-start.3 = (bf16[128,1664]{1,0:T(8,128)(2,1)S(1)}, bf16[128,1664]{1,0:T(8,128)(2,1)S(1)}, u32[]{:S(2)}, u32[]{:S(2)}) collective-permute-start(bf16[128,1664]{1,0:T(8,128)(2,1)S(1)} %stack.42.refs_0_.refs_4_), channel_id=1, source_target_pairs={{0,4},{4,64},{64,68},{68,0},{1,5},{5,65},{65,69},{69,1},{2,6},{6,6... | collective-permute-start | bytes 1277960 | tf_op jit(solution)/shard_map/ppermute | solution.py:648
  24.0 31.0 %collective-permute-start.4 = (bf16[128,1664]{1,0:T(8,128)(2,1)S(1)}, bf16[128,1664]{1,0:T(8,128)(2,1)S(1)}, u32[]{:S(2)}, u32[]{:S(2)}) collective-permute-start(bf16[128,1664]{1,0:T(8,128)(2,1)S(1)} %stack.42.refs_0_.refs_4_), channel_id=1, source_target_pairs={{0,64},{4,68},{64,0},{68,4},{1,65},{5,69},{65,1},{69,5},{2,66},{6,... | collective-permute-start | bytes 1277960 | tf_op jit(solution)/shard_map/ppermute | solution.py:648
  27.6 27.3 %collective-permute-start.5 = (bf16[128,1664]{1,0:T(8,128)(2,1)S(1)}, bf16[128,1664]{1,0:T(8,128)(2,1)S(1)}, u32[]{:S(2)}, u32[]{:S(2)}) collective-permute-start(bf16[128,1664]{1,0:T(8,128)(2,1)S(1)} %stack.42.refs_0_.refs_4_), channel_id=1, source_target_pairs={{0,68},{4,0},{64,4},{68,64},{1,69},{5,1},{65,5},{69,65},{2,70},{6,... | collective-permute-start | bytes 1277960 | tf_op jit(solution)/shard_map/ppermute | solution.py:648
  66.4 15.0 %collective-permute-start.12 = (bf16[128,512]{1,0:T(8,128)(2,1)S(1)}, bf16[128,512]{1,0:T(8,128)(2,1)S(1)}, u32[]{:S(2)}, u32[]{:S(2)}) collective-permute-start(bf16[128,512]{1,0:T(8,128)(2,1)S(1)} %get-tuple-element.138.refs_4_.refs_1_), channel_id=1, source_target_pairs={{0,28},{4,24},{8,4},{12,0},{16,12},{20,8},{24,20},{28,16},{1,29},{... | collective-permute-start | bytes 393224 | tf_op jit(solution)/shard_map/ppermute | solution.py:674
  93.3 14.7 %collective-permute-start.15 = (bf16[128,1024]{1,0:T(8,128)(2,1)S(1)}, bf16[128,1024]{1,0:T(8,128)(2,1)S(1)}, u32[]{:S(2)}, u32[]{:S(2)}) collective-permute-start(bf16[128,1024]{1,0:T(8,128)(2,1)S(1)} %attended.2.refs_1_.refs_7_), channel_id=1, source_target_pairs={{0,2},{1,3},{2,0},{3,1},{4,6},{5,7},{6,4},{7,5},{8,10},{9,11},{10,... | collective-permute-start | bytes 786440 | tf_op jit(solution)/shard_map/ppermute | solution.py:648
  147.2 14.6 %collective-permute-start.18 = (bf16[128,1024]{1,0:T(8,128)(2,1)S(1)}, bf16[128,1024]{1,0:T(8,128)(2,1)S(1)}, u32[]{:S(2)}, u32[]{:S(2)}) collective-permute-start(bf16[128,1024]{1,0:T(8,128)(2,1)S(1)} %get-tuple-element.151.refs_1_.refs_7_), channel_id=1, source_target_pairs={{0,2},{1,3},{2,0},{3,1},{4,6},{5,7},{6,4},{7,5},{8,10},{9,11},{10,... | collective-permute-start | bytes 786440 | tf_op jit(solution)/shard_map/ppermute | solution.py:648
  204.9 13.5 %collective-permute-start.31 = (bf16[128,1024]{1,0:T(8,128)(2,1)S(1)}, bf16[128,1024]{1,0:T(8,128)(2,1)S(1)}, u32[]{:S(2)}, u32[]{:S(2)}) collective-permute-start(bf16[128,1024]{1,0:T(8,128)(2,1)S(1)} %get-tuple-element.161.refs_1_.refs_6_), channel_id=1, source_target_pairs={{0,2},{1,3},{2,0},{3,1},{4,6},{5,7},{6,4},{7,5},{8,10},{9,11},{10,... | collective-permute-start | bytes 786440 | tf_op jit(solution)/shard_map/ppermute | solution.py:648
  228.8 26.9 %collective-permute-start.40 = (bf16[128,2048]{1,0:T(8,128)(2,1)S(1)}, bf16[128,2048]{1,0:T(8,128)(2,1)S(1)}, u32[]{:S(2)}, u32[]{:S(2)}) collective-permute-start(bf16[128,2048]{1,0:T(8,128)(2,1)S(1)} %get-tuple-element.181), channel_id=1, source_target_pairs={{0,4},{4,64},{64,68},{68,0},{1,5},{5,65},{65,69},{69,1},{2,6},{6,6... | collective-permute-start | bytes 1572872 | tf_op jit(solution)/shard_map/ppermute | solution.py:648
  234.0 25.1 %collective-permute-start.41 = (bf16[128,2048]{1,0:T(8,128)(2,1)S(1)}, bf16[128,2048]{1,0:T(8,128)(2,1)S(1)}, u32[]{:S(2)}, u32[]{:S(2)}) collective-permute-start(bf16[128,2048]{1,0:T(8,128)(2,1)S(1)} %get-tuple-element.182), channel_id=1, source_target_pairs={{0,64},{4,68},{64,0},{68,4},{1,65},{5,69},{65,1},{69,5},{2,66},{6,... | collective-permute-start | bytes 1572872 | tf_op jit(solution)/shard_map/ppermute | solution.py:648
  235.8 23.6 %collective-permute-start.42 = (bf16[128,2048]{1,0:T(8,128)(2,1)S(1)}, bf16[128,2048]{1,0:T(8,128)(2,1)S(1)}, u32[]{:S(2)}, u32[]{:S(2)}) collective-permute-start(bf16[128,2048]{1,0:T(8,128)(2,1)S(1)} %get-tuple-element.173.refs_14_), channel_id=1, source_target_pairs={{0,68},{4,0},{64,4},{68,64},{1,69},{5,1},{65,5},{69,65},{2,70},{6,... | collective-permute-start | bytes 1572872 | tf_op jit(solution)/shard_map/ppermute | solution.py:648
  253.5 14.1 %collective-permute-start.37 = (bf16[256,512]{1,0:T(8,128)(2,1)S(1)}, bf16[256,512]{1,0:T(8,128)(2,1)S(1)}, u32[]{:S(2)}, u32[]{:S(2)}) collective-permute-start(bf16[256,512]{1,0:T(8,128)(2,1)S(1)} %get-tuple-element.177), channel_id=1, source_target_pairs={{0,8},{8,16},{16,24},{24,0},{1,9},{9,17},{17,25},{25,1},{2,10},{10... | collective-permute-start | bytes 786440 | tf_op jit(solution)/shard_map/ppermute | solution.py:648
  276.2 16.1 %collective-permute-start.47 = (bf16[512,1408]{1,0:T(8,128)(2,1)S(1)}, bf16[512,1408]{1,0:T(8,128)(2,1)S(1)}, u32[]{:S(2)}, u32[]{:S(2)}) collective-permute-start(bf16[512,1408]{1,0:T(8,128)(2,1)S(1)} %late_other.2.refs_4_), channel_id=1, source_target_pairs={{0,32},{32,0},{1,33},{33,1},{2,34},{34,2},{3,35},{35,3},{4,36},{36... | collective-permute-start | bytes 4325384 | tf_op jit(solution)/shard_map/ppermute | solution.py:648
  282.4 14.5 %collective-permute-start.45 = (bf16[128,1024]{1,0:T(8,128)(2,1)S(1)}, bf16[128,1024]{1,0:T(8,128)(2,1)S(1)}, u32[]{:S(2)}, u32[]{:S(2)}) collective-permute-start(bf16[128,1024]{1,0:T(8,128)(2,1)S(1)} %get-tuple-element.189.refs_10_.refs_1_), channel_id=1, source_target_pairs={{0,2},{1,3},{2,0},{3,1},{4,6},{5,7},{6,4},{7,5},{8,10},{9,11},{10,... | collective-permute-start | bytes 786440 | tf_op jit(solution)/shard_map/ppermute | solution.py:648
  299.8 25.5 %collective-permute-start.54 = (bf16[512,2048]{1,0:T(8,128)(2,1)S(1)}, bf16[512,2048]{1,0:T(8,128)(2,1)S(1)}, u32[]{:S(2)}, u32[]{:S(2)}) collective-permute-start(bf16[512,2048]{1,0:T(8,128)(2,1)S(1)} %early_other.3.refs_5_), channel_id=1, source_target_pairs={{0,32},{32,0},{1,33},{33,1},{2,34},{34,2},{3,35},{35,3},{4,36},{36... | collective-permute-start | bytes 6291464 | tf_op jit(solution)/shard_map/ppermute | solution.py:648
  301.5 18.7 %collective-permute-start.56 = (bf16[128,1408]{1,0:T(8,128)(2,1)S(1)}, bf16[128,1408]{1,0:T(8,128)(2,1)S(1)}, u32[]{:S(2)}, u32[]{:S(2)}) collective-permute-start(bf16[128,1408]{1,0:T(8,128)(2,1)S(1)} %get-tuple-element.211), channel_id=1, source_target_pairs={{0,64},{4,68},{64,0},{68,4},{1,65},{5,69},{65,1},{69,5},{2,66},{6,... | collective-permute-start | bytes 1081352 | tf_op jit(solution)/shard_map/ppermute | solution.py:648
  303.8 18.9 %collective-permute-start.57 = (bf16[128,1408]{1,0:T(8,128)(2,1)S(1)}, bf16[128,1408]{1,0:T(8,128)(2,1)S(1)}, u32[]{:S(2)}, u32[]{:S(2)}) collective-permute-start(bf16[128,1408]{1,0:T(8,128)(2,1)S(1)} %get-tuple-element.200.refs_9_), channel_id=1, source_target_pairs={{0,68},{4,0},{64,4},{68,64},{1,69},{5,1},{65,5},{69,65},{2,70},{6,... | collective-permute-start | bytes 1081352 | tf_op jit(solution)/shard_map/ppermute | solution.py:648
  305.2 18.5 %collective-permute-start.51 = (bf16[128,1024]{1,0:T(8,128)(2,1)S(1)}, bf16[128,1024]{1,0:T(8,128)(2,1)S(1)}, u32[]{:S(2)}, u32[]{:S(2)}) collective-permute-start(bf16[128,1024]{1,0:T(8,128)(2,1)S(1)} %get-tuple-element.201.refs_1_), channel_id=1, source_target_pairs={{0,1},{1,2},{2,3},{3,0},{4,5},{5,6},{6,7},{7,4},{8,9},{9,10},{10,1... | collective-permute-start | bytes 786440 | tf_op jit(solution)/shard_map/ppermute | solution.py:648
  311.9 16.7 %collective-permute-start.52 = (bf16[128,1024]{1,0:T(8,128)(2,1)S(1)}, bf16[128,1024]{1,0:T(8,128)(2,1)S(1)}, u32[]{:S(2)}, u32[]{:S(2)}) collective-permute-start(bf16[128,1024]{1,0:T(8,128)(2,1)S(1)} %get-tuple-element.201.refs_1_), channel_id=1, source_target_pairs={{0,2},{1,3},{2,0},{3,1},{4,6},{5,7},{6,4},{7,5},{8,10},{9,11},{10,... | collective-permute-start | bytes 786440 | tf_op jit(solution)/shard_map/ppermute | solution.py:648
  323.7 15.0 %collective-permute-start.64 = (bf16[32,1408]{1,0:T(8,128)(2,1)S(1)}, bf16[32,1408]{1,0:T(8,128)(2,1)S(1)}, u32[]{:S(2)}, u32[]{:S(2)}) collective-permute-start(bf16[32,1408]{1,0:T(8,128)(2,1)S(1)} %get-tuple-element.229), channel_id=1, source_target_pairs={{0,8},{8,16},{16,24},{24,0},{1,9},{9,17},{17,25},{25,1},{2,10},{10... | collective-permute-start | bytes 270344 | tf_op jit(solution)/shard_map/ppermute | solution.py:648
  323.8 14.9 %collective-permute-start.65 = (bf16[32,1408]{1,0:T(8,128)(2,1)S(1)}, bf16[32,1408]{1,0:T(8,128)(2,1)S(1)}, u32[]{:S(2)}, u32[]{:S(2)}) collective-permute-start(bf16[32,1408]{1,0:T(8,128)(2,1)S(1)} %get-tuple-element.230), channel_id=1, source_target_pairs={{0,16},{8,24},{16,0},{24,8},{1,17},{9,25},{17,1},{25,9},{2,18},{10... | collective-permute-start | bytes 270344 | tf_op jit(solution)/shard_map/ppermute | solution.py:648
  339.6 14.7 %collective-permute-start.67 = (bf16[512,640]{1,0:T(8,128)(2,1)S(1)}, bf16[512,640]{1,0:T(8,128)(2,1)S(1)}, u32[]{:S(2)}, u32[]{:S(2)}) collective-permute-start(bf16[512,640]{1,0:T(8,128)(2,1)S(1)} %middle_other.1.refs_7_), channel_id=1, source_target_pairs={{0,32},{32,0},{1,33},{33,1},{2,34},{34,2},{3,35},{35,3},{4,36},{36... | collective-permute-start | bytes 1966088 | tf_op jit(solution)/shard_map/ppermute | solution.py:648
  339.7 26.8 %collective-permute-start.61 = (bf16[128,2048]{1,0:T(8,128)(2,1)S(1)}, bf16[128,2048]{1,0:T(8,128)(2,1)S(1)}, u32[]{:S(2)}, u32[]{:S(2)}) collective-permute-start(bf16[128,2048]{1,0:T(8,128)(2,1)S(1)} %get-tuple-element.221), channel_id=1, source_target_pairs={{0,4},{4,64},{64,68},{68,0},{1,5},{5,65},{65,69},{69,1},{2,6},{6,6... | collective-permute-start | bytes 1572872 | tf_op jit(solution)/shard_map/ppermute | solution.py:648
  339.8 26.7 %collective-permute-start.62 = (bf16[128,2048]{1,0:T(8,128)(2,1)S(1)}, bf16[128,2048]{1,0:T(8,128)(2,1)S(1)}, u32[]{:S(2)}, u32[]{:S(2)}) collective-permute-start(bf16[128,2048]{1,0:T(8,128)(2,1)S(1)} %get-tuple-element.222), channel_id=1, source_target_pairs={{0,64},{4,68},{64,0},{68,4},{1,65},{5,69},{65,1},{69,5},{2,66},{6,... | collective-permute-start | bytes 1572872 | tf_op jit(solution)/shard_map/ppermute | solution.py:648
  341.5 26.0 %collective-permute-start.63 = (bf16[128,2048]{1,0:T(8,128)(2,1)S(1)}, bf16[128,2048]{1,0:T(8,128)(2,1)S(1)}, u32[]{:S(2)}, u32[]{:S(2)}) collective-permute-start(bf16[128,2048]{1,0:T(8,128)(2,1)S(1)} %get-tuple-element.213.refs_14_), channel_id=1, source_target_pairs={{0,68},{4,0},{64,4},{68,64},{1,69},{5,1},{65,5},{69,65},{2,70},{6,... | collective-permute-start | bytes 1572872 | tf_op jit(solution)/shard_map/ppermute | solution.py:648
  352.7 18.5 %collective-permute-start.59 = (bf16[256,512]{1,0:T(8,128)(2,1)S(1)}, bf16[256,512]{1,0:T(8,128)(2,1)S(1)}, u32[]{:S(2)}, u32[]{:S(2)}) collective-permute-start(bf16[256,512]{1,0:T(8,128)(2,1)S(1)} %get-tuple-element.218), channel_id=1, source_target_pairs={{0,16},{8,24},{16,0},{24,8},{1,17},{9,25},{17,1},{25,9},{2,18},{10... | collective-permute-start | bytes 786440 | tf_op jit(solution)/shard_map/ppermute | solution.py:648
  354.3 16.8 %collective-permute-start.60 = (bf16[256,512]{1,0:T(8,128)(2,1)S(1)}, bf16[256,512]{1,0:T(8,128)(2,1)S(1)}, u32[]{:S(2)}, u32[]{:S(2)}) collective-permute-start(bf16[256,512]{1,0:T(8,128)(2,1)S(1)} %get-tuple-element.219.refs_3_), channel_id=1, source_target_pairs={{0,24},{8,0},{16,8},{24,16},{1,25},{9,1},{17,9},{25,17},{2,26},{10... | collective-permute-start | bytes 786440 | tf_op jit(solution)/shard_map/ppermute | solution.py:648
  382.4 14.5 %collective-permute-start.72 = (bf16[128,1024]{1,0:T(8,128)(2,1)S(1)}, bf16[128,1024]{1,0:T(8,128)(2,1)S(1)}, u32[]{:S(2)}, u32[]{:S(2)}) collective-permute-start(bf16[128,1024]{1,0:T(8,128)(2,1)S(1)} %get-tuple-element.239.refs_5_.refs_1_), channel_id=1, source_target_pairs={{0,1},{1,2},{2,3},{3,0},{4,5},{5,6},{6,7},{7,4},{8,9},{9,10},{10,1... | collective-permute-start | bytes 786440 | tf_op jit(solution)/shard_map/ppermute | solution.py:648
  400.3 16.4 %collective-permute-start.73 = (bf16[128,1024]{1,0:T(8,128)(2,1)S(1)}, bf16[128,1024]{1,0:T(8,128)(2,1)S(1)}, u32[]{:S(2)}, u32[]{:S(2)}) collective-permute-start(bf16[128,1024]{1,0:T(8,128)(2,1)S(1)} %get-tuple-element.239.refs_5_.refs_1_), channel_id=1, source_target_pairs={{0,2},{1,3},{2,0},{3,1},{4,6},{5,7},{6,4},{7,5},{8,10},{9,11},{10,... | collective-permute-start | bytes 786440 | tf_op jit(solution)/shard_map/ppermute | solution.py:648
  400.7 19.1 %collective-permute-start.74 = (bf16[128,1024]{1,0:T(8,128)(2,1)S(1)}, bf16[128,1024]{1,0:T(8,128)(2,1)S(1)}, u32[]{:S(2)}, u32[]{:S(2)}) collective-permute-start(bf16[128,1024]{1,0:T(8,128)(2,1)S(1)} %get-tuple-element.239.refs_5_.refs_1_), channel_id=1, source_target_pairs={{0,3},{1,0},{2,1},{3,2},{4,7},{5,4},{6,5},{7,6},{8,11},{9,8},{10,9... | collective-permute-start | bytes 786440 | tf_op jit(solution)/shard_map/ppermute | solution.py:648
  408.2 14.7 %collective-permute-start.89 = (bf16[32,2048]{1,0:T(8,128)(2,1)S(1)}, bf16[32,2048]{1,0:T(8,128)(2,1)S(1)}, u32[]{:S(2)}, u32[]{:S(2)}) collective-permute-start(bf16[32,2048]{1,0:T(8,128)(2,1)S(1)} %get-tuple-element.256), channel_id=1, source_target_pairs={{0,16},{8,24},{16,0},{24,8},{1,17},{9,25},{17,1},{25,9},{2,18},{10... | collective-permute-start | bytes 393224 | tf_op jit(solution)/shard_map/ppermute | solution.py:648
  412.8 13.6 %all-to-all-start = ((f32[32,2,32]{2,1,0:T(2,128)}), f32[32,2,32]{2,1,0:T(2,128)S(1)}, u32[]{:S(2)}, u32[]{:S(2)}) async-start(f32[32,2,32]{2,1,0:T(2,128)} %get-tuple-element.250.refs_5_), calls=%async_computation | async-start | bytes 65536 | tf_op jit(solution)/shard_map/all_to_all | solution.py:1068
  (106 other events, 916.2 us)
Sparse Core Ops, SparseCore 0:
  10.9 123.8 all-gather.1
